TPU v7x, 32 devices: a whole 2x2x4 slice. The times are simulated.
32 devices in a mesh: dp: 2 (over core), ctx: 4 (over z), grp: 4 (over y, x).
Axes of the slice: x: 2, y: 2, z: 4, core: 2. Of those that a mesh axis runs over, the one named last changes fastest.
Arguments:
- projected: bfloat16 [4, 1024, 3, 4096], P('dp', 'ctx', None, 'grp'), may hold values from -6 to 6
- short_w: float32 [3, 3, 4096], P(None, None, 'grp'), may hold values from -2.5 to 2.5
- medium_h: bfloat16 [256, 128], P('grp'), may hold values from -3 to 3
- out_w: bfloat16 [4096, 4096], P('ctx', 'grp'), may hold values from -0.09375 to 0.09375
- grad_out: bfloat16 [4, 1024, 4096], P('dp', 'ctx', 'grp'), may hold values from -6 to 6
Outputs:
- block_out: bfloat16 [4, 1024, 4096], P('dp', 'ctx', 'grp')
- grad_projected: bfloat16 [4, 1024, 3, 4096], P('dp', 'ctx', None, 'grp')
- filter_grad: float32 [256, 128], P('grp')
- short_grad: float32 [3, 3, 4096], P(None, None, 'grp')
All inputs are finite; a program needn't handle non-finite values.
Results may differ from a plain program's by a relative error of at most 0.0064.
Values may be sent and summed in bfloat16 or wider, within the bound.
No kernel may reach another device: no remote copies, remote signals or barrier semaphores. Data moves between devices by JAX's collectives and lax.ppermute only.
A program may use at most 128 MiB of HBM per device.

v0:
```python
import math

import jax
import jax.numpy as jnp
from jax import lax
from jax.sharding import PartitionSpec as P


def from_behind(block, axis, distance):
    devices = range(lax.axis_size(axis))
    route = [(i - distance, i) for i in devices if i - distance in devices]
    return lax.ppermute(block, axis, route)


def windows(padded, block_rows, reach):
    seqs_here = padded.shape[0]
    block_count = (padded.shape[1] - reach) // block_rows
    extended = jnp.pad(padded, ((0, 0), (0, block_rows - reach), (0, 0), (0, 0)))
    leading = extended[:, : block_count * block_rows].reshape(
        seqs_here, block_count, block_rows, padded.shape[2], padded.shape[3]
    )
    second = extended[:, block_rows:].reshape(
        seqs_here, block_count, block_rows, padded.shape[2], padded.shape[3]
    )[:, :, :reach]
    return jnp.concatenate([leading, second], axis=2)


def banded(filters, block_rows):
    groups_here = filters.shape[0]
    tap_count = filters.shape[1]
    line_width = block_rows + tap_count
    padded_line = jnp.concatenate(
        [filters, jnp.zeros((groups_here, block_rows), filters.dtype)], axis=1
    )
    tiled = jnp.broadcast_to(
        padded_line[:, None, :], (groups_here, block_rows, line_width)
    ).reshape(groups_here, block_rows * line_width)
    return tiled[:, : block_rows * (line_width - 1)].reshape(
        groups_here, block_rows, line_width - 1
    )


def band_conv(turned, matrix, block_rows):
    reach = matrix.shape[2] - block_rows
    windowed = windows(turned, block_rows, reach)
    result = jnp.einsum("gtj,sbjcg->sbtcg", matrix, windowed, preferred_element_type=jnp.float32)
    result = jnp.swapaxes(result, 3, 4)
    return result.reshape(
        turned.shape[0], turned.shape[1] - reach, turned.shape[2] * turned.shape[3]
    )


def lag_sums(grad_blocks, windowed, tap_count):
    products = jnp.einsum(
        "sbtcg,sbjcg->gtj", grad_blocks, windowed, preferred_element_type=jnp.float32
    )
    groups_here = products.shape[0]
    block_rows = products.shape[1]
    line_width = products.shape[2]
    flat_rows = jnp.pad(
        products.reshape(groups_here, block_rows * line_width), ((0, 0), (0, block_rows))
    )
    skewed = flat_rows.reshape(groups_here, block_rows, line_width + 1)[:, :, :tap_count]
    return jnp.sum(skewed, axis=1)[:, ::-1]


def featurize(padded, weights):
    short_reach = weights.shape[1] - 1
    row_count = padded.shape[1] - short_reach
    total = None
    for offset in range(weights.shape[1]):
        start = short_reach - offset
        term = weights[:, offset, :] * padded[:, start : start + row_count]
        total = term if total is None else total + term
    return total


def adjoint(padded, weights):
    short_reach = weights.shape[1] - 1
    row_count = padded.shape[1] - short_reach
    total = None
    for offset in range(weights.shape[1]):
        term = weights[:, offset, :] * padded[:, offset : offset + row_count]
        total = term if total is None else total + term
    return total


def short_sums(feature_grad, padded, short_taps):
    row_count = feature_grad.shape[1]
    short_reach = short_taps - 1
    terms = []
    for offset in range(short_taps):
        start = short_reach - offset
        terms.append(jnp.sum(feature_grad * padded[:, start : start + row_count], axis=(0, 1)))
    return jnp.stack(terms, axis=1)


def shards(projected, short_w, medium_h, out_w, grad_out):
    seq_local = projected.shape[0]
    row_count = projected.shape[1]
    chan_local = projected.shape[3]
    tap_count = medium_h.shape[1]
    reach = tap_count - 1
    short_taps = short_w.shape[1]
    short_reach = short_taps - 1
    group_local = medium_h.shape[0]
    group_size = chan_local // group_local
    block_rows = math.gcd(row_count, 128)
    rim_rows = reach + short_reach
    packed = jnp.concatenate(
        [
            projected[:, row_count - rim_rows :, 1:].reshape(seq_local, rim_rows * 2, chan_local),
            projected[:, row_count - short_reach :, 0],
        ],
        axis=1,
    )
    arrived = from_behind(packed, "ctx", 1)
    stream_front = arrived[:, : rim_rows * 2].reshape(seq_local, rim_rows, 2, chan_local)
    query_front = arrived[:, rim_rows * 2 :][:, :, None]
    stream_features = featurize(
        jnp.concatenate([stream_front, projected[:, :, 1:]], axis=1).astype(jnp.float32),
        short_w[1:],
    )
    query_features = featurize(
        jnp.concatenate([query_front, projected[:, :, 0:1]], axis=1).astype(jnp.float32),
        short_w[0:1],
    )
    features = jnp.concatenate([query_features, stream_features[:, reach:]], axis=2)
    product_pad = (stream_features[:, :, 0] * stream_features[:, :, 1]).astype(jnp.bfloat16)
    front_rows = jnp.concatenate([query_front, stream_front[:, rim_rows - short_reach :]], axis=2)
    padded_input = jnp.concatenate([front_rows, projected], axis=1)
    query = features[:, :, 0]
    keys = features[:, :, 1]
    values = features[:, :, 2]
    product_turned = jnp.swapaxes(
        product_pad.reshape(seq_local, row_count + reach, group_local, group_size), 2, 3
    )
    mixed = band_conv(product_turned, banded(medium_h[:, ::-1], block_rows), block_rows)
    gated = (query * mixed).astype(jnp.bfloat16)
    whole_gated = lax.all_gather(gated, "grp", axis=2, tiled=True)
    flat_gated = whole_gated.reshape(seq_local * row_count, whole_gated.shape[2])
    flat_cotangent = grad_out.reshape(seq_local * row_count, chan_local)
    projected_out = jnp.dot(
        flat_gated,
        lax.all_gather(out_w, "ctx", axis=0, tiled=True),
        preferred_element_type=jnp.float32,
    )
    block_out = projected_out.astype(jnp.bfloat16).reshape(seq_local, row_count, chan_local)
    input_part = lax.dot_general(
        flat_cotangent,
        lax.all_gather(out_w, "ctx", axis=0, tiled=True),
        (((1,), (1,)), ((), ())),
        preferred_element_type=jnp.float32,
    )
    summed = lax.psum_scatter(input_part, "grp", scatter_dimension=1, tiled=True)
    gated_grad = (
        lax.optimization_barrier(summed.astype(jnp.bfloat16))
        .astype(jnp.float32)
        .reshape(seq_local, row_count, chan_local)
    )
    query_grad = gated_grad * mixed
    mix_grad = (gated_grad * query).astype(jnp.bfloat16)
    mix_back = from_behind(mix_grad[:, :reach], "ctx", -1)
    mix_turned = jnp.swapaxes(
        jnp.concatenate([mix_grad, mix_back], axis=1).reshape(
            seq_local, row_count + reach, group_local, group_size
        ),
        2,
        3,
    )
    product_grad = band_conv(mix_turned, banded(medium_h, block_rows), block_rows)
    grad_blocks = jnp.swapaxes(
        mix_grad.reshape(seq_local, row_count // block_rows, block_rows, group_local, group_size),
        3,
        4,
    )
    filter_part = lag_sums(grad_blocks, windows(product_turned, block_rows, reach), tap_count)
    feature_grad = jnp.stack(
        [query_grad, product_grad * values, product_grad * keys], axis=2
    ).astype(jnp.bfloat16)
    grad_back = from_behind(feature_grad[:, :short_reach], "ctx", -1)
    grad_pad = jnp.concatenate([feature_grad, grad_back], axis=1).astype(jnp.float32)
    grad_projected = adjoint(grad_pad, short_w).astype(jnp.bfloat16)
    short_part = short_sums(
        feature_grad.astype(jnp.float32), padded_input.astype(jnp.float32), short_taps
    )
    filter_total, short_total = lax.psum((filter_part, short_part), ("dp", "ctx"))
    seq_total = seq_local * lax.axis_size("dp")
    length_total = row_count * lax.axis_size("ctx")
    filter_grad = filter_total / math.sqrt(seq_total * length_total * group_size)
    short_grad = short_total / math.sqrt(seq_total * length_total)
    return (block_out, grad_projected, filter_grad, short_grad)


def solution(mesh):
    in_specs = (
        P("dp", "ctx", None, "grp"),
        P(None, None, "grp"),
        P("grp", None),
        P("ctx", "grp"),
        P("dp", "ctx", "grp"),
    )
    out_specs = (
        P("dp", "ctx", "grp"),
        P("dp", "ctx", None, "grp"),
        P("grp", None),
        P(None, None, "grp"),
    )
    return jax.shard_map(shards, mesh=mesh, in_specs=in_specs, out_specs=out_specs, check_vma=False)
```

profile of v0, /device:TPU:0, one launch (start us, length us, event | category | flops | bytes accessed | tf_op | source)
XLA Modules:
  0.0 481.6 jit_solution(5256180814324350282)
XLA Ops:
  8.0 154.0 %all-gather.5.cloned.1.call-done = bf16[4096,1024]{1,0:T(8,128)(2,1)} async-done(((bf16[1024,1024]{1,0:T(8,128)(2,1)}), bf16[4096,1024]{1,0:T(8,128)(2,1)}) %all-gather.5.cloned.1.call-update) | async-done | bytes 8388624 | tf_op jit(solution)/shard_map/all_gather | solution.py:145
  162.0 10.1 %fusion.40 = f32[512,4096]{1,0:T(8,128)} fusion(bf16[512,1024]{1,0:T(8,128)(2,1)S(1)} %bitcast.109, bf16[4096,1024]{1,0:T(8,128)(2,1)} %all-gather.5.cloned.1.call-done), kind=kOutput, calls=%fused_computation.79 | convolution fusion | flops 4294967296 | bytes 17825792 | tf_op jit(solution)/shard_map/dot_general | solution.py:149
  175.6 2.4 pad_maximum_fusion.2
  178.0 2.8 collective-permute-start
  180.8 4.7 copy.74
  186.6 2.6 copy.124
  189.3 2.2 slice.206
  191.5 16.0 %reshape.172 = bf16[64,128,255,1,1]{2,1,0,3,4:T(8,128)(2,1)} reshape(bf16[64,32640]{1,0:T(8,128)(2,1)} %slice.206) | data formatting | bytes 8355840 | tf_op jit(solution)/shard_map/reshape | solution.py:38
  207.8 2.6 copy.123
  210.4 2.2 slice.202
  212.6 16.0 %reshape.171 = bf16[64,128,255,1,1]{2,1,0,3,4:T(8,128)(2,1)} reshape(bf16[64,32640]{1,0:T(8,128)(2,1)} %slice.202) | data formatting | bytes 8355840 | tf_op jit(solution)/shard_map/reshape | solution.py:38
  228.7 3.1 slice.193
  231.8 5.0 %copy.77 = bf16[2,129,2,1024]{1,3,0,2:T(8,128)(2,1)} copy(bf16[2,129,2,1024]{3,0,2,1:T(2,128)(2,1)} %bitcast.120) | data formatting | bytes 2113536 | tf_op jit(solution)/shard_map/reshape | solution.py:118
  237.6 3.1 maximum_convert_fusion.2
  240.7 4.4 fusion.6
  245.5 2.3 copy-done.2
  253.4 2.7 reshape.160
  256.1 2.7 reshape.155
  260.8 2.4 maximum_convert_fusion.3
  263.2 5.6 %maximum_convert_fusion.1 = f32[2,258,3,1024]{1,3,0,2:T(8,128)} fusion(bf16[2,256,3,1024]{1,3,0,2:T(8,128)(2,1)S(1)} %copy-done.3, bf16[2,2,3,1024]{1,3,0,2:T(8,128)(2,1)S(1)} %copy.99), kind=kLoop, calls=%fused_computation.18 | loop fusion | flops 6340608 | bytes 9510912 | tf_op jit(solution)/shard_map/convert_element_type | solution.py:185
  268.8 1.7 convert_element_type.64
  272.4 1.8 copy.86
  274.2 6.1 %fusion.21 = (bf16[2,256,1024]{1,2,0:T(8,128)(2,1)S(1)}, f32[2,256,1,1024]{1,3,0,2:T(8,128)}) fusion(f32[2,256,1024]{1,2,0:T(8,128)} %copy.86, f32[2,258,1,1024]{1,3,0,2:T(8,128)} %maximum_convert_fusion.3, f32[1024]{0:T(1024)S(1)} %bitcast.133, f32[1024]{0:T(1024)S(1)} %bitcast.134, f32[1024]{0:T(1024)S(1)} %bitcast.132), kind=kLoop, calls=%fused_computation.44 | loop fusion | flops 3670016 | bytes 11546624 | tf_op jit(solution)/shard_map/convert_element_type | solution.py:162
  282.5 2.0 copy.85
  284.5 3.4 squeeze.14
  288.0 2.4 reshape.168
  290.4 3.5 fusion.32
  293.9 4.6 convolution_bitcast_fusion
  298.5 9.2 %reshape.169 = f32[64,32640]{1,0:T(8,128)} reshape(f32[64,128,255]{2,1,0:T(8,128)} %convolution_bitcast_fusion) | data formatting | bytes 16711680 | tf_op jit(solution)/shard_map/reshape | solution.py:61
  307.7 4.0 pad.16
  311.8 2.5 copy.125
  315.9 1.9 multiply_convert_fusion
  323.8 4.1 fusion.27
  329.0 2.7 reshape.167
  331.7 4.6 fusion.14
  336.4 11.5 %fusion = (f32[3,1024]{1,0:T(4,128)S(1)}, f32[3,1024]{1,0:T(4,128)S(1)}, f32[3,1024]{1,0:T(4,128)S(1)}) fusion(f32[2,258,3,1024]{1,3,0,2:T(8,128)} %maximum_convert_fusion.1, bf16[2,256,1,1024]{1,3,0,2:T(8,128)(2,1)S(1)} %get-tuple-element.24, bf16[2,256,1,1024]{1,3,0,2:T(8,128)(2,1)S(1)} %get-tuple-element.23, ...), kind=kLoop, calls=%fused_computation.3 | loop fusion | flops 14146560 | bytes 22056960 | tf_op jit(solution)/shard_map/reduce_sum | solution.py:94
  348.6 2.8 fusion.20
  351.5 1.9 pad_maximum_fusion
  354.8 1.7 copy.92
  357.8 5.1 %collective-permute-done.2 = bf16[2,2,3,1024]{3,1,2,0:T(2,128)(2,1)S(1)} collective-permute-done((bf16[2,2,3,1024]{3,1,2,0:T(2,128)(2,1)S(1)}, bf16[2,2,3,1024]{3,1,2,0:T(2,128)(2,1)S(1)}, u32[]{:S(2)}, u32[]{:S(2)}) %collective-permute-start.2) | collective-permute-done | bytes 24608 | tf_op jit(solution)/shard_map/ppermute | solution.py:12
  362.9 1.7 copy.93
  364.6 2.6 maximum_convert_fusion
  367.3 5.8 %fusion.4 = bf16[2,256,3,1024]{1,3,0,2:T(8,128)(2,1)} fusion(f32[2,258,3,1024]{1,3,0,2:T(8,128)S(1)} %maximum_convert_fusion, f32[3,1024]{1,0:T(4,128)S(1)} %get-tuple-element.42, f32[3,1024]{1,0:T(4,128)S(1)} %get-tuple-element.43, f32[3,1024]{1,0:T(4,128)S(1)} %bitcast.126), kind=kLoop, calls=%fused_computation.8 | loop fusion | flops 9437184 | bytes 22056960 | tf_op jit(solution)/shard_map/convert_element_type | solution.py:183
  373.0 4.6 copy.101
  377.7 22.4 %all-reduce.8.cloned.1.call-done = (f32[64,128]{1,0:T(8,128)}, f32[3,3,1024]{2,0,1:T(4,128)}) async-done(((f32[64,128]{1,0:T(8,128)}, f32[3,3,1024]{2,0,1:T(4,128)}), (f32[64,128]{1,0:T(8,128)}, f32[3,3,1024]{2,0,1:T(4,128)})) %all-reduce.8.cloned.1.call-update) | async-done | bytes 69648 | tf_op jit(solution)/shard_map/psum | solution.py:187
  402.9 55.4 %all-gather.3.cloned.1.call-done = bf16[2,256,4096]{1,2,0:T(8,128)(2,1)} async-done(((bf16[2,256,1024]{1,2,0:T(8,128)(2,1)}), bf16[2,256,4096]{1,2,0:T(8,128)(2,1)}) %all-gather.3.cloned.1.call-update) | async-done | bytes 4194320 | tf_op jit(solution)/shard_map/all_gather | solution.py:140
  458.2 6.5 %copy.83 = bf16[2,256,4096]{2,1,0:T(8,128)(2,1)} copy(bf16[2,256,4096]{1,2,0:T(8,128)(2,1)} %all-gather.3.cloned.1.call-done) | data formatting | bytes 8388608 | tf_op jit(solution)/shard_map/all_gather | solution.py:140
  464.7 10.2 %convolution_convert_fusion = bf16[512,1024]{1,0:T(8,128)(2,1)} fusion(bf16[512,4096]{1,0:T(8,128)(2,1)} %bitcast.123, bf16[4096,1024]{1,0:T(8,128)(2,1)} %all-gather.5.cloned.1.call-done), kind=kOutput, calls=%fused_computation.55 | convolution fusion | flops 4295491584 | bytes 13631488 | tf_op jit(solution)/shard_map/dot_general | solution.py:143
  (98 shorter events, 33.3 us)
Async XLA Ops:
  7.2 154.8 %copy-start = (bf16[2,256,1024]{2,1,0:T(8,128)(2,1)S(1)}, bf16[2,256,1024]{2,1,0:T(8,128)(2,1)}, u32[]{:S(2)}) copy-start(bf16[2,256,1024]{2,1,0:T(8,128)(2,1)} %param.9) | copy-start | bytes 3145732
  7.2 154.8 %all-gather.5.cloned.1.call-start = ((), (), s32[]{:S(2)}) async-start(), calls=%async_computation.2 | async-start | bytes 10485760 | tf_op jit(solution)/shard_map/all_gather | solution.py:145
  7.9 260.9 %reduce-scatter.2.cloned.1.call-start = ((), (), s32[]{:S(2)}) async-start(), calls=%async_computation.3 | async-start | bytes 10485760 | tf_op jit(solution)/shard_map/reduce_scatter | solution.py:155
  172.1 227.9 %all-reduce.8.cloned.1.call-start = ((), (), s32[]{:S(2)}) async-start(), calls=%async_computation.4 | async-start | bytes 163840 | tf_op jit(solution)/shard_map/psum | solution.py:187
  178.0 50.7 %collective-permute-start = (bf16[2,260,1024]{2,0,1:T(2,128)(2,1)}, bf16[2,260,1024]{2,0,1:T(2,128)(2,1)}, u32[]{:S(2)}, u32[]{:S(2)}) collective-permute-start(bf16[2,260,1024]{2,0,1:T(2,128)(2,1)} %pad_maximum_fusion.2), channel_id=1, source_target_pairs={{0,4},{4,8},{8,12},{1,5},{5,9},{9,13},{2,6},{6,10},{10,14},{3,7},{... | collective-permute-start | bytes 3194888 | tf_op jit(solution)/shard_map/ppermute | solution.py:12
  185.5 0.7 copy-start.17
  191.5 16.0 %copy-start.16 = (f32[3,3,1024]{2,1,0:T(4,128)S(1)}, f32[3,3,1024]{2,1,0:T(4,128)}, u32[]{:S(2)}) copy-start(f32[3,3,1024]{2,1,0:T(4,128)} %param.6) | copy-start | bytes 110596
  228.6 8.9 %slice-start.1 = ((bf16[2,256,3,1024]{1,3,0,2:T(8,128)(2,1)}), bf16[2,256,2,1024]{1,3,0,2:T(8,128)(2,1)S(1)}, s32[]{:S(2)}) async-start(bf16[2,256,3,1024]{1,3,0,2:T(8,128)(2,1)} %copy.74), calls=%async_computation.6 | async-start | bytes 4194304 | tf_op jit(solution)/shard_map/slice | solution.py:121
  245.1 2.6 copy-start.2
  248.5 2.2 copy-start.5
  250.7 1.6 copy-start.10
  256.1 4.6 slice-start
  260.8 2.4 copy-start.3
  280.3 7.7 %copy-start.14 = (bf16[2,256,1024]{1,2,0:T(8,128)(2,1)}, bf16[2,256,1024]{1,2,0:T(8,128)(2,1)S(1)}, u32[]{:S(2)}) copy-start(bf16[2,256,1024]{1,2,0:T(8,128)(2,1)S(1)} %get-tuple-element.21) | copy-start | bytes 3145732
  281.2 36.6 %collective-permute-start.1 = (bf16[2,127,1024]{1,2,0:T(8,128)(2,1)}, bf16[2,127,1024]{1,2,0:T(8,128)(2,1)}, u32[]{:S(2)}, u32[]{:S(2)}) collective-permute-start(bf16[2,127,1024]{1,2,0:T(8,128)(2,1)} %slice.203), channel_id=1, source_target_pairs={{4,0},{8,4},{12,8},{5,1},{9,5},{13,9},{6,2},{10,6},{14,10},{7,3},{... | collective-permute-start | bytes 1560584 | tf_op jit(solution)/shard_map/ppermute | solution.py:12
  284.5 3.4 copy-start.13
  290.4 3.5 copy-start.11
  314.3 1.6 copy-start.12
  315.9 1.9 copy-start.15
  336.3 11.6 %copy-start.6 = (bf16[2,256,1,1024]{1,3,0,2:T(8,128)(2,1)}, bf16[2,256,1,1024]{1,3,0,2:T(8,128)(2,1)S(1)}, u32[]{:S(2)}) copy-start(bf16[2,256,1,1024]{1,3,0,2:T(8,128)(2,1)S(1)} %get-tuple-element.23) | copy-start | bytes 3145732
  336.3 11.6 %copy-start.8 = (bf16[2,256,1,1024]{1,3,0,2:T(8,128)(2,1)}, bf16[2,256,1,1024]{1,3,0,2:T(8,128)(2,1)S(1)}, u32[]{:S(2)}) copy-start(bf16[2,256,1,1024]{1,3,0,2:T(8,128)(2,1)S(1)} %get-tuple-element.24) | copy-start | bytes 3145732
  336.3 12.3 %copy-start.4 = (f32[2,256,1,1024]{1,3,0,2:T(8,128)S(1)}, f32[2,256,1,1024]{1,3,0,2:T(8,128)}, u32[]{:S(2)}) copy-start(f32[2,256,1,1024]{1,3,0,2:T(8,128)} %get-tuple-element.22) | copy-start | bytes 6291460
  348.6 109.7 %all-gather.3.cloned.1.call-start = ((), (), s32[]{:S(2)}) async-start(), calls=%async_computation.1 | async-start | bytes 5242880 | tf_op jit(solution)/shard_map/all_gather | solution.py:140
  353.3 11.3 %copy-start.7 = (bf16[2,256,1,1024]{1,3,0,2:T(8,128)(2,1)S(1)}, bf16[2,256,1,1024]{1,3,0,2:T(8,128)(2,1)}, u32[]{:S(2)}) copy-start(bf16[2,256,1,1024]{1,3,0,2:T(8,128)(2,1)} %copy-done.6) | copy-start | bytes 3145732
  353.3 11.3 %copy-start.9 = (bf16[2,256,1,1024]{1,3,0,2:T(8,128)(2,1)S(1)}, bf16[2,256,1,1024]{1,3,0,2:T(8,128)(2,1)}, u32[]{:S(2)}) copy-start(bf16[2,256,1,1024]{1,3,0,2:T(8,128)(2,1)} %copy-done.8) | copy-start | bytes 3145732
  356.5 6.4 %collective-permute-start.2 = (bf16[2,2,3,1024]{3,1,2,0:T(2,128)(2,1)S(1)}, bf16[2,2,3,1024]{3,1,2,0:T(2,128)(2,1)S(1)}, u32[]{:S(2)}, u32[]{:S(2)}) collective-permute-start(bf16[2,2,3,1024]{3,1,2,0:T(2,128)(2,1)S(1)} %copy.92), channel_id=1, source_target_pairs={{4,0},{8,4},{12,8},{5,1},{9,5},{13,9},{6,2},{10,6},{14,10},{7,3},{... | collective-permute-start | bytes 73736 | tf_op jit(solution)/shard_map/ppermute | solution.py:12
  464.7 10.2 %copy-start.1 = (bf16[2,256,1024]{2,1,0:T(8,128)(2,1)S(1)}, bf16[2,256,1024]{2,1,0:T(8,128)(2,1)}, u32[]{:S(2)}) copy-start(bf16[2,256,1024]{2,1,0:T(8,128)(2,1)} %param.9) | copy-start | bytes 3145732
Sparse Core Ops, SparseCore 0:
  9.6 152.3 all-gather.4
  172.2 84.6 reduce-scatter.1
  348.7 51.3 all-reduce.7
  402.3 55.8 all-gather.2
where the time goes:
time: 487 us; the launch traced here: 482 us
  waiting for transfers between devices  238 us (49%)
  local copies, waits for them, and re-layouts  128 us (26%)
  other arithmetic  65.5 us (13%)
  matrix products  30.6 us (6%)
  between operations  14.5 us (3%)
  starting transfers between devices  5.54 us (1%)
    all_gather x1, waiting for transfers between devices, shards(): lax.all_gather(out_w, 'ctx', axis=0, tiled=True)  154 us
    all_gather x1, waiting for transfers between devices, shards(): whole_gated = lax.all_gather(gated, 'grp', axis=2, tiled=True)  55.4 us
    reshape x2, local copies, waits for them, and re-layouts, banded(): tiled[:, :block_rows * (line_width - 1)]  31.9 us
    unnamed x49, local copies, waits for them, and re-layouts  24.2 us
    psum x1, waiting for transfers between devices, shards(): lax.psum((filter_part, short_part), ('dp', 'ctx'))  22.4 us
    reduce_sum x1, other arithmetic, short_sums(): jnp.sum(feature_grad * padded[:, start:start + row_count], axis=(0, 1))  11.5 us
    dot_general x1, matrix products, shards(): jnp.dot(flat_gated, lax.all_gather(out_w, 'ctx', axis=0, tiled=True), pre...  10.2 us
    dot_general x1, matrix products, shards(): lax.dot_general(flat_cotangent, lax.all_gather(out_w, 'ctx', axis=0, tile...  10.1 us
  transfers between devices with their start and end apart: 7, of which 4 were waited for; matrix products, arithmetic and copies ran while one was open for 31% of the time, Pallas kernels for 0%

commit v1 on v0

v1 whole, which is shorter than its diff:
```python
import functools
import math

import jax
import jax.numpy as jnp
from jax import lax
from jax.experimental import pallas as pl
from jax.experimental.pallas import tpu as pltpu
from jax.sharding import PartitionSpec as P

LANES = 128
HALO = 144
EXTRA = 16
F32 = jnp.float32
BF16 = jnp.bfloat16


def params(mib=32):
    return pltpu.CompilerParams(vmem_limit_bytes=mib * 1024 * 1024)


def shift(block, axis, distance, first=0):
    count = lax.axis_size(axis)
    if distance > 0:
        route = [(i, i + distance) for i in range(first, count - distance)]
    else:
        route = [(i, i + distance) for i in range(-distance, count - first)]
    return lax.ppermute(block, axis, route)


def pick_groups(stacked, rows, group_size):
    width = stacked.shape[1]
    lane = lax.broadcasted_iota(jnp.int32, (1, width), 1) % LANES
    groups = LANES // group_size
    total = stacked[:rows]
    for g in range(1, groups):
        total = jnp.where(lane >= g * group_size, stacked[g * rows : (g + 1) * rows], total)
    return total


def fill_band(line_ref, band_ref, rows):
    for g in range(line_ref.shape[0]):
        wide = jnp.broadcast_to(line_ref[g : g + 1, :], (rows, line_ref.shape[1]))
        moved = pltpu.roll(wide, 0, 1, stride=1, stride_axis=0)
        band_ref[g * rows : (g + 1) * rows, :] = moved.astype(BF16)


def features_kernel(x_ref, front_ref, w_ref, product_ref, q_ref, k_ref, v_ref, pad):
    seqs, rows = x_ref.shape[1], x_ref.shape[2]
    for s in range(seqs):
        found = []
        for j, out_ref in enumerate((q_ref, k_ref, v_ref)):
            own = s * 3 + j
            pad[own, 0:8] = front_ref[j, s]
            pad[own, 8 : 8 + rows] = x_ref[j, s].astype(F32)
            total = w_ref[j, 0:1] * pad[own, 8 : 8 + rows]
            total = total + w_ref[j, 1:2] * pad[own, 7 : 7 + rows]
            total = total + w_ref[j, 2:3] * pad[own, 6 : 6 + rows]
            out_ref[s] = total
            found.append(total)
        product_ref[s] = (found[1] * found[2]).astype(BF16)


def features(x, front, short_w):
    _, seqs, rows, width = x.shape
    at4 = lambda i: (0, 0, 0, i)
    at3 = lambda i: (0, 0, i)
    wide = pl.BlockSpec((seqs, rows, LANES), at3)
    shape = (seqs, rows, width)
    return pl.pallas_call(
        features_kernel,
        grid=(width // LANES,),
        in_specs=[
            pl.BlockSpec((3, seqs, rows, LANES), at4),
            pl.BlockSpec((3, seqs, 8, LANES), at4),
            pl.BlockSpec((3, 3, LANES), at3),
        ],
        out_specs=[wide] * 4,
        out_shape=[jax.ShapeDtypeStruct(shape, BF16)] + [jax.ShapeDtypeStruct(shape, F32)] * 3,
        scratch_shapes=[pltpu.VMEM((3 * seqs, rows + 8, LANES), F32)],
        compiler_params=params(),
        name="features",
    )(x, front, short_w)


def mix_kernel(group_size, line_ref, low_ref, high_ref, q_ref, mixed_ref, gated_ref, band, columns):
    seqs, rows = low_ref.shape[0], low_ref.shape[1]
    fill_band(line_ref, band, rows)
    for s in range(seqs):
        at = slice(s * LANES, (s + 1) * LANES)
        columns[:rows, at] = low_ref[s]
        columns[rows:, at] = high_ref[s]
    stacked = jnp.dot(band[...], columns[...], preferred_element_type=F32)
    mixed = pick_groups(stacked, rows, group_size)
    for s in range(seqs):
        part = mixed[:, s * LANES : (s + 1) * LANES]
        mixed_ref[s] = part
        gated_ref[s] = (q_ref[s] * part).astype(BF16)


def mix(line, low, low_at, high, high_at, query, query_at, rows, group_size):
    seqs, _, width = query.shape
    groups = LANES // group_size
    part = lambda at: pl.BlockSpec((seqs, rows, LANES), lambda i: (0, at, i))
    shape = (seqs, rows, width)
    return pl.pallas_call(
        functools.partial(mix_kernel, group_size),
        grid=(width // LANES,),
        in_specs=[
            pl.BlockSpec((groups, 2 * rows), lambda i: (i, 0)),
            part(low_at),
            part(high_at),
            part(query_at),
        ],
        out_specs=[part(0), part(0)],
        out_shape=[jax.ShapeDtypeStruct(shape, F32), jax.ShapeDtypeStruct(shape, BF16)],
        scratch_shapes=[
            pltpu.VMEM((groups * rows, 2 * rows), BF16),
            pltpu.VMEM((2 * rows, seqs * LANES), BF16),
        ],
        compiler_params=params(),
        name="mix",
    )(line, low, high, query)


def fetch_rows(pos_ref, own_ref, near, far, buffer, sems, slot, owner, at, half):
    here, core = pos_ref[0], pos_ref[1]
    steps = len(near) + 1
    step = lax.rem(here - owner + steps, steps)

    def copies(first, second, start):
        mine = pl.multiple_of(at + core * half, half)
        other = pl.multiple_of(at + (1 - core) * half, half)
        for which, (source, place) in enumerate(((first, mine), (second, other))):
            copy = pltpu.make_async_copy(
                source, buffer.at[slot, pl.ds(place, half)], sems.at[slot, which]
            )
            copy.start() if start else copy.wait()

    def begin():
        @pl.when(step == 0)
        def _():
            mine = pl.multiple_of(at + core * half, half)
            other = pl.multiple_of(at + (1 - core) * half, half)
            copies(own_ref.at[pl.ds(mine, half)], own_ref.at[pl.ds(other, half)], True)

        for other_step in range(1, steps):

            @pl.when(step == other_step)
            def _(other_step=other_step):
                copies(near[other_step - 1], far[other_step - 1], True)

    def end():
        copies(near[0], far[0], False)

    return begin, end


def grad_kernel(steps, at, half, pos_ref, cot_ref, own_ref, *refs):
    near, far = refs[: steps - 1], refs[steps - 1 : 2 * steps - 2]
    outs = refs[2 * steps - 2 : 3 * steps - 2]
    buffer, sems = refs[3 * steps - 2 :]
    group = pos_ref[2]
    ends = []
    for partner in range(steps):
        owner = lax.bitwise_xor(group, partner)
        slot_own = own_ref.at[pl.ds(at, 2 * half)]
        begin, end = fetch_rows(
            pos_ref, slot_own, near, far, buffer, sems, partner, owner, 0, half
        )
        begin()
        ends.append(end)
    for partner in list(range(1, steps)) + [0]:
        ends[partner]()
        outs[partner][...] = lax.dot_general(
            cot_ref[...],
            buffer[partner],
            (((1,), (1,)), ((), ())),
            preferred_element_type=F32,
        ).astype(outs[partner].dtype)


def grad_parts(pos, cotangent, out_w, near, far, at):
    rows, width = cotangent.shape
    steps = len(near) + 1
    half = near[0].shape[0]
    anywhere = pl.BlockSpec(memory_space=pl.ANY)
    return pl.pallas_call(
        functools.partial(grad_kernel, steps, at, half),
        in_specs=[pl.BlockSpec(memory_space=pltpu.SMEM), pl.BlockSpec(memory_space=pltpu.VMEM)]
        + [anywhere] * (2 * steps - 1),
        out_specs=[pl.BlockSpec(memory_space=pltpu.VMEM)] * steps,
        out_shape=[jax.ShapeDtypeStruct((rows, 2 * half), F32)]
        + [jax.ShapeDtypeStruct((rows, 2 * half), BF16)] * (steps - 1),
        scratch_shapes=[
            pltpu.VMEM((steps, 2 * half, width), BF16),
            pltpu.SemaphoreType.DMA((steps, 2)),
        ],
        compiler_params=params(),
        name="grad_parts",
    )(pos, cotangent, out_w, *near, *far)


def out_kernel(steps, pieces, parts, half, pos_ref, own_ref, *refs):
    count = pieces * (steps - 1)
    nears, fars = refs[:count], refs[count : 2 * count]
    gated = refs[2 * count : 2 * count + steps * parts]
    out_ref = refs[2 * count + steps * parts]
    buffers = refs[2 * count + steps * parts + 1 : -2]
    sems, total = refs[-2:]
    group = pos_ref[2]
    ends = {}
    for partner in range(steps):
        owner = lax.bitwise_xor(group, partner)
        for p in range(pieces):
            begin, end = fetch_rows(
                pos_ref,
                own_ref.at[pl.ds(p * 2 * half, 2 * half)],
                nears[p * (steps - 1) : (p + 1) * (steps - 1)],
                fars[p * (steps - 1) : (p + 1) * (steps - 1)],
                buffers[p],
                sems.at[p],
                partner,
                owner,
                0,
                half,
            )
            begin()
            ends[partner, p] = end
    for partner in range(steps):
        for p in range(pieces):
            ends[partner, p]()
        for b in range(parts):
            block = gated[partner * parts + b]
            seqs, rows, width = block.shape
            for p in range(pieces):
                left = block[:, :, p * 2 * half : (p + 1) * 2 * half].reshape(seqs * rows, 2 * half)
                term = jnp.dot(left, buffers[p][partner], preferred_element_type=F32)
                if partner == 0 and p == 0:
                    total[b] = term
                elif partner == steps - 1 and p == pieces - 1:
                    done = (total[b] + term).astype(BF16)
                    for s in range(seqs):
                        out_ref[s, b * rows : (b + 1) * rows] = done[s * rows : (s + 1) * rows]
                else:
                    total[b] += term


def block_output(pos, out_w, nears, fars, gated):
    steps, parts = len(gated), len(gated[0])
    pieces = len(nears)
    half = nears[0][0].shape[0]
    seqs, rows, _ = gated[0][0].shape
    width = out_w.shape[1]
    anywhere = pl.BlockSpec(memory_space=pl.ANY)
    inside = pl.BlockSpec(memory_space=pltpu.VMEM)
    count = pieces * (steps - 1)
    return pl.pallas_call(
        functools.partial(out_kernel, steps, pieces, parts, half),
        in_specs=[pl.BlockSpec(memory_space=pltpu.SMEM)]
        + [anywhere] * (1 + 2 * count)
        + [inside] * (steps * parts),
        out_specs=inside,
        out_shape=jax.ShapeDtypeStruct((seqs, parts * rows, width), BF16),
        scratch_shapes=[pltpu.VMEM((steps, 2 * half, width), BF16)] * pieces
        + [
            pltpu.SemaphoreType.DMA((pieces, steps, 2)),
            pltpu.VMEM((parts, seqs * rows, width), F32),
        ],
        compiler_params=params(48),
        name="block_output",
    )(
        pos,
        out_w,
        *[block for piece in nears for block in piece],
        *[block for piece in fars for block in piece],
        *[block for partner in gated for block in partner],
    )


def mix_grad_kernel(steps, *refs):
    terms = refs[:steps]
    q_ref, low_ref, high_ref, mix_ref, query_ref, pack_ref = refs[steps:]
    seqs, rows = q_ref.shape[0], low_ref.shape[1]
    for s in range(seqs):
        for b, mixed_ref in enumerate((low_ref, high_ref)):
            at = slice(b * rows, (b + 1) * rows)
            total = terms[0][s, at].astype(F32)
            for term in terms[1:]:
                total = total + term[s, at].astype(F32)
            gated_grad = total.astype(BF16).astype(F32)
            mix_ref[s, at] = (gated_grad * q_ref[s, at]).astype(BF16)
            query_ref[s, at] = (gated_grad * mixed_ref[s]).astype(BF16)
        pack_ref[s, :HALO] = mix_ref[s, :HALO]
        pack_ref[s, HALO:] = query_ref[s, :EXTRA]


def mix_grads(terms, query, mixed, offset):
    seqs, rows, width = terms[0].shape
    half = rows // 2
    first = offset // LANES
    local = lambda count: pl.BlockSpec((seqs, count, LANES), lambda i: (0, 0, i))
    wide = lambda count: pl.BlockSpec((seqs, count, LANES), lambda i: (0, 0, first + i))
    return pl.pallas_call(
        functools.partial(mix_grad_kernel, len(terms)),
        grid=(width // LANES,),
        in_specs=[local(rows)] * len(terms) + [wide(rows), wide(half), wide(half)],
        out_specs=[local(rows), local(rows), local(HALO + EXTRA)],
        out_shape=[
            jax.ShapeDtypeStruct((seqs, rows, width), BF16),
            jax.ShapeDtypeStruct((seqs, rows, width), BF16),
            jax.ShapeDtypeStruct((seqs, HALO + EXTRA, width), BF16),
        ],
        compiler_params=params(),
        name="mix_grads",
    )(*terms, query, *mixed)


def filter_kernel(group_size, mix_ref, product_ref, front_ref, out_ref, left, columns):
    seqs = mix_ref.shape[0]
    rows = front_ref.shape[1]
    groups = LANES // group_size
    lane = lax.broadcasted_iota(jnp.int32, (1, LANES), 1) // group_size
    total = None
    for b in range(mix_ref.shape[1] // rows):
        for s in range(seqs):
            at = slice(s * LANES, (s + 1) * LANES)
            block = mix_ref[s, b * rows : (b + 1) * rows]
            for g in range(groups):
                keep = (lane == g).astype(F32).astype(BF16)
                left[b, g * rows : (g + 1) * rows, at] = block * keep
            if b == 0:
                columns[b, :rows, at] = front_ref[s]
            else:
                columns[b, :rows, at] = product_ref[s, (b - 1) * rows : b * rows]
            columns[b, rows:, at] = product_ref[s, b * rows : (b + 1) * rows]
        term = lax.dot_general(
            left[b], columns[b], (((1,), (1,)), ((), ())), preferred_element_type=F32
        )
        total = term if total is None else total + term
    span = 2 * rows
    folded = []
    for g in range(groups):
        sum_g = None
        for a in range(rows // 8):
            tile = total[g * rows + a * 8 : g * rows + a * 8 + 8]
            tile = pltpu.roll(tile, (span - a * 8) % span, 1)
            sum_g = tile if sum_g is None else sum_g + tile
        folded.append(sum_g)
    stacked = jnp.stack(folded, axis=0)
    result = None
    for r in range(8):
        row = pltpu.roll(stacked[:, r, :], (span - r) % span, 1)
        result = row if result is None else result + row
    out_ref[...] = result


def filter_sums(mix_grad, product, front, offset, group_size):
    seqs, rows, width = mix_grad.shape
    block_rows = front.shape[1]
    first = offset // LANES
    groups = LANES // group_size
    blocks = rows // block_rows
    return pl.pallas_call(
        functools.partial(filter_kernel, group_size),
        grid=(width // LANES,),
        in_specs=[
            pl.BlockSpec((seqs, rows, LANES), lambda i: (0, 0, i)),
            pl.BlockSpec((seqs, rows, LANES), lambda i: (0, 0, first + i)),
            pl.BlockSpec((seqs, block_rows, LANES), lambda i: (0, 0, first + i)),
        ],
        out_specs=pl.BlockSpec((groups, 2 * block_rows), lambda i: (i, 0)),
        out_shape=jax.ShapeDtypeStruct((width // group_size, 2 * block_rows), F32),
        scratch_shapes=[
            pltpu.VMEM((blocks, groups * block_rows, seqs * LANES), BF16),
            pltpu.VMEM((blocks, 2 * block_rows, seqs * LANES), BF16),
        ],
        compiler_params=params(),
        name="filter_sums",
    )(mix_grad, product, front)


def input_grad_kernel(
    group_size,
    line_ref,
    mix_ref,
    query_ref,
    back_ref,
    k_ref,
    v_ref,
    x_ref,
    front_ref,
    next_ref,
    w_ref,
    out_ref,
    sums_ref,
    band,
    columns,
    grads,
    inputs,
    edge,
):
    seqs, rows = mix_ref.shape[0], mix_ref.shape[1]
    block = line_ref.shape[1] // 2
    groups = LANES // group_size
    fill_band(line_ref, band, block)
    found = []
    for b in range(rows // block):
        for s in range(seqs):
            at = slice(s * LANES, (s + 1) * LANES)
            columns[b, :block, at] = mix_ref[s, b * block : (b + 1) * block]
            if (b + 1) * block < rows:
                columns[b, block:, at] = mix_ref[s, (b + 1) * block : (b + 2) * block]
            else:
                columns[b, block:, at] = back_ref[s, :block]
        stacked = jnp.dot(band[...], columns[b], preferred_element_type=F32)
        found.append(pick_groups(stacked, block, group_size))
    last = rows // block
    for s in range(seqs):
        at = slice(s * LANES, (s + 1) * LANES)
        columns[last, :HALO, at] = back_ref[s, :HALO]
        columns[last, HALO:, at] = jnp.zeros((2 * block - HALO, LANES), BF16)
    few = jnp.concatenate([band[g * block : g * block + EXTRA] for g in range(groups)], axis=0)
    stacked = jnp.dot(few, columns[last], preferred_element_type=F32)
    beyond = pick_groups(stacked, EXTRA, group_size)
    for s in range(seqs):
        at = slice(s * LANES, (s + 1) * LANES)
        after = []
        for j in (1, 2):
            own = s * 2 + j - 1
            edge[own, 0:8] = x_ref[j, s, rows - 16 :].astype(F32)[8:]
            edge[own, 8:16] = next_ref[j - 1, s]
            total = w_ref[j, 0:1] * edge[own, 8:16]
            total = total + w_ref[j, 1:2] * edge[own, 7:15]
            total = total + w_ref[j, 2:3] * edge[own, 6:14]
            after.append(total)
        for j in range(3):
            own = s * 3 + j
            if j == 0:
                grads[own, :rows] = query_ref[s].astype(F32)
                grads[own, rows:] = back_ref[s, HALO:].astype(F32)[:8]
            else:
                factor_ref = v_ref if j == 1 else k_ref
                for b in range(rows // block):
                    part = slice(b * block, (b + 1) * block)
                    value = found[b][:, at] * factor_ref[s, part]
                    grads[own, part] = value.astype(BF16).astype(F32)
                value = beyond[:8, at] * after[2 - j]
                grads[own, rows:] = value.astype(BF16).astype(F32)
            inputs[own, 0:8] = front_ref[j, s]
            inputs[own, 8 : 8 + rows] = x_ref[j, s].astype(F32)
            total = None
            for i in range(3):
                term = w_ref[j, i : i + 1] * grads[own, i : i + rows]
                total = term if total is None else total + term
            out_ref[j, s] = total.astype(BF16)
    for j in range(3):
        for i in range(3):
            total = None
            for s in range(seqs):
                own = s * 3 + j
                term = grads[own, :rows] * inputs[own, 8 - i : 8 - i + rows]
                term = jnp.sum(term, axis=0, keepdims=True)
                total = term if total is None else total + term
            sums_ref[j * 3 + i : j * 3 + i + 1] = total


def input_grads(line, mix_grad, query_grad, back, keys, values, x, front, following, short_w, offset, group_size):
    seqs, rows, width = mix_grad.shape
    block = line.shape[1] // 2
    first = offset // LANES
    groups = LANES // group_size
    local = lambda count: pl.BlockSpec((seqs, count, LANES), lambda i: (0, 0, i))
    wide3 = lambda *sizes: pl.BlockSpec(sizes + (LANES,), lambda i: (0, 0, first + i))
    wide4 = lambda *sizes: pl.BlockSpec(sizes + (LANES,), lambda i: (0, 0, 0, first + i))
    return pl.pallas_call(
        functools.partial(input_grad_kernel, group_size),
        grid=(width // LANES,),
        in_specs=[
            pl.BlockSpec((groups, 2 * block), lambda i: (first + i, 0)),
            local(rows),
            local(rows),
            local(HALO + EXTRA),
            wide3(seqs, rows),
            wide3(seqs, rows),
            wide4(3, seqs, rows),
            wide4(3, seqs, 8),
            wide4(2, seqs, 8),
            wide3(3, 3),
        ],
        out_specs=[
            pl.BlockSpec((3, seqs, rows, LANES), lambda i: (0, 0, 0, i)),
            pl.BlockSpec((9, LANES), lambda i: (0, i)),
        ],
        out_shape=[
            jax.ShapeDtypeStruct((3, seqs, rows, width), BF16),
            jax.ShapeDtypeStruct((9, width), F32),
        ],
        scratch_shapes=[
            pltpu.VMEM((groups * block, 2 * block), BF16),
            pltpu.VMEM((rows // block + 1, 2 * block, seqs * LANES), BF16),
            pltpu.VMEM((3 * seqs, rows + 8, LANES), F32),
            pltpu.VMEM((3 * seqs, rows + 8, LANES), F32),
            pltpu.VMEM((2 * seqs, 16, LANES), F32),
        ],
        compiler_params=params(),
        name="input_grads",
    )(line, mix_grad, query_grad, back, keys, values, x, front, following, short_w)


def chain(pieces, axis):
    count = lax.axis_size(axis)
    here = lax.axis_index(axis)
    up = [[piece] for piece in pieces]
    down = [[piece] for piece in pieces]
    for step in range(1, count):
        for p in range(len(pieces)):
            up[p].append(shift(up[p][-1], axis, 1, step - 1))
            down[p].append(shift(down[p][-1], axis, -1, step - 1))
    return [
        [jnp.where(here >= s, up[p][s], down[p][count - s]) for s in range(1, count)]
        for p in range(len(pieces))
    ]


def total_over(block, axes):
    count = math.prod(lax.axis_size(axis) for axis in axes)
    if count & (count - 1):
        return lax.psum(block, axes)
    step = count // 2
    order = []
    while step:
        order.append(step)
        step //= 2
    for step in order:
        block = block + lax.ppermute(block, axes, [(i, i ^ step) for i in range(count)])
    return block


def shards(projected, short_w, medium_h, out_w, grad_out):
    seqs, rows, _, width = projected.shape
    taps = medium_h.shape[1]
    group_size = width // medium_h.shape[0]
    members = lax.axis_size("grp")
    cores = lax.axis_size("dp")
    partners = range(members)
    to = lambda block, k: lax.ppermute(block, "grp", [(i, i ^ k) for i in partners])
    pos = jnp.stack([lax.axis_index("ctx"), lax.axis_index("dp"), lax.axis_index("grp")])
    pos = pos.astype(jnp.int32)
    ring = out_w.shape[0] == width and lax.axis_size("ctx") == members and cores == 2
    pieces = 2 if ring else 1
    span = width // pieces

    if ring:
        half = span // 2
        core = lax.axis_index("dp")
        sent = [
            lax.dynamic_slice_in_dim(out_w, p * span + core * half, half, axis=0)
            for p in range(pieces)
        ]
        near = chain(sent, "ctx")
        far = [[lax.ppermute(block, "dp", [(0, 1), (1, 0)]) for block in piece] for piece in near]

    x = jnp.transpose(projected, (2, 0, 1, 3))
    front = shift(x[:, :, rows - 2 :], "ctx", 1).astype(F32)
    front = jnp.pad(front, ((0, 0), (0, 0), (6, 0), (0, 0)))
    following = shift(x[1:, :, :2], "ctx", -1).astype(F32)
    following = jnp.pad(following, ((0, 0), (0, 0), (0, 6), (0, 0)))
    filters = medium_h.astype(F32)
    empty = jnp.zeros_like(filters)
    causal = jnp.concatenate([empty[:, :1], filters[:, ::-1], empty[:, 1:]], axis=1)
    anticausal = jnp.concatenate([filters, empty], axis=1)

    product, query, keys, values = features(x, front, short_w)
    product_front = shift(product[:, rows - taps :], "ctx", 1)
    mixed_high, gated_high = mix(causal, product, 0, product, 1, query, 1, taps, group_size)
    mixed_low, gated_low = mix(causal, product_front, 0, product, 0, query, 0, taps, group_size)
    gated = [[gated_low, gated_high]]
    for k in partners[1:]:
        gated.append([to(gated_low, k), to(gated_high, k)])

    cotangent = grad_out.reshape(seqs * rows, width)
    if not ring:
        whole_w = lax.all_gather(out_w, "ctx", axis=0, tiled=True)
        own = lax.axis_index("grp")
        blocks = [
            lax.dynamic_slice_in_dim(whole_w, lax.bitwise_xor(own, k) * width, width, axis=0)
            for k in partners
        ]

    outs, sums = [], []
    for p in range(pieces):
        if ring:
            parts = grad_parts(pos, cotangent, out_w, near[p], far[p], p * span)
        else:
            parts = [
                lax.dot_general(
                    cotangent, block, (((1,), (1,)), ((), ())), preferred_element_type=F32
                ).astype(F32 if k == 0 else BF16)
                for k, block in enumerate(blocks)
            ]
        terms = [parts[0]] + [to(parts[k], k) for k in partners[1:]]
        terms = [term.reshape(seqs, rows, span) for term in terms]
        mix_grad, query_grad, pack = mix_grads(terms, query, (mixed_low, mixed_high), p * span)
        back = shift(pack, "ctx", -1)
        folded = filter_sums(mix_grad, product, product_front, p * span, group_size)
        grad, short = input_grads(
            anticausal,
            mix_grad,
            query_grad,
            back,
            keys,
            values,
            x,
            front,
            following,
            short_w,
            p * span,
            group_size,
        )
        outs.append(grad)
        flat = jnp.concatenate(
            [folded[:, 1 : taps + 1].reshape(-1, LANES), short.reshape(-1, LANES)], axis=0
        )
        sums.append(total_over(flat, ("dp", "ctx")))

    if ring:
        block_out = block_output(pos, out_w, near, far, gated)
    else:
        total = None
        for k in partners:
            left = jnp.concatenate(gated[k], axis=1).reshape(seqs * rows, width)
            term = jnp.dot(left, blocks[k], preferred_element_type=F32)
            total = term if total is None else total + term
        block_out = total.astype(BF16).reshape(seqs, rows, width)

    grad_projected = jnp.transpose(jnp.concatenate(outs, axis=3), (1, 2, 0, 3))
    group_rows = span // group_size * taps // LANES
    filter_total = jnp.concatenate(
        [part[:group_rows].reshape(-1, taps) for part in sums], axis=0
    )[:, ::-1]
    short_total = jnp.concatenate(
        [part[group_rows:].reshape(3, 3, span) for part in sums], axis=2
    )
    seq_total = seqs * cores
    length_total = rows * lax.axis_size("ctx")
    filter_grad = filter_total / math.sqrt(seq_total * length_total * group_size)
    short_grad = short_total / math.sqrt(seq_total * length_total)
    return (block_out, grad_projected, filter_grad, short_grad)


def solution(mesh):
    in_specs = (
        P("dp", "ctx", None, "grp"),
        P(None, None, "grp"),
        P("grp", None),
        P("ctx", "grp"),
        P("dp", "ctx", "grp"),
    )
    out_specs = (
        P("dp", "ctx", "grp"),
        P("dp", "ctx", None, "grp"),
        P("grp", None),
        P(None, None, "grp"),
    )
    return jax.shard_map(shards, mesh=mesh, in_specs=in_specs, out_specs=out_specs, check_vma=False)
```

time: 487 us -> 243 us (0.50)
  waiting for transfers between devices: 238 us -> 72.5 us
  local copies, waits for them, and re-layouts: 128 us -> 38.4 us
  starting transfers between devices: 5.54 us -> 62.2 us
  Pallas kernels: 0 us -> 56.1 us
  other arithmetic: 65.5 us -> 9.85 us
  matrix products: 30.6 us -> 0 us
  between operations: 14.5 us -> 1.46 us
    all_gather x2 -> x0, waiting for transfers between devices: 209 us -> none  [the longest x1 154 us: shards(): lax.all_gather(out_w, 'ctx', axis=0, tiled=True)]
    ppermute x3 -> x41, waiting for transfers between devices: 5.07 us -> 72.5 us  [the longest x17 52.9 us: shift(): return lax.ppermute(block, axis, route)]
    reshape x15 -> x4, local copies, waits for them, and re-layouts: 63.3 us -> 2.15 us  [the longest x2 2.12 us: shards(): short.reshape(-1, LANES)]
    ppermute x3 -> x41, starting transfers between devices: 5.38 us -> 62.2 us  [the longest x17 39.4 us: shift(): return lax.ppermute(block, axis, route)]
    pallas_call x0 -> x12, Pallas kernels: none -> 56.1 us  [the longest x2 11.2 us: input_grads(): pl.pallas_call(functools.partial(input_grad_kernel, group_size), grid=(wi...]
    convert_element_type x10 -> x0, other arithmetic: 30.7 us -> none  [the longest x1 6.12 us: shards(): mix_grad = (gated_grad * query).astype(jnp.bfloat16)]
    dot_general x5 -> x0, matrix products: 30.6 us -> none  [the longest x1 10.2 us: shards(): jnp.dot(flat_gated, lax.all_gather(out_w, 'ctx', axis=0, tiled=True), pre...]
    psum x1 -> x0, waiting for transfers between devices: 22.4 us -> none  [shards(): lax.psum((filter_part, short_part), ('dp', 'ctx'))]
  transfers between devices with their start and end apart: 7 -> 41, of which waited for: 4 -> 12; matrix products, arithmetic and copies ran while one was open for 31% -> 7% of each run, Pallas kernels for 0% -> 23%
where the time goes in v1:
time: 243 us; the launch traced here: 241 us
  waiting for transfers between devices  72.5 us (30%)
  starting transfers between devices  62.2 us (26%)
  Pallas kernels  56.1 us (23%)
  local copies, waits for them, and re-layouts  38.4 us (16%)
  other arithmetic  9.85 us (4%)
    ppermute x17, waiting for transfers between devices, shift(): return lax.ppermute(block, axis, route)  52.9 us
    ppermute x17, starting transfers between devices, shift(): return lax.ppermute(block, axis, route)  39.4 us
    unnamed x120, local copies, waits for them, and re-layouts  33.3 us
    ppermute x12, waiting for transfers between devices, shards(): lax.ppermute(block, 'grp', [(i, i ^ k) for i in partners])  18.7 us
    ppermute x12, starting transfers between devices, shards(): lax.ppermute(block, 'grp', [(i, i ^ k) for i in partners])  16.1 us
    pallas_call x2, Pallas kernels, input_grads(): pl.pallas_call(functools.partial(input_grad_kernel, group_size), grid=(wi...  11.2 us
    pallas_call x1, Pallas kernels, block_output(): pl.pallas_call(functools.partial(out_kernel, steps, pieces, parts, half),...  9.61 us
    pallas_call x2, Pallas kernels, mix(): pl.pallas_call(functools.partial(mix_kernel, group_size), grid=(width //...  9.41 us
  transfers between devices with their start and end apart: 41, of which 12 were waited for; matrix products, arithmetic and copies ran while one was open for 7% of the time, Pallas kernels for 23%

profile of v1, /device:TPU:0, one launch (start us, length us, event | category | flops | bytes accessed | tf_op | source)
XLA Modules:
  0.0 240.5 jit_solution(923612365746821732)
XLA Ops:
  3.2 1.4 collective-permute-start.1
  4.7 7.0 %collective-permute-start = (bf16[256,1024]{1,0:T(8,128)(2,1)S(1)}, bf16[256,1024]{1,0:T(8,128)(2,1)}, u32[]{:S(2)}, u32[]{:S(2)}) collective-permute-start(bf16[256,1024]{1,0:T(8,128)(2,1)S(1)} %get-tuple-element.61), channel_id=1, source_target_pairs={{0,4},{4,8},{8,12},{1,5},{5,9},{9,13},{2,6},{6,10},{10,14},{3,7},{... | collective-permute-start | bytes 1572872 | tf_op jit(solution)/shard_map/ppermute | solution.py:28
  11.7 3.9 %collective-permute-start.6 = (bf16[256,1024]{1,0:T(8,128)(2,1)S(1)}, bf16[256,1024]{1,0:T(8,128)(2,1)}, u32[]{:S(2)}, u32[]{:S(2)}) collective-permute-start(bf16[256,1024]{1,0:T(8,128)(2,1)S(1)} %get-tuple-element.60), channel_id=1, source_target_pairs={{0,4},{4,8},{8,12},{1,5},{5,9},{9,13},{2,6},{6,10},{10,14},{3,7},{... | collective-permute-start | bytes 1572872 | tf_op jit(solution)/shard_map/ppermute | solution.py:28
  15.6 4.1 %collective-permute-done.7 = bf16[256,1024]{1,0:T(8,128)(2,1)} collective-permute-done((bf16[256,1024]{1,0:T(8,128)(2,1)S(1)}, bf16[256,1024]{1,0:T(8,128)(2,1)}, u32[]{:S(2)}, u32[]{:S(2)}) %collective-permute-start.7) | collective-permute-done | bytes 524320 | tf_op jit(solution)/shard_map/ppermute | solution.py:28
  21.0 9.9 %collective-permute-done.1 = bf16[256,1024]{1,0:T(8,128)(2,1)} collective-permute-done((bf16[256,1024]{1,0:T(8,128)(2,1)S(1)}, bf16[256,1024]{1,0:T(8,128)(2,1)}, u32[]{:S(2)}, u32[]{:S(2)}) %collective-permute-start.1) | collective-permute-done | bytes 524320 | tf_op jit(solution)/shard_map/ppermute | solution.py:28
  32.2 1.5 collective-permute-start.4
  33.7 1.5 collective-permute-start.10
  35.2 2.2 copy.12
  37.4 9.2 %collective-permute-start.18 = (bf16[3,2,2,1024]{3,2,1,0:T(2,128)(2,1)S(1)}, bf16[3,2,2,1024]{3,2,1,0:T(2,128)(2,1)S(1)}, u32[]{:S(2)}, u32[]{:S(2)}) collective-permute-start(bf16[3,2,2,1024]{3,2,1,0:T(2,128)(2,1)S(1)} %slice.44), channel_id=1, source_target_pairs={{0,4},{4,8},{8,12},{1,5},{5,9},{9,13},{2,6},{6,10},{10,14},{3,7},{... | collective-permute-start | bytes 73736 | tf_op jit(solution)/shard_map/ppermute | solution.py:28
  46.7 1.4 collective-permute-done.18
  48.2 4.2 %features.1 = (bf16[2,256,1024]{2,1,0:T(8,128)(2,1)S(1)}, f32[2,256,1024]{2,1,0:T(8,128)S(1)}, f32[2,256,1024]{2,1,0:T(8,128)S(1)}, f32[2,256,1024]{2,1,0:T(8,128)S(1)}) custom-call(bf16[3,2,256,1024]{3,2,1,0:T(8,128)(2,1)S(1)} %bitcast.19, f32[3,2,8,1024]{3,2,1,0:T(8,128)S(1)} %pad_convert_fusion.front_ref, f32[3,3,1024]{2,1,0:T(4,128)S(1)} %copy-done.52), custom_call_target="tpu_custom_call" | custom-call | tf_op jit(solution)/shard_map/features/pallas_call | solution.py:70
  53.8 1.5 broadcast_select_fusion.3.refs_1_
  59.2 17.9 %collective-permute-done.9 = bf16[256,1024]{1,0:T(8,128)(2,1)S(1)} collective-permute-done((bf16[256,1024]{1,0:T(8,128)(2,1)}, bf16[256,1024]{1,0:T(8,128)(2,1)S(1)}, u32[]{:S(2)}, u32[]{:S(2)}) %collective-permute-start.9) | collective-permute-done | bytes 524320 | tf_op jit(solution)/shard_map/ppermute | solution.py:28
  79.3 7.0 %collective-permute-done.3 = bf16[256,1024]{1,0:T(8,128)(2,1)S(1)} collective-permute-done((bf16[256,1024]{1,0:T(8,128)(2,1)}, bf16[256,1024]{1,0:T(8,128)(2,1)S(1)}, u32[]{:S(2)}, u32[]{:S(2)}) %collective-permute-start.3) | collective-permute-done | bytes 524320 | tf_op jit(solution)/shard_map/ppermute | solution.py:28
  88.2 2.6 %collective-permute-start.19 = (bf16[2,128,1024]{2,1,0:T(8,128)(2,1)S(1)}, bf16[2,128,1024]{2,1,0:T(8,128)(2,1)S(1)}, u32[]{:S(2)}, u32[]{:S(2)}) collective-permute-start(bf16[2,128,1024]{2,1,0:T(8,128)(2,1)S(1)} %slice.36), channel_id=1, source_target_pairs={{0,4},{4,8},{8,12},{1,5},{5,9},{9,13},{2,6},{6,10},{10,14},{3,7},{... | collective-permute-start | bytes 1572872 | tf_op jit(solution)/shard_map/ppermute | solution.py:28
  90.9 4.6 %grad_parts.3 = (f32[512,512]{1,0:T(8,128)S(1)}, bf16[512,512]{1,0:T(8,128)(2,1)S(1)}, bf16[512,512]{1,0:T(8,128)(2,1)}, bf16[512,512]{1,0:T(8,128)(2,1)}) custom-call(s32[3]{0:T(128)S(1)} %pad_add_fusion.pos_ref, bf16[512,1024]{1,0:T(8,128)(2,1)S(1)} %bitcast.23, bf16[1024,1024]{1,0:T(8,128)(2,1)S(1)} %copy-done.5, ...), custom_call_target="tpu_custom_call" | custom-call | tf_op jit(solution)/shard_map/grad_parts/pallas_call | solution.py:188
  96.5 1.5 collective-permute-start.31
  98.0 1.5 collective-permute-start.32
  100.0 4.4 %grad_parts.2 = (f32[512,512]{1,0:T(8,128)S(1)}, bf16[512,512]{1,0:T(8,128)(2,1)}, bf16[512,512]{1,0:T(8,128)(2,1)}, bf16[512,512]{1,0:T(8,128)(2,1)}) custom-call(s32[3]{0:T(128)S(1)} %pad_add_fusion.pos_ref, bf16[512,1024]{1,0:T(8,128)(2,1)S(1)} %bitcast.24, bf16[1024,1024]{1,0:T(8,128)(2,1)S(1)} %copy-done.5, ...), custom_call_target="tpu_custom_call" | custom-call | tf_op jit(solution)/shard_map/grad_parts/pallas_call | solution.py:188
  105.5 1.5 collective-permute-start.26
  107.8 1.5 collective-permute-start.27
  109.3 1.9 collective-permute-done.31
  112.0 2.4 %collective-permute-start.28 = (bf16[512,512]{1,0:T(8,128)(2,1)}, bf16[512,512]{1,0:T(8,128)(2,1)}, u32[]{:S(2)}, u32[]{:S(2)}) collective-permute-start(bf16[512,512]{1,0:T(8,128)(2,1)} %get-tuple-element.37), channel_id=1, source_target_pairs={{0,3},{1,2},{2,1},{3,0},{4,7},{5,6},{6,5},{7,4},{8,11},{9,10},{10,... | collective-permute-start | bytes 1572872 | tf_op jit(solution)/shard_map/ppermute | solution.py:547
  114.8 1.6 copy-done.1
  117.6 4.8 %mix.3 = (f32[2,128,1024]{2,1,0:T(8,128)S(1)}, bf16[2,128,1024]{2,1,0:T(8,128)(2,1)}) custom-call(f32[64,256]{1,0:T(8,128)S(1)} %maximum_maximum_fusion.line_ref, bf16[2,256,1024]{2,1,0:T(8,128)(2,1)S(1)} %copy-done.4, bf16[2,256,1024]{2,1,0:T(8,128)(2,1)S(1)} %copy-done.4, f32[2,256,1024]{2,1,0:T(8,128)S(1)} %copy-done.1), custom_call_target="tpu_custom_call" | custom-call | tf_op jit(solution)/shard_map/mix/pallas_call | solution.py:106
  122.3 2.0 collective-permute-done.32
  124.7 1.7 collective-permute-start.23
  126.4 4.7 %mix.2 = (f32[2,128,1024]{2,1,0:T(8,128)S(1)}, bf16[2,128,1024]{2,1,0:T(8,128)(2,1)}) custom-call(f32[64,256]{1,0:T(8,128)S(1)} %maximum_maximum_fusion.line_ref, bf16[2,128,1024]{2,1,0:T(8,128)(2,1)S(1)} %copy-done.13, bf16[2,256,1024]{2,1,0:T(8,128)(2,1)S(1)} %copy-done.4, f32[2,256,1024]{2,1,0:T(8,128)S(1)} %copy-done.1), custom_call_target="tpu_custom_call" | custom-call | tf_op jit(solution)/shard_map/mix/pallas_call | solution.py:106
  131.1 2.9 %mix_grads.3 = (bf16[2,256,512]{2,1,0:T(8,128)(2,1)S(1)}, bf16[2,256,512]{2,1,0:T(8,128)(2,1)S(1)}, bf16[2,160,512]{2,1,0:T(8,128)(2,1)S(1)}) custom-call(f32[2,256,512]{2,1,0:T(8,128)S(1)} %bitcast.25, bf16[2,256,512]{2,1,0:T(8,128)(2,1)S(1)} %bitcast.27, bf16[2,256,512]{2,1,0:T(8,128)(2,1)} %bitcast.11.refs_2_, bf16[2,256,512]{2,1,0:T(8,128)(2,1)} %bitcast.12.refs_3_, ...), custom_call_target="tpu_custom_call" | custom-call | tf_op jit(solution)/shard_map/mix_grads/pallas_call | solution.py:304
  135.3 11.5 %collective-permute-done.27 = bf16[512,512]{1,0:T(8,128)(2,1)} collective-permute-done((bf16[512,512]{1,0:T(8,128)(2,1)}, bf16[512,512]{1,0:T(8,128)(2,1)}, u32[]{:S(2)}, u32[]{:S(2)}) %collective-permute-start.27) | collective-permute-done | bytes 524320 | tf_op jit(solution)/shard_map/ppermute | solution.py:547
  146.8 3.8 %mix_grads.2 = (bf16[2,256,512]{2,1,0:T(8,128)(2,1)S(1)}, bf16[2,256,512]{2,1,0:T(8,128)(2,1)S(1)}, bf16[2,160,512]{2,1,0:T(8,128)(2,1)}) custom-call(f32[2,256,512]{2,1,0:T(8,128)S(1)} %bitcast.26, bf16[2,256,512]{2,1,0:T(8,128)(2,1)} %bitcast.6.refs_1_, bf16[2,256,512]{2,1,0:T(8,128)(2,1)} %bitcast.7.refs_2_, bf16[2,256,512]{2,1,0:T(8,128)(2,1)} %bitcast.8.refs_3_, ...), custom_call_target="tpu_custom_call" | custom-call | tf_op jit(solution)/shard_map/mix_grads/pallas_call | solution.py:304
  151.4 1.6 collective-permute-start.29
  153.0 1.5 collective-permute-start.30
  154.5 12.6 %collective-permute-done.30 = bf16[2,2,2,1024]{3,2,1,0:T(2,128)(2,1)S(1)} collective-permute-done((bf16[2,2,2,1024]{3,2,1,0:T(2,128)(2,1)S(1)}, bf16[2,2,2,1024]{3,2,1,0:T(2,128)(2,1)S(1)}, u32[]{:S(2)}, u32[]{:S(2)}) %collective-permute-start.30) | collective-permute-done | bytes 16416 | tf_op jit(solution)/shard_map/ppermute | solution.py:28
  167.0 1.5 collective-permute-start.25
  168.6 3.0 %filter_sums.3 = f32[32,256]{1,0:T(8,128)S(1)} custom-call(bf16[2,256,512]{2,1,0:T(8,128)(2,1)S(1)} %get-tuple-element.50.mix_ref, bf16[2,256,1024]{2,1,0:T(8,128)(2,1)S(1)} %copy-done.4, bf16[2,128,1024]{2,1,0:T(8,128)(2,1)S(1)} %copy-done.13), custom_call_target="tpu_custom_call" | custom-call | tf_op jit(solution)/shard_map/filter_sums/pallas_call | solution.py:364
  172.3 3.0 %filter_sums.2 = f32[32,256]{1,0:T(8,128)S(1)} custom-call(bf16[2,256,512]{2,1,0:T(8,128)(2,1)S(1)} %get-tuple-element.40.mix_ref, bf16[2,256,1024]{2,1,0:T(8,128)(2,1)S(1)} %copy-done.4, bf16[2,128,1024]{2,1,0:T(8,128)(2,1)S(1)} %copy-done.13), custom_call_target="tpu_custom_call" | custom-call | tf_op jit(solution)/shard_map/filter_sums/pallas_call | solution.py:364
  176.0 1.5 collective-permute-start.20
  177.5 5.4 %input_grads.3 = (bf16[3,2,256,512]{3,2,1,0:T(8,128)(2,1)S(1)}, f32[9,512]{1,0:T(8,128)S(1)}) custom-call(f32[64,256]{1,0:T(8,128)S(1)} %concatenate.22.line_ref, bf16[2,256,512]{2,1,0:T(8,128)(2,1)S(1)} %get-tuple-element.50.mix_ref, bf16[2,256,512]{2,1,0:T(8,128)(2,1)S(1)} %get-tuple-element.51.query_ref, ...), custom_call_target="tpu_custom_call" | custom-call | tf_op jit(solution)/shard_map/input_grads/pallas_call | solution.py:476
  186.5 1.6 copy-done.8
  188.1 1.6 copy-done.11
  192.6 5.8 %input_grads.2 = (bf16[3,2,256,512]{3,2,1,0:T(8,128)(2,1)S(1)}, f32[9,512]{1,0:T(8,128)S(1)}) custom-call(f32[64,256]{1,0:T(8,128)S(1)} %concatenate.22.line_ref, bf16[2,256,512]{2,1,0:T(8,128)(2,1)S(1)} %copy-done.28, bf16[2,256,512]{2,1,0:T(8,128)(2,1)S(1)} %copy-done.49, bf16[2,160,512]{2,1,0:T(8,128)(2,1)} %collective-permute-done.29.back_ref, ...), custom_call_target="tpu_custom_call" | custom-call | tf_op jit(solution)/shard_map/input_grads/pallas_call | solution.py:476
  201.7 1.5 collective-permute-start.24
  205.6 2.8 %collective-permute-start.39 = (f32[68,128]{1,0:T(8,128)S(1)}, f32[68,128]{1,0:T(8,128)S(1)}, u32[]{:S(2)}, u32[]{:S(2)}) collective-permute-start(f32[68,128]{1,0:T(8,128)S(1)} %fusion), channel_id=1, source_target_pairs={{0,8},{4,12},{8,0},{12,4},{16,24},{20,28},{24,16},{28,20},{1,9},{5... | collective-permute-start | bytes 104456 | tf_op jit(solution)/shard_map/ppermute | solution.py:536
  209.4 3.2 %collective-permute-done.24.refs_18_ = bf16[2,128,1024]{2,1,0:T(8,128)(2,1)S(1)} collective-permute-done((bf16[2,128,1024]{2,1,0:T(8,128)(2,1)}, bf16[2,128,1024]{2,1,0:T(8,128)(2,1)S(1)}, u32[]{:S(2)}, u32[]{:S(2)}) %collective-permute-start.24) | collective-permute-done | bytes 524320 | tf_op jit(solution)/shard_map/ppermute | solution.py:547
  224.9 9.6 %block_output.1 = bf16[2,256,1024]{2,1,0:T(8,128)(2,1)} custom-call(s32[3]{0:T(128)S(1)} %pad_add_fusion.pos_ref, bf16[1024,1024]{1,0:T(8,128)(2,1)} %own_ref.5, bf16[256,1024]{1,0:T(8,128)(2,1)S(1)} %copy-done.23, bf16[256,1024]{1,0:T(8,128)(2,1)S(1)} %copy-done.15, bf16[256,1024]{1,0:T(8,128)(2,1)S(1)} %copy-done.25, bf16[256,1024]{1,0:T(8,128)(2,1)S(1)} %copy-done.19, ...), custom_call_target="tpu_custom_call" | custom-call | tf_op jit(solution)/shard_map/block_output/pallas_call | solution.py:258
  235.1 1.6 collective-permute-start.37
  237.1 2.0 copy.10
  (208 shorter events, 51.6 us)
Async XLA Ops:
  1.9 17.8 %collective-permute-start.7 = (bf16[256,1024]{1,0:T(8,128)(2,1)S(1)}, bf16[256,1024]{1,0:T(8,128)(2,1)}, u32[]{:S(2)}, u32[]{:S(2)}) collective-permute-start(bf16[256,1024]{1,0:T(8,128)(2,1)S(1)} %get-tuple-element.60), channel_id=1, source_target_pairs={{4,0},{8,4},{12,8},{5,1},{9,5},{13,9},{6,2},{10,6},{14,10},{7,3},{... | collective-permute-start | bytes 1572872 | tf_op jit(solution)/shard_map/ppermute | solution.py:28
  3.2 45.0 %copy-start.52 = (f32[3,3,1024]{2,1,0:T(4,128)S(1)}, f32[3,3,1024]{2,1,0:T(4,128)}, u32[]{:S(2)}) copy-start(f32[3,3,1024]{2,1,0:T(4,128)} %w_ref.5) | copy-start | bytes 110596
  3.2 27.7 %collective-permute-start.1 = (bf16[256,1024]{1,0:T(8,128)(2,1)S(1)}, bf16[256,1024]{1,0:T(8,128)(2,1)}, u32[]{:S(2)}, u32[]{:S(2)}) collective-permute-start(bf16[256,1024]{1,0:T(8,128)(2,1)S(1)} %get-tuple-element.61), channel_id=1, source_target_pairs={{4,0},{8,4},{12,8},{5,1},{9,5},{13,9},{6,2},{10,6},{14,10},{7,3},{... | collective-permute-start | bytes 1572872 | tf_op jit(solution)/shard_map/ppermute | solution.py:28
  4.7 27.6 %collective-permute-start = (bf16[256,1024]{1,0:T(8,128)(2,1)S(1)}, bf16[256,1024]{1,0:T(8,128)(2,1)}, u32[]{:S(2)}, u32[]{:S(2)}) collective-permute-start(bf16[256,1024]{1,0:T(8,128)(2,1)S(1)} %get-tuple-element.61), channel_id=1, source_target_pairs={{0,4},{4,8},{8,12},{1,5},{5,9},{9,13},{2,6},{6,10},{10,14},{3,7},{... | collective-permute-start | bytes 1572872 | tf_op jit(solution)/shard_map/ppermute | solution.py:28
  11.7 22.1 %collective-permute-start.6 = (bf16[256,1024]{1,0:T(8,128)(2,1)S(1)}, bf16[256,1024]{1,0:T(8,128)(2,1)}, u32[]{:S(2)}, u32[]{:S(2)}) collective-permute-start(bf16[256,1024]{1,0:T(8,128)(2,1)S(1)} %get-tuple-element.60), channel_id=1, source_target_pairs={{0,4},{4,8},{8,12},{1,5},{5,9},{9,13},{2,6},{6,10},{10,14},{3,7},{... | collective-permute-start | bytes 1572872 | tf_op jit(solution)/shard_map/ppermute | solution.py:28
  19.7 32.8 %collective-permute-start.8 = (bf16[256,1024]{1,0:T(8,128)(2,1)}, bf16[256,1024]{1,0:T(8,128)(2,1)}, u32[]{:S(2)}, u32[]{:S(2)}) collective-permute-start(bf16[256,1024]{1,0:T(8,128)(2,1)} %collective-permute-done.7), channel_id=1, source_target_pairs={{4,0},{8,4},{5,1},{9,5},{6,2},{10,6},{7,3},{11,7},{20,16},{24,20},... | collective-permute-start | bytes 1572872 | tf_op jit(solution)/shard_map/ppermute | solution.py:28
  30.9 22.9 %collective-permute-start.2 = (bf16[256,1024]{1,0:T(8,128)(2,1)}, bf16[256,1024]{1,0:T(8,128)(2,1)}, u32[]{:S(2)}, u32[]{:S(2)}) collective-permute-start(bf16[256,1024]{1,0:T(8,128)(2,1)} %collective-permute-done.1), channel_id=1, source_target_pairs={{4,0},{8,4},{5,1},{9,5},{6,2},{10,6},{7,3},{11,7},{20,16},{24,20},... | collective-permute-start | bytes 1572872 | tf_op jit(solution)/shard_map/ppermute | solution.py:28
  32.2 21.6 %collective-permute-start.4 = (bf16[256,1024]{1,0:T(8,128)(2,1)}, bf16[256,1024]{1,0:T(8,128)(2,1)}, u32[]{:S(2)}, u32[]{:S(2)}) collective-permute-start(bf16[256,1024]{1,0:T(8,128)(2,1)} %collective-permute-done), channel_id=1, source_target_pairs={{4,8},{8,12},{5,9},{9,13},{6,10},{10,14},{7,11},{11,15},{20,24},{2... | collective-permute-start | bytes 1572872 | tf_op jit(solution)/shard_map/ppermute | solution.py:28
  33.7 21.7 %collective-permute-start.10 = (bf16[256,1024]{1,0:T(8,128)(2,1)}, bf16[256,1024]{1,0:T(8,128)(2,1)}, u32[]{:S(2)}, u32[]{:S(2)}) collective-permute-start(bf16[256,1024]{1,0:T(8,128)(2,1)} %collective-permute-done.6), channel_id=1, source_target_pairs={{4,8},{8,12},{5,9},{9,13},{6,10},{10,14},{7,11},{11,15},{20,24},{2... | collective-permute-start | bytes 1572872 | tf_op jit(solution)/shard_map/ppermute | solution.py:28
  37.4 10.7 %collective-permute-start.18 = (bf16[3,2,2,1024]{3,2,1,0:T(2,128)(2,1)S(1)}, bf16[3,2,2,1024]{3,2,1,0:T(2,128)(2,1)S(1)}, u32[]{:S(2)}, u32[]{:S(2)}) collective-permute-start(bf16[3,2,2,1024]{3,2,1,0:T(2,128)(2,1)S(1)} %slice.44), channel_id=1, source_target_pairs={{0,4},{4,8},{8,12},{1,5},{5,9},{9,13},{2,6},{6,10},{10,14},{3,7},{... | collective-permute-start | bytes 73736 | tf_op jit(solution)/shard_map/ppermute | solution.py:28
  52.4 26.8 %copy-start = (f32[2,256,1024]{2,1,0:T(8,128)}, f32[2,256,1024]{2,1,0:T(8,128)S(1)}, u32[]{:S(2)}) copy-start(f32[2,256,1024]{2,1,0:T(8,128)S(1)} %get-tuple-element.31.q_ref.refs_4_) | copy-start | bytes 6291460
  52.5 24.6 %collective-permute-start.9 = (bf16[256,1024]{1,0:T(8,128)(2,1)}, bf16[256,1024]{1,0:T(8,128)(2,1)S(1)}, u32[]{:S(2)}, u32[]{:S(2)}) collective-permute-start(bf16[256,1024]{1,0:T(8,128)(2,1)} %collective-permute-done.8), channel_id=1, source_target_pairs={{4,0},{5,1},{6,2},{7,3},{20,16},{21,17},{22,18},{23,19}} | collective-permute-start | bytes 1572872 | tf_op jit(solution)/shard_map/ppermute | solution.py:28
  55.3 44.7 %copy-start.14 = (bf16[256,1024]{1,0:T(8,128)(2,1)}, bf16[256,1024]{1,0:T(8,128)(2,1)S(1)}, u32[]{:S(2)}) copy-start(bf16[256,1024]{1,0:T(8,128)(2,1)S(1)} %broadcast_select_fusion.3.refs_1_) | copy-start | bytes 1572868
  55.3 42.6 %collective-permute-start.13 = (bf16[256,1024]{1,0:T(8,128)(2,1)S(1)}, bf16[256,1024]{1,0:T(8,128)(2,1)S(1)}, u32[]{:S(2)}, u32[]{:S(2)}) collective-permute-start(bf16[256,1024]{1,0:T(8,128)(2,1)S(1)} %broadcast_select_fusion.3.refs_1_), channel_id=1, source_target_pairs={{0,16},{16,0},{1,17},{17,1},{2,18},{18,2},{3,19},{19,3},{4,20},{20... | collective-permute-start | bytes 1572872 | tf_op jit(solution)/shard_map/ppermute | solution.py:562
  55.4 22.5 %collective-permute-start.11 = (bf16[256,1024]{1,0:T(8,128)(2,1)}, bf16[256,1024]{1,0:T(8,128)(2,1)S(1)}, u32[]{:S(2)}, u32[]{:S(2)}) collective-permute-start(bf16[256,1024]{1,0:T(8,128)(2,1)} %collective-permute-done.10), channel_id=1, source_target_pairs={{8,12},{9,13},{10,14},{11,15},{24,28},{25,29},{26,30},{27,31}} | collective-permute-start | bytes 1572872 | tf_op jit(solution)/shard_map/ppermute | solution.py:28
  57.2 33.6 %copy-start.16 = (bf16[256,1024]{1,0:T(8,128)(2,1)}, bf16[256,1024]{1,0:T(8,128)(2,1)S(1)}, u32[]{:S(2)}) copy-start(bf16[256,1024]{1,0:T(8,128)(2,1)S(1)} %broadcast_select_fusion.2.refs_4_.refs_1_) | copy-start | bytes 1572868
  57.2 33.6 %copy-start.5 = (bf16[1024,1024]{1,0:T(8,128)(2,1)S(1)}, bf16[1024,1024]{1,0:T(8,128)(2,1)}, u32[]{:S(2)}) copy-start(bf16[1024,1024]{1,0:T(8,128)(2,1)} %own_ref.5) | copy-start | bytes 6291460
  57.3 33.6 %copy-start.26 = (bf16[2,256,1024]{2,1,0:T(8,128)(2,1)S(1)}, bf16[2,256,1024]{2,1,0:T(8,128)(2,1)}, u32[]{:S(2)}) copy-start(bf16[2,256,1024]{2,1,0:T(8,128)(2,1)} %param.9) | copy-start | bytes 3145732
  57.3 30.7 %collective-permute-start.16 = (bf16[256,1024]{1,0:T(8,128)(2,1)S(1)}, bf16[256,1024]{1,0:T(8,128)(2,1)S(1)}, u32[]{:S(2)}, u32[]{:S(2)}) collective-permute-start(bf16[256,1024]{1,0:T(8,128)(2,1)S(1)} %broadcast_select_fusion.2.refs_4_.refs_1_), channel_id=1, source_target_pairs={{0,16},{16,0},{1,17},{17,1},{2,18},{18,2},{3,19},{19,3},{4,20},{20... | collective-permute-start | bytes 1572872 | tf_op jit(solution)/shard_map/ppermute | solution.py:562
  57.8 28.4 %collective-permute-start.3 = (bf16[256,1024]{1,0:T(8,128)(2,1)}, bf16[256,1024]{1,0:T(8,128)(2,1)S(1)}, u32[]{:S(2)}, u32[]{:S(2)}) collective-permute-start(bf16[256,1024]{1,0:T(8,128)(2,1)} %collective-permute-done.2), channel_id=1, source_target_pairs={{4,0},{5,1},{6,2},{7,3},{20,16},{21,17},{22,18},{23,19}} | collective-permute-start | bytes 1572872 | tf_op jit(solution)/shard_map/ppermute | solution.py:28
  77.1 9.2 %collective-permute-start.5 = (bf16[256,1024]{1,0:T(8,128)(2,1)}, bf16[256,1024]{1,0:T(8,128)(2,1)S(1)}, u32[]{:S(2)}, u32[]{:S(2)}) collective-permute-start(bf16[256,1024]{1,0:T(8,128)(2,1)} %collective-permute-done.4), channel_id=1, source_target_pairs={{8,12},{9,13},{10,14},{11,15},{24,28},{25,29},{26,30},{27,31}} | collective-permute-start | bytes 1572872 | tf_op jit(solution)/shard_map/ppermute | solution.py:28
  77.9 10.3 %collective-permute-start.15 = (bf16[256,1024]{1,0:T(8,128)(2,1)S(1)}, bf16[256,1024]{1,0:T(8,128)(2,1)S(1)}, u32[]{:S(2)}, u32[]{:S(2)}) collective-permute-start(bf16[256,1024]{1,0:T(8,128)(2,1)S(1)} %broadcast_select_fusion.4.refs_3_.refs_0_), channel_id=1, source_target_pairs={{0,16},{16,0},{1,17},{17,1},{2,18},{18,2},{3,19},{19,3},{4,20},{20... | collective-permute-start | bytes 1572872 | tf_op jit(solution)/shard_map/ppermute | solution.py:562
  86.2 4.6 %collective-permute-start.17 = (bf16[256,1024]{1,0:T(8,128)(2,1)S(1)}, bf16[256,1024]{1,0:T(8,128)(2,1)S(1)}, u32[]{:S(2)}, u32[]{:S(2)}) collective-permute-start(bf16[256,1024]{1,0:T(8,128)(2,1)S(1)} %broadcast_select_fusion.refs_5_.refs_2_), channel_id=1, source_target_pairs={{0,16},{16,0},{1,17},{17,1},{2,18},{18,2},{3,19},{19,3},{4,20},{20... | collective-permute-start | bytes 1572872 | tf_op jit(solution)/shard_map/ppermute | solution.py:562
  86.3 13.2 %collective-permute-start.12 = (bf16[256,1024]{1,0:T(8,128)(2,1)S(1)}, bf16[256,1024]{1,0:T(8,128)(2,1)S(1)}, u32[]{:S(2)}, u32[]{:S(2)}) collective-permute-start(bf16[256,1024]{1,0:T(8,128)(2,1)S(1)} %broadcast_select_fusion.5.refs_0_), channel_id=1, source_target_pairs={{0,16},{16,0},{1,17},{17,1},{2,18},{18,2},{3,19},{19,3},{4,20},{20... | collective-permute-start | bytes 1572872 | tf_op jit(solution)/shard_map/ppermute | solution.py:562
  88.0 12.0 %collective-permute-start.14 = (bf16[256,1024]{1,0:T(8,128)(2,1)S(1)}, bf16[256,1024]{1,0:T(8,128)(2,1)S(1)}, u32[]{:S(2)}, u32[]{:S(2)}) collective-permute-start(bf16[256,1024]{1,0:T(8,128)(2,1)S(1)} %broadcast_select_fusion.1.refs_2_), channel_id=1, source_target_pairs={{0,16},{16,0},{1,17},{17,1},{2,18},{18,2},{3,19},{19,3},{4,20},{20... | collective-permute-start | bytes 1572872 | tf_op jit(solution)/shard_map/ppermute | solution.py:562
  88.2 18.8 %collective-permute-start.19 = (bf16[2,128,1024]{2,1,0:T(8,128)(2,1)S(1)}, bf16[2,128,1024]{2,1,0:T(8,128)(2,1)S(1)}, u32[]{:S(2)}, u32[]{:S(2)}) collective-permute-start(bf16[2,128,1024]{2,1,0:T(8,128)(2,1)S(1)} %slice.36), channel_id=1, source_target_pairs={{0,4},{4,8},{8,12},{1,5},{5,9},{9,13},{2,6},{6,10},{10,14},{3,7},{... | collective-permute-start | bytes 1572872 | tf_op jit(solution)/shard_map/ppermute | solution.py:28
  96.5 14.8 %collective-permute-start.31 = (bf16[512,512]{1,0:T(8,128)(2,1)S(1)}, bf16[512,512]{1,0:T(8,128)(2,1)S(1)}, u32[]{:S(2)}, u32[]{:S(2)}) collective-permute-start(bf16[512,512]{1,0:T(8,128)(2,1)S(1)} %get-tuple-element.47), channel_id=1, source_target_pairs={{0,1},{1,0},{2,3},{3,2},{4,5},{5,4},{6,7},{7,6},{8,9},{9,8},{10,11... | collective-permute-start | bytes 1572872 | tf_op jit(solution)/shard_map/ppermute | solution.py:547
  98.0 26.4 %collective-permute-start.32 = (bf16[512,512]{1,0:T(8,128)(2,1)}, bf16[512,512]{1,0:T(8,128)(2,1)}, u32[]{:S(2)}, u32[]{:S(2)}) collective-permute-start(bf16[512,512]{1,0:T(8,128)(2,1)} %get-tuple-element.48), channel_id=1, source_target_pairs={{0,2},{1,3},{2,0},{3,1},{4,6},{5,7},{6,4},{7,5},{8,10},{9,11},{10,... | collective-permute-start | bytes 1572872 | tf_op jit(solution)/shard_map/ppermute | solution.py:547
  99.5 25.1 %collective-permute-start.33 = (bf16[512,512]{1,0:T(8,128)(2,1)}, bf16[512,512]{1,0:T(8,128)(2,1)}, u32[]{:S(2)}, u32[]{:S(2)}) collective-permute-start(bf16[512,512]{1,0:T(8,128)(2,1)} %get-tuple-element.49), channel_id=1, source_target_pairs={{0,3},{1,2},{2,1},{3,0},{4,7},{5,6},{6,5},{7,4},{8,11},{9,10},{10,... | collective-permute-start | bytes 1572872 | tf_op jit(solution)/shard_map/ppermute | solution.py:547
  105.5 28.5 %collective-permute-start.26 = (bf16[512,512]{1,0:T(8,128)(2,1)}, bf16[512,512]{1,0:T(8,128)(2,1)}, u32[]{:S(2)}, u32[]{:S(2)}) collective-permute-start(bf16[512,512]{1,0:T(8,128)(2,1)} %get-tuple-element.35), channel_id=1, source_target_pairs={{0,1},{1,0},{2,3},{3,2},{4,5},{5,4},{6,7},{7,6},{8,9},{9,8},{10,11... | collective-permute-start | bytes 1572872 | tf_op jit(solution)/shard_map/ppermute | solution.py:547
  107.8 39.0 %collective-permute-start.27 = (bf16[512,512]{1,0:T(8,128)(2,1)}, bf16[512,512]{1,0:T(8,128)(2,1)}, u32[]{:S(2)}, u32[]{:S(2)}) collective-permute-start(bf16[512,512]{1,0:T(8,128)(2,1)} %get-tuple-element.36), channel_id=1, source_target_pairs={{0,2},{1,3},{2,0},{3,1},{4,6},{5,7},{6,4},{7,5},{8,10},{9,11},{10,... | collective-permute-start | bytes 1572872 | tf_op jit(solution)/shard_map/ppermute | solution.py:547
  112.0 34.8 %collective-permute-start.28 = (bf16[512,512]{1,0:T(8,128)(2,1)}, bf16[512,512]{1,0:T(8,128)(2,1)}, u32[]{:S(2)}, u32[]{:S(2)}) collective-permute-start(bf16[512,512]{1,0:T(8,128)(2,1)} %get-tuple-element.37), channel_id=1, source_target_pairs={{0,3},{1,2},{2,1},{3,0},{4,7},{5,6},{6,5},{7,4},{8,11},{9,10},{10,... | collective-permute-start | bytes 1572872 | tf_op jit(solution)/shard_map/ppermute | solution.py:547
  124.3 77.3 %collective-permute-start.21 = (bf16[2,128,1024]{2,1,0:T(8,128)(2,1)}, bf16[2,128,1024]{2,1,0:T(8,128)(2,1)}, u32[]{:S(2)}, u32[]{:S(2)}) collective-permute-start(bf16[2,128,1024]{2,1,0:T(8,128)(2,1)} %get-tuple-element.33.refs_13_), channel_id=1, source_target_pairs={{0,1},{1,0},{2,3},{3,2},{4,5},{5,4},{6,7},{7,6},{8,9},{9,8},{10,11... | collective-permute-start | bytes 1572872 | tf_op jit(solution)/shard_map/ppermute | solution.py:547
  124.7 78.5 %collective-permute-start.23 = (bf16[2,128,1024]{2,1,0:T(8,128)(2,1)}, bf16[2,128,1024]{2,1,0:T(8,128)(2,1)}, u32[]{:S(2)}, u32[]{:S(2)}) collective-permute-start(bf16[2,128,1024]{2,1,0:T(8,128)(2,1)} %get-tuple-element.33.refs_13_), channel_id=1, source_target_pairs={{0,2},{1,3},{2,0},{3,1},{4,6},{5,7},{6,4},{7,5},{8,10},{9,11},{10,... | collective-permute-start | bytes 1572872 | tf_op jit(solution)/shard_map/ppermute | solution.py:547
  134.0 42.0 %collective-permute-start.34 = (bf16[2,160,512]{2,1,0:T(8,128)(2,1)S(1)}, bf16[2,160,512]{2,1,0:T(8,128)(2,1)S(1)}, u32[]{:S(2)}, u32[]{:S(2)}) collective-permute-start(bf16[2,160,512]{2,1,0:T(8,128)(2,1)S(1)} %get-tuple-element.52), channel_id=1, source_target_pairs={{4,0},{8,4},{12,8},{5,1},{9,5},{13,9},{6,2},{10,6},{14,10},{7,3},{... | collective-permute-start | bytes 983048 | tf_op jit(solution)/shard_map/ppermute | solution.py:28
  151.4 31.5 %copy-start.27 = (bf16[2,256,512]{2,1,0:T(8,128)(2,1)}, bf16[2,256,512]{2,1,0:T(8,128)(2,1)S(1)}, u32[]{:S(2)}) copy-start(bf16[2,256,512]{2,1,0:T(8,128)(2,1)S(1)} %get-tuple-element.40.mix_ref) | copy-start | bytes 1572868
  151.4 34.6 %collective-permute-start.29 = (bf16[2,160,512]{2,1,0:T(8,128)(2,1)}, bf16[2,160,512]{2,1,0:T(8,128)(2,1)}, u32[]{:S(2)}, u32[]{:S(2)}) collective-permute-start(bf16[2,160,512]{2,1,0:T(8,128)(2,1)} %get-tuple-element.42), channel_id=1, source_target_pairs={{4,0},{8,4},{12,8},{5,1},{9,5},{13,9},{6,2},{10,6},{14,10},{7,3},{... | collective-permute-start | bytes 983048 | tf_op jit(solution)/shard_map/ppermute | solution.py:28
  153.0 14.0 %collective-permute-start.30 = (bf16[2,2,2,1024]{3,2,1,0:T(2,128)(2,1)S(1)}, bf16[2,2,2,1024]{3,2,1,0:T(2,128)(2,1)S(1)}, u32[]{:S(2)}, u32[]{:S(2)}) collective-permute-start(bf16[2,2,2,1024]{3,2,1,0:T(2,128)(2,1)S(1)} %slice.45), channel_id=1, source_target_pairs={{4,0},{8,4},{12,8},{5,1},{9,5},{13,9},{6,2},{10,6},{14,10},{7,3},{... | collective-permute-start | bytes 49160 | tf_op jit(solution)/shard_map/ppermute | solution.py:28
  167.0 42.1 %collective-permute-start.25 = (bf16[2,128,1024]{2,1,0:T(8,128)(2,1)}, bf16[2,128,1024]{2,1,0:T(8,128)(2,1)}, u32[]{:S(2)}, u32[]{:S(2)}) collective-permute-start(bf16[2,128,1024]{2,1,0:T(8,128)(2,1)} %get-tuple-element.33.refs_13_), channel_id=1, source_target_pairs={{0,3},{1,2},{2,1},{3,0},{4,7},{5,6},{6,5},{7,4},{8,11},{9,10},{10,... | collective-permute-start | bytes 1572872 | tf_op jit(solution)/shard_map/ppermute | solution.py:547
  176.0 33.4 %collective-permute-start.20 = (bf16[2,128,1024]{2,1,0:T(8,128)(2,1)}, bf16[2,128,1024]{2,1,0:T(8,128)(2,1)}, u32[]{:S(2)}, u32[]{:S(2)}) collective-permute-start(bf16[2,128,1024]{2,1,0:T(8,128)(2,1)} %get-tuple-element.32.refs_12_), channel_id=1, source_target_pairs={{0,1},{1,0},{2,3},{3,2},{4,5},{5,4},{6,7},{7,6},{8,9},{9,8},{10,11... | collective-permute-start | bytes 1572872 | tf_op jit(solution)/shard_map/ppermute | solution.py:547
  186.0 23.3 %collective-permute-start.22 = (bf16[2,128,1024]{2,1,0:T(8,128)(2,1)}, bf16[2,128,1024]{2,1,0:T(8,128)(2,1)}, u32[]{:S(2)}, u32[]{:S(2)}) collective-permute-start(bf16[2,128,1024]{2,1,0:T(8,128)(2,1)} %get-tuple-element.32.refs_12_), channel_id=1, source_target_pairs={{0,2},{1,3},{2,0},{3,1},{4,6},{5,7},{6,4},{7,5},{8,10},{9,11},{10,... | collective-permute-start | bytes 1572872 | tf_op jit(solution)/shard_map/ppermute | solution.py:547
  201.7 10.9 %collective-permute-start.24 = (bf16[2,128,1024]{2,1,0:T(8,128)(2,1)}, bf16[2,128,1024]{2,1,0:T(8,128)(2,1)S(1)}, u32[]{:S(2)}, u32[]{:S(2)}) collective-permute-start(bf16[2,128,1024]{2,1,0:T(8,128)(2,1)} %get-tuple-element.32.refs_12_), channel_id=1, source_target_pairs={{0,3},{1,2},{2,1},{3,0},{4,7},{5,6},{6,5},{7,4},{8,11},{9,10},{10,... | collective-permute-start | bytes 1572872 | tf_op jit(solution)/shard_map/ppermute | solution.py:547
  203.2 1.2 collective-permute-start.38
  204.4 1.2 collective-permute-start.35
  205.6 28.8 %collective-permute-start.39 = (f32[68,128]{1,0:T(8,128)S(1)}, f32[68,128]{1,0:T(8,128)S(1)}, u32[]{:S(2)}, u32[]{:S(2)}) collective-permute-start(f32[68,128]{1,0:T(8,128)S(1)} %fusion), channel_id=1, source_target_pairs={{0,8},{4,12},{8,0},{12,4},{16,24},{20,28},{24,16},{28,20},{1,9},{5... | collective-permute-start | bytes 104456 | tf_op jit(solution)/shard_map/ppermute | solution.py:536
  209.1 25.9 %collective-permute-start.36 = (f32[68,128]{1,0:T(8,128)S(1)}, f32[68,128]{1,0:T(8,128)S(1)}, u32[]{:S(2)}, u32[]{:S(2)}) collective-permute-start(f32[68,128]{1,0:T(8,128)S(1)} %fusion.1), channel_id=1, source_target_pairs={{0,8},{4,12},{8,0},{12,4},{16,24},{20,28},{24,16},{28,20},{1,9},{5... | collective-permute-start | bytes 104456 | tf_op jit(solution)/shard_map/ppermute | solution.py:536
  234.5 4.6 %collective-permute-start.40 = (f32[68,128]{1,0:T(8,128)S(1)}, f32[68,128]{1,0:T(8,128)S(1)}, u32[]{:S(2)}, u32[]{:S(2)}) collective-permute-start(f32[68,128]{1,0:T(8,128)S(1)} %add.38), channel_id=1, source_target_pairs={{0,4},{4,0},{8,12},{12,8},{16,20},{20,16},{24,28},{28,24},{1,5},{5... | collective-permute-start | bytes 104456 | tf_op jit(solution)/shard_map/ppermute | solution.py:536
  235.1 4.0 %collective-permute-start.37 = (f32[68,128]{1,0:T(8,128)S(1)}, f32[68,128]{1,0:T(8,128)S(1)}, u32[]{:S(2)}, u32[]{:S(2)}) collective-permute-start(f32[68,128]{1,0:T(8,128)S(1)} %add.35), channel_id=1, source_target_pairs={{0,4},{4,0},{8,12},{12,8},{16,20},{20,16},{24,28},{28,24},{1,5},{5... | collective-permute-start | bytes 104456 | tf_op jit(solution)/shard_map/ppermute | solution.py:536
  (52 other events, 386.1 us)

commit v2 on v1

v2 whole, which is shorter than its diff:
```python
import functools
import math

import jax
import jax.numpy as jnp
from jax import lax
from jax.experimental import pallas as pl
from jax.experimental.pallas import tpu as pltpu
from jax.sharding import PartitionSpec as P

LANES = 128
HALO = 144
FIRST = 3
EXTRA = 16
F32 = jnp.float32
BF16 = jnp.bfloat16


def params(mib=24):
    return pltpu.CompilerParams(vmem_limit_bytes=mib * 1024 * 1024)


def shift(block, axis, distance):
    devices = range(lax.axis_size(axis))
    route = [(i, i + distance) for i in devices if i + distance in devices]
    return lax.ppermute(block, axis, route)


def after(block, *others):
    return lax.optimization_barrier((block, *others))[0]


def pick_groups(stacked, rows, group_size):
    width = stacked.shape[1]
    lane = lax.broadcasted_iota(jnp.int32, (1, width), 1) % LANES
    groups = LANES // group_size
    total = stacked[:rows]
    for g in range(1, groups):
        total = jnp.where(lane >= g * group_size, stacked[g * rows : (g + 1) * rows], total)
    return total


def fill_band(line_ref, band_ref, rows):
    for g in range(line_ref.shape[0]):
        wide = jnp.broadcast_to(line_ref[g : g + 1, :], (rows, line_ref.shape[1]))
        moved = pltpu.roll(wide, 0, 1, stride=1, stride_axis=0)
        band_ref[g * rows : (g + 1) * rows, :] = moved.astype(BF16)


def convolve(x_ref, w_ref, pad, j, s, head):
    rows = x_ref.shape[2]
    own = s * 3 + j
    pad[own, 0:8] = head
    pad[own, 8 : 8 + rows] = x_ref[j, s].astype(F32)
    total = w_ref[j, 0:1] * pad[own, 8 : 8 + rows]
    total = total + w_ref[j, 1:2] * pad[own, 7 : 7 + rows]
    return total + w_ref[j, 2:3] * pad[own, 6 : 6 + rows]


def front_rows(front_ref, j, s, taps):
    return front_ref[s, taps : taps + 2 * EXTRA].astype(F32)[j * 8 : j * 8 + 8]


def product_kernel(x_ref, w_ref, product_ref, pack_ref, pad):
    seqs, rows = x_ref.shape[1], x_ref.shape[2]
    taps = pack_ref.shape[1] - 2 * EXTRA
    nothing = jnp.zeros((8, LANES), F32)
    for s in range(seqs):
        keys = convolve(x_ref, w_ref, pad, 1, s, nothing)
        values = convolve(x_ref, w_ref, pad, 2, s, nothing)
        product = (keys * values).astype(BF16)
        product_ref[s] = product
        pack_ref[s, :taps] = product[rows - taps :]
        tails = [x_ref[j, s, rows - 16 :].astype(F32)[8:] for j in range(3)]
        pack_ref[s, taps:] = jnp.concatenate(tails + [nothing], axis=0).astype(BF16)


def products(x, short_w, taps):
    _, seqs, rows, width = x.shape
    at3 = lambda i: (0, 0, i)
    return pl.pallas_call(
        product_kernel,
        grid=(width // LANES,),
        in_specs=[
            pl.BlockSpec((3, seqs, rows, LANES), lambda i: (0, 0, 0, i)),
            pl.BlockSpec((3, 3, LANES), at3),
        ],
        out_specs=[
            pl.BlockSpec((seqs, rows, LANES), at3),
            pl.BlockSpec((seqs, taps + 2 * EXTRA, LANES), at3),
        ],
        out_shape=[
            jax.ShapeDtypeStruct((seqs, rows, width), BF16),
            jax.ShapeDtypeStruct((seqs, taps + 2 * EXTRA, width), BF16),
        ],
        scratch_shapes=[pltpu.VMEM((3 * seqs, rows + 8, LANES), F32)],
        compiler_params=params(),
        name="products",
    )(x, short_w)


def mix_high_kernel(
    group_size, line_ref, low_ref, high_ref, x_ref, w_ref, mixed_ref, gated_ref, band, columns, pad
):
    seqs, rows = low_ref.shape[0], low_ref.shape[1]
    fill_band(line_ref, band, rows)
    for s in range(seqs):
        at = slice(s * LANES, (s + 1) * LANES)
        columns[:rows, at] = low_ref[s]
        columns[rows:, at] = high_ref[s]
    stacked = jnp.dot(band[...], columns[...], preferred_element_type=F32)
    mixed = pick_groups(stacked, rows, group_size)
    nothing = jnp.zeros((8, LANES), F32)
    for s in range(seqs):
        part = mixed[:, s * LANES : (s + 1) * LANES]
        mixed_ref[s] = part
        query = convolve(x_ref, w_ref, pad, 0, s, nothing)[rows:]
        gated_ref[s] = (query * part).astype(BF16)


def mix_high(line, product, x, short_w, rows, group_size):
    _, seqs, length, width = x.shape
    groups = LANES // group_size
    part = lambda at: pl.BlockSpec((seqs, rows, LANES), lambda i: (0, at, i))
    shape = (seqs, rows, width)
    return pl.pallas_call(
        functools.partial(mix_high_kernel, group_size),
        grid=(width // LANES,),
        in_specs=[
            pl.BlockSpec((groups, 2 * rows), lambda i: (i, 0)),
            part(0),
            part(1),
            pl.BlockSpec((1, seqs, length, LANES), lambda i: (0, 0, 0, i)),
            pl.BlockSpec((3, 3, LANES), lambda i: (0, 0, i)),
        ],
        out_specs=[part(0), part(0)],
        out_shape=[jax.ShapeDtypeStruct(shape, F32), jax.ShapeDtypeStruct(shape, BF16)],
        scratch_shapes=[
            pltpu.VMEM((groups * rows, 2 * rows), BF16),
            pltpu.VMEM((2 * rows, seqs * LANES), BF16),
            pltpu.VMEM((3 * seqs, length + 8, LANES), F32),
        ],
        compiler_params=params(),
        name="mix_high",
    )(line, product, product, x, short_w)


def mix_low_kernel(
    group_size,
    line_ref,
    front_ref,
    product_ref,
    x_ref,
    w_ref,
    mixed_ref,
    gated_ref,
    head_ref,
    band,
    columns,
    pad,
):
    seqs, rows = product_ref.shape[0], product_ref.shape[1]
    fill_band(line_ref, band, rows)
    queries = []
    for s in range(seqs):
        at = slice(s * LANES, (s + 1) * LANES)
        found = [
            convolve(x_ref, w_ref, pad, j, s, front_rows(front_ref, j, s, rows)) for j in range(3)
        ]
        queries.append(found[0])
        head = (found[1][:EXTRA] * found[2][:EXTRA]).astype(BF16)
        head_ref[s] = head
        columns[:rows, at] = front_ref[s, :rows]
        columns[rows : rows + EXTRA, at] = head
        columns[rows + EXTRA :, at] = product_ref[s, EXTRA:]
    stacked = jnp.dot(band[...], columns[...], preferred_element_type=F32)
    mixed = pick_groups(stacked, rows, group_size)
    for s in range(seqs):
        part = mixed[:, s * LANES : (s + 1) * LANES]
        mixed_ref[s] = part
        gated_ref[s] = (queries[s] * part).astype(BF16)


def mix_low(line, front, product, x, short_w, rows, group_size):
    _, seqs, _, width = x.shape
    groups = LANES // group_size
    part = lambda count: pl.BlockSpec((seqs, count, LANES), lambda i: (0, 0, i))
    shape = (seqs, rows, width)
    return pl.pallas_call(
        functools.partial(mix_low_kernel, group_size),
        grid=(width // LANES,),
        in_specs=[
            pl.BlockSpec((groups, 2 * rows), lambda i: (i, 0)),
            part(front.shape[1]),
            part(rows),
            pl.BlockSpec((3, seqs, rows, LANES), lambda i: (0, 0, 0, i)),
            pl.BlockSpec((3, 3, LANES), lambda i: (0, 0, i)),
        ],
        out_specs=[part(rows), part(rows), part(EXTRA)],
        out_shape=[
            jax.ShapeDtypeStruct(shape, F32),
            jax.ShapeDtypeStruct(shape, BF16),
            jax.ShapeDtypeStruct((seqs, EXTRA, width), BF16),
        ],
        scratch_shapes=[
            pltpu.VMEM((groups * rows, 2 * rows), BF16),
            pltpu.VMEM((2 * rows, seqs * LANES), BF16),
            pltpu.VMEM((3 * seqs, rows + 8, LANES), F32),
        ],
        compiler_params=params(),
        name="mix_low",
    )(line, front, product, x, short_w)


class Gathered:
    def __init__(self, w, steps, start):
        self.arrays, self.start, self.span = [w], start, w.shape[0] // steps

    def fetch(self, pos_ref, refs, buffer, base, sems, partner):
        owner = lax.bitwise_xor(pos_ref[2], partner)
        rows = pl.ds(pl.multiple_of(owner * self.span, self.span), self.span)
        place = buffer.at[partner, pl.ds(base, self.span)]
        copy = pltpu.make_async_copy(refs[0].at[rows], place, sems.at[partner, 0])
        copy.start()
        return [copy]


class Passed:
    def __init__(self, own, near, far, start):
        self.arrays, self.start, self.span = [own, *near, *far], start, 2 * near[0].shape[0]

    def fetch(self, pos_ref, refs, buffer, base, sems, partner):
        steps, half = (len(refs) + 1) // 2, self.span // 2
        owner = lax.bitwise_xor(pos_ref[2], partner)
        step = lax.rem(pos_ref[0] - owner + steps, steps)
        mine = pl.multiple_of(pos_ref[1] * half, half)
        other = pl.multiple_of((1 - pos_ref[1]) * half, half)

        def copies(first, second):
            return [
                pltpu.make_async_copy(
                    source, buffer.at[partner, pl.ds(base + place, half)], sems.at[partner, which]
                )
                for which, (source, place) in enumerate(((first, mine), (second, other)))
            ]

        for distance in range(steps):

            @pl.when(step == distance)
            def _(distance=distance):
                if distance == 0:
                    pair = [refs[0].at[pl.ds(self.start + at, half)] for at in (mine, other)]
                else:
                    pair = [refs[distance], refs[steps - 1 + distance]]
                for copy in copies(*pair):
                    copy.start()

        return copies(refs[1], refs[steps])


def grad_kernel(weights, steps, pos_ref, cot_ref, *refs):
    held = len(weights.arrays)
    outs, (buffer, sems) = refs[held : held + steps], refs[held + steps :]
    order = list(range(1, steps)) + [0]
    copies = {
        partner: weights.fetch(pos_ref, refs[:held], buffer, 0, sems, partner)
        for partner in order
    }
    for partner in order:
        for copy in copies[partner]:
            copy.wait()
        outs[partner][...] = lax.dot_general(
            cot_ref[...],
            buffer[partner],
            (((1,), (1,)), ((), ())),
            preferred_element_type=F32,
        ).astype(outs[partner].dtype)


def grad_parts(pos, cotangent, weights, steps):
    rows, width = cotangent.shape
    span = weights.span
    inside = pl.BlockSpec(memory_space=pltpu.VMEM)
    return pl.pallas_call(
        functools.partial(grad_kernel, weights, steps),
        in_specs=[pl.BlockSpec(memory_space=pltpu.SMEM), inside]
        + [pl.BlockSpec(memory_space=pl.ANY)] * len(weights.arrays),
        out_specs=[inside] * steps,
        out_shape=[jax.ShapeDtypeStruct((rows, span), F32)]
        + [jax.ShapeDtypeStruct((rows, span), BF16)] * (steps - 1),
        scratch_shapes=[
            pltpu.VMEM((steps, span, width), BF16),
            pltpu.SemaphoreType.DMA((steps, 2)),
        ],
        compiler_params=params(56),
        name="grad_parts",
    )(pos, cotangent, *weights.arrays)


def out_kernel(weights, steps, pos_ref, *refs):
    out_ref, buffer, *sems = refs[-2 - len(weights) :]
    copies = {partner: [] for partner in range(steps)}
    for piece, piece_sems in zip(weights, sems):
        held, refs = refs[: len(piece.arrays)], refs[len(piece.arrays) :]
        for partner in range(steps):
            copies[partner] += piece.fetch(
                pos_ref, held, buffer, piece.start, piece_sems, partner
            )
    total = None
    for partner in range(steps):
        for copy in copies[partner]:
            copy.wait()
        left = refs[partner][...].reshape(-1, buffer.shape[1])
        term = jnp.dot(left, buffer[partner], preferred_element_type=F32)
        total = term if total is None else total + term
    out_ref[...] = total.astype(BF16).reshape(out_ref.shape)


def block_output(pos, weights, gated, at, blocks, before):
    steps = len(gated)
    seqs, rows, depth = gated[0].shape
    width = weights[0].arrays[0].shape[1]
    inside = pl.BlockSpec(memory_space=pltpu.VMEM)
    anywhere = pl.BlockSpec(memory_space=pl.ANY)
    arrays = [array for piece in weights for array in piece.arrays]
    before = [] if before is None else [before]
    return pl.pallas_call(
        functools.partial(out_kernel, weights, steps),
        grid=(1,),
        in_specs=[pl.BlockSpec(memory_space=pltpu.SMEM)]
        + [anywhere] * len(arrays)
        + [inside] * steps
        + [anywhere] * len(before),
        out_specs=pl.BlockSpec((seqs, rows, width), lambda i: (0, at, 0)),
        out_shape=jax.ShapeDtypeStruct((seqs, blocks * rows, width), BF16),
        scratch_shapes=[pltpu.VMEM((steps, depth, width), BF16)]
        + [pltpu.SemaphoreType.DMA((steps, 2))] * len(weights),
        input_output_aliases={1 + len(arrays) + steps: 0} if before else {},
        compiler_params=params(56),
        name="block_output",
    )(pos, *arrays, *gated, *before)


def mix_grad_kernel(steps, *refs):
    terms = refs[:steps]
    low_ref, high_ref, x_ref, front_ref, w_ref, mix_ref, query_ref, pack_ref, pad = refs[steps:]
    seqs, rows = x_ref.shape[1], low_ref.shape[1]
    for s in range(seqs):
        query = convolve(x_ref, w_ref, pad, 0, s, front_rows(front_ref, 0, s, rows))
        for b, mixed_ref in enumerate((low_ref, high_ref)):
            at = slice(b * rows, (b + 1) * rows)
            total = terms[0][s, at].astype(F32)
            for term in terms[1:]:
                total = total + term[s, at].astype(F32)
            gated_grad = total.astype(BF16).astype(F32)
            mix_ref[s, at] = (gated_grad * query[at]).astype(BF16)
            query_ref[s, at] = (gated_grad * mixed_ref[s]).astype(BF16)
        pack_ref[s, :HALO] = mix_ref[s, :HALO]
        pack_ref[s, HALO : HALO + EXTRA] = query_ref[s, :EXTRA]
        heads = [x_ref[j, s, :EXTRA].astype(F32)[:8] for j in (1, 2)]
        pack_ref[s, HALO + EXTRA :] = jnp.concatenate(heads, axis=0).astype(BF16)


def mix_grads(terms, mixed, x, front, short_w, offset):
    seqs, rows, width = terms[0].shape
    half = rows // 2
    first = offset // LANES
    local = lambda count: pl.BlockSpec((seqs, count, LANES), lambda i: (0, 0, i))
    wide = lambda count: pl.BlockSpec((seqs, count, LANES), lambda i: (0, 0, first + i))
    return pl.pallas_call(
        functools.partial(mix_grad_kernel, len(terms)),
        grid=(width // LANES,),
        in_specs=[local(rows)] * len(terms)
        + [wide(half), wide(half)]
        + [
            pl.BlockSpec((3, seqs, rows, LANES), lambda i: (0, 0, 0, first + i)),
            wide(front.shape[1]),
            pl.BlockSpec((3, 3, LANES), lambda i: (0, 0, first + i)),
        ],
        out_specs=[local(rows), local(rows), local(HALO + 2 * EXTRA)],
        out_shape=[
            jax.ShapeDtypeStruct((seqs, rows, width), BF16),
            jax.ShapeDtypeStruct((seqs, rows, width), BF16),
            jax.ShapeDtypeStruct((seqs, HALO + 2 * EXTRA, width), BF16),
        ],
        scratch_shapes=[pltpu.VMEM((3 * seqs, rows + 8, LANES), F32)],
        compiler_params=params(),
        name="mix_grads",
    )(*terms, *mixed, x, front, short_w)


def filter_kernel(
    group_size, mix_ref, product_ref, head_ref, front_ref, out_ref, left, columns
):
    seqs = mix_ref.shape[0]
    rows = out_ref.shape[1]
    groups = LANES // group_size
    lane = lax.broadcasted_iota(jnp.int32, (1, LANES), 1) // group_size
    total = None
    for b in range(mix_ref.shape[1] // rows):
        for s in range(seqs):
            at = slice(s * LANES, (s + 1) * LANES)
            block = mix_ref[s, b * rows : (b + 1) * rows]
            for g in range(groups):
                keep = (lane == g).astype(F32).astype(BF16)
                left[b, g * rows : (g + 1) * rows, at] = block * keep
            if b == 0:
                columns[b, :rows, at] = front_ref[s, :rows]
            else:
                columns[b, :rows, at] = product_ref[s, (b - 1) * rows : b * rows]
            columns[b, rows:, at] = product_ref[s, b * rows : (b + 1) * rows]
            if b < 2:
                start = (1 - b) * rows
                columns[b, start : start + EXTRA, at] = head_ref[s]
        term = lax.dot_general(
            left[b], columns[b], (((1,), (1,)), ((), ())), preferred_element_type=F32
        )
        total = term if total is None else total + term
    span = 2 * rows
    folded = []
    for g in range(groups):
        sum_g = None
        for a in range(rows // 8):
            tile = total[g * rows + a * 8 : g * rows + a * 8 + 8]
            tile = pltpu.roll(tile, (span - a * 8) % span, 1)
            sum_g = tile if sum_g is None else sum_g + tile
        folded.append(sum_g)
    stacked = jnp.stack(folded, axis=0)
    result = None
    for r in range(8):
        row = pltpu.roll(stacked[:, r, :], span - r - 1, 1)
        result = row if result is None else result + row
    out_ref[...] = result[:, :rows]


def filter_sums(mix_grad, product, head, front, block_rows, offset, group_size):
    seqs, rows, width = mix_grad.shape
    first = offset // LANES
    groups = LANES // group_size
    blocks = rows // block_rows
    return pl.pallas_call(
        functools.partial(filter_kernel, group_size),
        grid=(width // LANES,),
        in_specs=[
            pl.BlockSpec((seqs, rows, LANES), lambda i: (0, 0, i)),
            pl.BlockSpec((seqs, rows, LANES), lambda i: (0, 0, first + i)),
            pl.BlockSpec((seqs, EXTRA, LANES), lambda i: (0, 0, first + i)),
            pl.BlockSpec((seqs, front.shape[1], LANES), lambda i: (0, 0, first + i)),
        ],
        out_specs=pl.BlockSpec((groups, block_rows), lambda i: (i, 0)),
        out_shape=jax.ShapeDtypeStruct((width // group_size, block_rows), F32),
        scratch_shapes=[
            pltpu.VMEM((blocks, groups * block_rows, seqs * LANES), BF16),
            pltpu.VMEM((blocks, 2 * block_rows, seqs * LANES), BF16),
        ],
        compiler_params=params(),
        name="filter_sums",
    )(mix_grad, product, head, front)


def input_grad_kernel(
    group_size,
    line_ref,
    mix_ref,
    query_ref,
    back_ref,
    x_ref,
    front_ref,
    w_ref,
    filter_ref,
    out_ref,
    sums_ref,
    band,
    columns,
    grads,
    inputs,
    edge,
):
    seqs, rows = mix_ref.shape[0], mix_ref.shape[1]
    block = line_ref.shape[1] // 2
    groups = LANES // group_size
    fill_band(line_ref, band, block)
    found = []
    for b in range(rows // block):
        for s in range(seqs):
            at = slice(s * LANES, (s + 1) * LANES)
            columns[b, :block, at] = mix_ref[s, b * block : (b + 1) * block]
            if (b + 1) * block < rows:
                columns[b, block:, at] = mix_ref[s, (b + 1) * block : (b + 2) * block]
            else:
                columns[b, block:, at] = back_ref[s, :block]
        stacked = jnp.dot(band[...], columns[b], preferred_element_type=F32)
        found.append(pick_groups(stacked, block, group_size))
    last = rows // block
    for s in range(seqs):
        at = slice(s * LANES, (s + 1) * LANES)
        columns[last, :HALO, at] = back_ref[s, :HALO]
        columns[last, HALO:, at] = jnp.zeros((2 * block - HALO, LANES), BF16)
    few = jnp.concatenate([band[g * block : g * block + EXTRA] for g in range(groups)], axis=0)
    stacked = jnp.dot(few, columns[last], preferred_element_type=F32)
    beyond = pick_groups(stacked, EXTRA, group_size)
    for s in range(seqs):
        at = slice(s * LANES, (s + 1) * LANES)
        after = []
        for j in (1, 2):
            own = s * 2 + j - 1
            edge[own, 0:8] = x_ref[j, s, rows - 16 :].astype(F32)[8:]
            edge[own, 8:16] = back_ref[s, HALO + EXTRA :].astype(F32)[8 * j - 8 : 8 * j]
            total = w_ref[j, 0:1] * edge[own, 8:16]
            total = total + w_ref[j, 1:2] * edge[own, 7:15]
            total = total + w_ref[j, 2:3] * edge[own, 6:14]
            after.append(total)
        streams = [
            convolve(x_ref, w_ref, inputs, j, s, front_rows(front_ref, j, s, block))
            for j in range(1, 3)
        ]
        inputs[s * 3, 0:8] = front_rows(front_ref, 0, s, block)
        inputs[s * 3, 8 : 8 + rows] = x_ref[0, s].astype(F32)
        for j in range(3):
            own = s * 3 + j
            if j == 0:
                grads[own, :rows] = query_ref[s].astype(F32)
                grads[own, rows:] = back_ref[s, HALO : HALO + EXTRA].astype(F32)[:8]
            else:
                factor = streams[2 - j]
                for b in range(rows // block):
                    part = slice(b * block, (b + 1) * block)
                    value = found[b][:, at] * factor[part]
                    grads[own, part] = value.astype(BF16).astype(F32)
                value = beyond[:8, at] * after[2 - j]
                grads[own, rows:] = value.astype(BF16).astype(F32)
            total = None
            for i in range(3):
                term = w_ref[j, i : i + 1] * grads[own, i : i + rows]
                total = term if total is None else total + term
            out_ref[j, s] = total.astype(BF16)
    for j in range(3):
        for i in range(3):
            total = None
            for s in range(seqs):
                own = s * 3 + j
                term = grads[own, :rows] * inputs[own, 8 - i : 8 - i + rows]
                term = jnp.sum(term, axis=0, keepdims=True)
                total = term if total is None else total + term
            sums_ref[0, groups + j * 3 + i : groups + j * 3 + i + 1] = total
    sums_ref[0, :groups] = filter_ref[...]
    sums_ref[0, groups + 9 :] = jnp.zeros((sums_ref.shape[1] - groups - 9, LANES), F32)


def input_grads(
    line, mix_grad, query_grad, back, x, front, short_w, filter_part, offset, group_size
):
    seqs, rows, width = mix_grad.shape
    block = line.shape[1] // 2
    first = offset // LANES
    groups = LANES // group_size
    local = lambda count: pl.BlockSpec((seqs, count, LANES), lambda i: (0, 0, i))
    wide3 = lambda *sizes: pl.BlockSpec(sizes + (LANES,), lambda i: (0, 0, first + i))
    wide4 = lambda *sizes: pl.BlockSpec(sizes + (LANES,), lambda i: (0, 0, 0, first + i))
    return pl.pallas_call(
        functools.partial(input_grad_kernel, group_size),
        grid=(width // LANES,),
        in_specs=[
            pl.BlockSpec((groups, 2 * block), lambda i: (first + i, 0)),
            local(rows),
            local(rows),
            local(HALO + 2 * EXTRA),
            wide4(3, seqs, rows),
            wide3(seqs, front.shape[1]),
            wide3(3, 3),
            pl.BlockSpec((groups, block), lambda i: (i, 0)),
        ],
        out_specs=[
            pl.BlockSpec((3, seqs, rows, LANES), lambda i: (0, 0, 0, i)),
            pl.BlockSpec((1, groups + 16, LANES), lambda i: (i, 0, 0)),
        ],
        out_shape=[
            jax.ShapeDtypeStruct((3, seqs, rows, width), BF16),
            jax.ShapeDtypeStruct((width // LANES, groups + 16, LANES), F32),
        ],
        scratch_shapes=[
            pltpu.VMEM((groups * block, 2 * block), BF16),
            pltpu.VMEM((rows // block + 1, 2 * block, seqs * LANES), BF16),
            pltpu.VMEM((3 * seqs, rows + 8, LANES), F32),
            pltpu.VMEM((3 * seqs, rows + 8, LANES), F32),
            pltpu.VMEM((2 * seqs, 16, LANES), F32),
        ],
        compiler_params=params(),
        name="input_grads",
    )(line, mix_grad, query_grad, back, x, front, short_w, filter_part)


def total_over(block, axes):
    count = math.prod(lax.axis_size(axis) for axis in axes)
    if count & (count - 1):
        return lax.psum(block, axes)
    step = count // 2
    order = []
    while step:
        order.append(step)
        step //= 2
    for step in order:
        block = block + lax.ppermute(block, axes, [(i, i ^ step) for i in range(count)])
    return block


def shards(projected, short_w, medium_h, out_w, grad_out):
    seqs, rows, _, width = projected.shape
    taps = medium_h.shape[1]
    group_size = width // medium_h.shape[0]
    groups = LANES // group_size
    members = lax.axis_size("grp")
    cores = lax.axis_size("dp")
    length = lax.axis_size("ctx")
    partners = range(members)
    to = lambda block, k: lax.ppermute(block, "grp", [(i, i ^ k) for i in partners])
    around = lambda block: lax.ppermute(block, "ctx", [(i, (i + 1) % length) for i in range(length)])
    swap = lambda block: lax.ppermute(block, "dp", [(0, 1), (1, 0)])
    core = lax.axis_index("dp")
    pos = jnp.stack([lax.axis_index("ctx"), core, lax.axis_index("grp")]).astype(jnp.int32)

    depth = out_w.shape[0]
    ring = depth == width and cores == 2
    cut = width * FIRST // 8 if ring else depth

    def own_half(start, stop):
        half = (stop - start) // cores
        return lax.dynamic_slice_in_dim(out_w, start + core * half, half, axis=0)

    first = lax.all_gather(own_half(0, cut), ("ctx", "dp"), axis=0, tiled=True)
    weights = [Gathered(first, members, 0)]
    if ring:
        near = [around(own_half(cut, depth))]

    x = jnp.transpose(projected, (2, 0, 1, 3))
    filters = medium_h.astype(F32)
    empty = jnp.zeros_like(filters)
    causal = jnp.concatenate([empty[:, :1], filters[:, ::-1], empty[:, 1:]], axis=1)
    anticausal = jnp.concatenate([filters, empty], axis=1)

    cotangent = grad_out.reshape(seqs * rows, width)
    product, pack = products(x, short_w, taps)
    mixed_high, gated_high = mix_high(causal, product, x, short_w, taps, group_size)
    high = [gated_high] + [to(gated_high, k) for k in partners[1:]]
    if ring:
        near.append(around(after(near[-1], mixed_high)))
        for _ in range(length - 3):
            near.append(around(after(near[-1], *high[1:])))

    def send_parts(piece, ready, before):
        parts = grad_parts(pos, after(cotangent, *ready), piece, members)
        shape = (seqs, rows, piece.span)
        parts = [after(block, *before) for block in parts]
        sent = [parts[0]] + [to(parts[k], k) for k in partners[1:]]
        return [block.reshape(shape) for block in sent]

    all_terms = [send_parts(weights[0], high[1:], [])]
    if ring:
        near[-1] = after(near[-1], *all_terms[0][1:3])
        pack = after(pack, near[-1])
        weights.append(Passed(out_w, near, [swap(block) for block in near], cut))
        all_terms.append(send_parts(weights[1], [], all_terms[0][1:]))

    front = shift(pack, "ctx", 1)
    mixed_low, gated_low, head = mix_low(causal, front, product, x, short_w, taps, group_size)
    sent = after(gated_low, all_terms[-1][0])
    low = [gated_low] + [to(sent, k) for k in partners[1:]]
    block_out = block_output(pos, weights, high, 1, 2, None)

    outs, sums = [], []
    for p, piece in enumerate(weights):
        terms = all_terms[p]
        if p:
            terms = [after(terms[0], outs[-1], block_out)] + terms[1:]
        mix_grad, query_grad, pack = mix_grads(
            terms, (mixed_low, mixed_high), x, front, short_w, piece.start
        )
        back = shift(pack, "ctx", -1)
        back = after(back, *([] if p else [block_out]))
        folded = filter_sums(mix_grad, product, head, front, taps, piece.start, group_size)
        grad, part = input_grads(
            anticausal,
            mix_grad,
            query_grad,
            back,
            x,
            front,
            short_w,
            folded,
            piece.start,
            group_size,
        )
        outs.append(grad)
        sums.append(part)
    block_out = block_output(pos, weights, low, 0, 2, block_out)
    total = total_over(jnp.concatenate(sums, axis=0), ("dp", "ctx"))

    grad_projected = jnp.transpose(jnp.concatenate(outs, axis=3), (1, 2, 0, 3))
    filter_total = total[:, :groups].reshape(-1, taps)[:, ::-1]
    short_total = jnp.swapaxes(total[:, groups : groups + 9], 0, 1).reshape(3, 3, width)
    seq_total = seqs * cores
    length_total = rows * length
    filter_grad = filter_total / math.sqrt(seq_total * length_total * group_size)
    short_grad = short_total / math.sqrt(seq_total * length_total)
    return (block_out, grad_projected, filter_grad, short_grad)


def solution(mesh):
    in_specs = (
        P("dp", "ctx", None, "grp"),
        P(None, None, "grp"),
        P("grp", None),
        P("ctx", "grp"),
        P("dp", "ctx", "grp"),
    )
    out_specs = (
        P("dp", "ctx", "grp"),
        P("dp", "ctx", None, "grp"),
        P("grp", None),
        P(None, None, "grp"),
    )
    return jax.shard_map(shards, mesh=mesh, in_specs=in_specs, out_specs=out_specs, check_vma=False)
```

time: 243 us -> 191 us (0.79)
  starting transfers between devices: 62.2 us -> 38.5 us
  waiting for transfers between devices: 72.5 us -> 51.5 us
  local copies, waits for them, and re-layouts: 38.4 us -> 19.2 us
  between operations: 1.46 us -> 14.5 us
  Pallas kernels: 56.1 us -> 64.6 us
  other arithmetic: 9.85 us -> 1.8 us
    ppermute x17 -> x3, waiting for transfers between devices: 52.9 us -> 5.4 us  [shift(): return lax.ppermute(block, axis, route)]
    ppermute x17 -> x3, starting transfers between devices: 39.4 us -> 6.12 us  [shift(): return lax.ppermute(block, axis, route)]
    ppermute x6, waiting for transfers between devices: 0.02 us -> 22.5 us  [the longest x3 22.5 us: shards(): lax.ppermute(block, 'ctx', [(i, (i + 1) % length) for i in range(length)])]
    unnamed x120 -> x63, local copies, waits for them, and re-layouts: 33.3 us -> 13.9 us
    ppermute x6, starting transfers between devices: 1.44 us -> 11.4 us  [the longest x3 10.9 us: shards(): lax.ppermute(block, 'ctx', [(i, (i + 1) % length) for i in range(length)])]
    pallas_call x6 -> x7, Pallas kernels: 32.2 us -> 40.9 us  [the longest x2 15.1 us: grad_parts(): pl.pallas_call(functools.partial(grad_kernel, weights, steps), in_specs=[...]
    select_n x6 -> x0, other arithmetic: 5.04 us -> none  [chain(): jnp.where(here >= s, up[p][s], down[p][count - s])]
    ppermute x12, waiting for transfers between devices: 18.7 us -> 21.8 us  [shards(): lax.ppermute(block, 'grp', [(i, i ^ k) for i in partners])]
  transfers between devices with their start and end apart: 41 -> 25, of which waited for: 12 -> 13; matrix products, arithmetic and copies ran while one was open for 7% -> 4% of each run, Pallas kernels for 23% -> 32%
where the time goes in v2:
time: 191 us; the launch traced here: 190 us
  Pallas kernels  64.6 us (34%)
  waiting for transfers between devices  51.5 us (27%)
  starting transfers between devices  38.5 us (20%)
  local copies, waits for them, and re-layouts  19.2 us (10%)
  between operations  14.5 us (8%)
    ppermute x3, waiting for transfers between devices, shards(): lax.ppermute(block, 'ctx', [(i, (i + 1) % length) for i in range(length)])  22.5 us
    ppermute x12, waiting for transfers between devices, shards(): lax.ppermute(block, 'grp', [(i, i ^ k) for i in partners])  21.8 us
    ppermute x12, starting transfers between devices, shards(): lax.ppermute(block, 'grp', [(i, i ^ k) for i in partners])  16 us
    pallas_call x2, Pallas kernels, grad_parts(): pl.pallas_call(functools.partial(grad_kernel, weights, steps), in_specs=[...  15.1 us
    pallas_call x2, Pallas kernels, block_output(): pl.pallas_call(functools.partial(out_kernel, weights, steps), grid=(1,),...  15.1 us
    unnamed x63, local copies, waits for them, and re-layouts  13.9 us
    pallas_call x2, Pallas kernels, input_grads(): pl.pallas_call(functools.partial(input_grad_kernel, group_size), grid=(wi...  11.3 us
    ppermute x3, starting transfers between devices, shards(): lax.ppermute(block, 'ctx', [(i, (i + 1) % length) for i in range(length)])  10.9 us
  transfers between devices with their start and end apart: 25, of which 13 were waited for; matrix products, arithmetic and copies ran while one was open for 4% of the time, Pallas kernels for 32%

profile of v2, /device:TPU:0, one launch (start us, length us, event | category | flops | bytes accessed | tf_op | source)
XLA Modules:
  0.0 190.1 jit_solution(10132987953818964045)
XLA Ops:
  7.2 1.8 constant_dynamic-slice_fusion.1
  9.0 2.0 %constant_dynamic-slice_fusion = bf16[320,1024]{1,0:T(8,128)(2,1)} fusion(bf16[1024,1024]{1,0:T(8,128)(2,1)} %refs_1_.3, s32[]{:T(128)S(6)} %select_n.7), kind=kLoop, calls=%fused_computation.10 | loop fusion | bytes 1310724 | tf_op jit(solution)/shard_map/dynamic_slice | solution.py:628
  11.0 3.0 %collective-permute-start = (bf16[320,1024]{1,0:T(8,128)(2,1)}, bf16[320,1024]{1,0:T(8,128)(2,1)}, u32[]{:S(2)}, u32[]{:S(2)}) collective-permute-start(bf16[320,1024]{1,0:T(8,128)(2,1)} %constant_dynamic-slice_fusion), channel_id=1, source_target_pairs={{0,4},{4,8},{8,12},{12,0},{1,5},{5,9},{9,13},{13,1},{2,6},{6,10},{... | collective-permute-start | bytes 1966088 | tf_op jit(solution)/shard_map/ppermute | solution.py:617
  14.9 2.2 %copy.16 = bf16[2,256,3,1024]{3,1,0,2:T(8,128)(2,1)S(1)} copy(bf16[2,256,3,1024]{3,1,2,0:T(8,128)(2,1)} %param.5) | data formatting | bytes 6291456 | tf_op args[0]
  17.1 2.7 %products.1 = (bf16[2,256,1024]{2,1,0:T(8,128)(2,1)S(1)}, bf16[2,160,1024]{2,1,0:T(8,128)(2,1)S(1)}) custom-call(bf16[3,2,256,1024]{3,2,1,0:T(8,128)(2,1)S(1)} %bitcast.22, f32[3,3,1024]{2,1,0:T(4,128)S(1)} %copy-done.4), custom_call_target="tpu_custom_call" | custom-call | tf_op jit(solution)/shard_map/products/pallas_call | solution.py:81
  19.9 0.9 copy-done.20
  20.9 3.8 %mix_high.1 = (f32[2,128,1024]{2,1,0:T(8,128)S(1)}, bf16[2,128,1024]{2,1,0:T(8,128)(2,1)S(1)}) custom-call(f32[64,256]{1,0:T(8,128)S(1)} %maximum_maximum_fusion.line_ref, bf16[2,256,1024]{2,1,0:T(8,128)(2,1)S(1)} %get-tuple-element.41.low_ref.high_ref.product_ref, bf16[2,256,1024]{2,1,0:T(8,128)(2,1)S(1)} %get-tuple-element.41.low_ref.high_ref.product_ref, ...), custom_call_target="tpu_custom_call" | custom-call | tf_op jit(solution)/shard_map/mix_high/pallas_call | solution.py:126
  24.7 1.0 copy-done
  25.7 1.0 copy-done.2
  26.7 11.7 %collective-permute-done.refs_1_.refs_2_ = bf16[320,1024]{1,0:T(8,128)(2,1)} collective-permute-done((bf16[320,1024]{1,0:T(8,128)(2,1)}, bf16[320,1024]{1,0:T(8,128)(2,1)}, u32[]{:S(2)}, u32[]{:S(2)}) %collective-permute-start) | collective-permute-done | bytes 655392 | tf_op jit(solution)/shard_map/ppermute | solution.py:617
  38.4 7.9 %collective-permute-start.1 = (bf16[320,1024]{1,0:T(8,128)(2,1)}, bf16[320,1024]{1,0:T(8,128)(2,1)}, u32[]{:S(2)}, u32[]{:S(2)}) collective-permute-start(bf16[320,1024]{1,0:T(8,128)(2,1)} %collective-permute-done.refs_1_.refs_2_), channel_id=1, source_target_pairs={{0,4},{4,8},{8,12},{12,0},{1,5},{5,9},{9,13},{13,1},{2,6},{6,10},{... | collective-permute-start | bytes 1966088 | tf_op jit(solution)/shard_map/ppermute | solution.py:617
  46.2 2.5 %collective-permute-start.4 = (bf16[2,128,1024]{2,1,0:T(8,128)(2,1)S(1)}, bf16[2,128,1024]{2,1,0:T(8,128)(2,1)S(1)}, u32[]{:S(2)}, u32[]{:S(2)}) collective-permute-start(bf16[2,128,1024]{2,1,0:T(8,128)(2,1)S(1)} %get-tuple-element.44.refs_8_), channel_id=1, source_target_pairs={{0,3},{1,2},{2,1},{3,0},{4,7},{5,6},{6,5},{7,4},{8,11},{9,10},{10,... | collective-permute-start | bytes 1572872 | tf_op jit(solution)/shard_map/ppermute | solution.py:616
  49.7 10.4 %collective-permute-done.4.refs_11_ = bf16[2,128,1024]{2,1,0:T(8,128)(2,1)S(1)} collective-permute-done((bf16[2,128,1024]{2,1,0:T(8,128)(2,1)S(1)}, bf16[2,128,1024]{2,1,0:T(8,128)(2,1)S(1)}, u32[]{:S(2)}, u32[]{:S(2)}) %collective-permute-start.4) | collective-permute-done | bytes 524320 | tf_op jit(solution)/shard_map/ppermute | solution.py:616
  60.1 5.5 %collective-permute-done.3.refs_10_ = bf16[2,128,1024]{2,1,0:T(8,128)(2,1)S(1)} collective-permute-done((bf16[2,128,1024]{2,1,0:T(8,128)(2,1)S(1)}, bf16[2,128,1024]{2,1,0:T(8,128)(2,1)S(1)}, u32[]{:S(2)}, u32[]{:S(2)}) %collective-permute-start.3) | collective-permute-done | bytes 524320 | tf_op jit(solution)/shard_map/ppermute | solution.py:616
  65.7 5.0 %collective-permute-done.1.refs_2_.refs_3_ = bf16[320,1024]{1,0:T(8,128)(2,1)} collective-permute-done((bf16[320,1024]{1,0:T(8,128)(2,1)}, bf16[320,1024]{1,0:T(8,128)(2,1)}, u32[]{:S(2)}, u32[]{:S(2)}) %collective-permute-start.1) | collective-permute-done | bytes 655392 | tf_op jit(solution)/shard_map/ppermute | solution.py:617
  71.3 6.4 %grad_parts.2 = (f32[512,384]{1,0:T(8,128)}, bf16[512,384]{1,0:T(8,128)(2,1)}, bf16[512,384]{1,0:T(8,128)(2,1)}, bf16[512,384]{1,0:T(8,128)(2,1)}) custom-call(s32[3]{0:T(128)} %pad_add_fusion.pos_ref, bf16[512,1024]{1,0:T(8,128)(2,1)} %bitcast.34, bf16[1536,1024]{1,0:T(8,128)(2,1)} %all-gather.2.cloned.1.call-done.refs_0_), custom_call_target="tpu_custom_call" | custom-call | tf_op jit(solution)/shard_map/grad_parts/pallas_call | solution.py:284
  77.7 1.6 collective-permute-start.7
  79.3 1.5 collective-permute-start.6
  81.3 5.8 %collective-permute-done.5.refs_3_.refs_4_ = bf16[320,1024]{1,0:T(8,128)(2,1)} collective-permute-done((bf16[320,1024]{1,0:T(8,128)(2,1)}, bf16[320,1024]{1,0:T(8,128)(2,1)}, u32[]{:S(2)}, u32[]{:S(2)}) %collective-permute-start.5) | collective-permute-done | bytes 655392 | tf_op jit(solution)/shard_map/ppermute | solution.py:617
  88.7 2.4 %collective-permute-start.12 = (bf16[512,384]{1,0:T(8,128)(2,1)}, bf16[512,384]{1,0:T(8,128)(2,1)S(1)}, u32[]{:S(2)}, u32[]{:S(2)}) collective-permute-start(bf16[512,384]{1,0:T(8,128)(2,1)} %get-tuple-element.54), channel_id=1, source_target_pairs={{0,3},{1,2},{2,1},{3,0},{4,7},{5,6},{6,5},{7,4},{8,11},{9,10},{10,... | collective-permute-start | bytes 1179656 | tf_op jit(solution)/shard_map/ppermute | solution.py:616
  91.1 3.4 %collective-permute-start.11 = (bf16[2,160,1024]{2,1,0:T(8,128)(2,1)S(1)}, bf16[2,160,1024]{2,1,0:T(8,128)(2,1)S(1)}, u32[]{:S(2)}, u32[]{:S(2)}) collective-permute-start(bf16[2,160,1024]{2,1,0:T(8,128)(2,1)S(1)} %copy-done.21), channel_id=1, source_target_pairs={{0,4},{4,8},{8,12},{1,5},{5,9},{9,13},{2,6},{6,10},{10,14},{3,7},{... | collective-permute-start | bytes 1966088 | tf_op jit(solution)/shard_map/ppermute | solution.py:26
  94.5 0.9 copy-done.22
  95.7 8.7 %grad_parts.3 = (f32[512,640]{1,0:T(8,128)}, bf16[512,640]{1,0:T(8,128)(2,1)}, bf16[512,640]{1,0:T(8,128)(2,1)}, bf16[512,640]{1,0:T(8,128)(2,1)}) custom-call(s32[3]{0:T(128)} %pad_add_fusion.pos_ref, bf16[512,1024]{1,0:T(8,128)(2,1)} %bitcast.35, bf16[1024,1024]{1,0:T(8,128)(2,1)} %refs_1_.3, bf16[320,1024]{1,0:T(8,128)(2,1)} %collective-permute-done.refs_1_.refs_2_, ...), custom_call_target="tpu_custom_call" | custom-call | tf_op jit(solution)/shard_map/grad_parts/pallas_call | solution.py:284
  105.2 1.0 collective-permute-start.19
  106.2 1.0 collective-permute-start.18
  107.2 1.5 collective-permute-start.17
  108.8 4.1 %mix_low.1 = (f32[2,128,1024]{2,1,0:T(8,128)S(1)}, bf16[2,128,1024]{2,1,0:T(8,128)(2,1)S(1)}, bf16[2,16,1024]{2,1,0:T(8,128)(2,1)S(1)}) custom-call(f32[64,256]{1,0:T(8,128)S(1)} %maximum_maximum_fusion.line_ref, bf16[2,160,1024]{2,1,0:T(8,128)(2,1)S(1)} %collective-permute-done.11.front_ref.refs_7_, bf16[2,256,1024]{2,1,0:T(8,128)(2,1)S(1)} %copy-done.1, ...), custom_call_target="tpu_custom_call" | custom-call | tf_op jit(solution)/shard_map/mix_low/pallas_call | solution.py:189
  113.8 2.3 %mix_grads.2 = (bf16[2,256,384]{2,1,0:T(8,128)(2,1)S(1)}, bf16[2,256,384]{2,1,0:T(8,128)(2,1)S(1)}, bf16[2,176,384]{2,1,0:T(8,128)(2,1)}) custom-call(f32[2,256,384]{2,1,0:T(8,128)S(1)} %bitcast.30, bf16[2,256,384]{2,1,0:T(8,128)(2,1)S(1)} %bitcast.32, bf16[2,256,384]{2,1,0:T(8,128)(2,1)S(1)} %bitcast.31, bf16[2,256,384]{2,1,0:T(8,128)(2,1)S(1)} %bitcast.33, ...), custom_call_target="tpu_custom_call" | custom-call | tf_op jit(solution)/shard_map/mix_grads/pallas_call | solution.py:370
  116.9 1.5 collective-permute-start.16
  118.4 7.5 %block_output.2.refs_12_ = bf16[2,256,1024]{2,1,0:T(8,128)(2,1)} custom-call(s32[3]{0:T(128)} %pad_add_fusion.pos_ref, bf16[1536,1024]{1,0:T(8,128)(2,1)} %all-gather.2.cloned.1.call-done.refs_0_, bf16[1024,1024]{1,0:T(8,128)(2,1)} %refs_1_.3, bf16[320,1024]{1,0:T(8,128)(2,1)} %collective-permute-done.refs_1_.refs_2_, ...), custom_call_target="tpu_custom_call" | custom-call | tf_op jit(solution)/shard_map/block_output/pallas_call | solution.py:327
  126.0 2.3 %filter_sums.2.filter_ref = f32[24,128]{1,0:T(8,128)S(1)} custom-call(bf16[2,256,384]{2,1,0:T(8,128)(2,1)S(1)} %get-tuple-element.59.mix_ref, bf16[2,256,1024]{2,1,0:T(8,128)(2,1)S(1)} %copy-done.1, bf16[2,16,1024]{2,1,0:T(8,128)(2,1)S(1)} %get-tuple-element.63.head_ref, bf16[2,160,1024]{2,1,0:T(8,128)(2,1)S(1)} %collective-permute-done.11.front_ref.refs_7_), custom_call_target="tpu_custom_call" | custom-call | tf_op jit(solution)/shard_map/filter_sums/pallas_call | solution.py:441
  128.3 1.0 copy-done.13
  129.3 4.2 %input_grads.2 = (bf16[3,2,256,384]{3,2,1,0:T(8,128)(2,1)S(1)}, f32[3,24,128]{2,1,0:T(8,128)S(1)}) custom-call(f32[64,256]{1,0:T(8,128)S(1)} %concatenate.13.line_ref, bf16[2,256,384]{2,1,0:T(8,128)(2,1)S(1)} %get-tuple-element.59.mix_ref, bf16[2,256,384]{2,1,0:T(8,128)(2,1)S(1)} %copy-done.13, bf16[2,176,384]{2,1,0:T(8,128)(2,1)S(1)} %collective-permute-done.16.back_ref, ...), custom_call_target="tpu_custom_call" | custom-call | tf_op jit(solution)/shard_map/input_grads/pallas_call | solution.py:560
  133.5 3.4 %collective-permute-done.18 = bf16[512,640]{1,0:T(8,128)(2,1)} collective-permute-done((bf16[512,640]{1,0:T(8,128)(2,1)}, bf16[512,640]{1,0:T(8,128)(2,1)}, u32[]{:S(2)}, u32[]{:S(2)}) %collective-permute-start.18) | collective-permute-done | bytes 655392 | tf_op jit(solution)/shard_map/ppermute | solution.py:616
  136.9 4.0 %mix_grads.3 = (bf16[2,256,640]{2,1,0:T(8,128)(2,1)S(1)}, bf16[2,256,640]{2,1,0:T(8,128)(2,1)S(1)}, bf16[2,176,640]{2,1,0:T(8,128)(2,1)S(1)}) custom-call(f32[2,256,640]{2,1,0:T(8,128)S(1)} %bitcast.29, bf16[2,256,640]{2,1,0:T(8,128)(2,1)} %bitcast.10.refs_1_, bf16[2,256,640]{2,1,0:T(8,128)(2,1)} %bitcast.11.refs_2_, bf16[2,256,640]{2,1,0:T(8,128)(2,1)} %bitcast.12.refs_3_, ...), custom_call_target="tpu_custom_call" | custom-call | tf_op jit(solution)/shard_map/mix_grads/pallas_call | solution.py:370
  140.9 1.3 collective-permute-start.20
  142.2 1.2 collective-permute-start.15
  143.5 1.0 collective-permute-start.14
  144.5 1.3 collective-permute-start.13
  145.8 3.8 %filter_sums.3.filter_ref = f32[40,128]{1,0:T(8,128)S(1)} custom-call(bf16[2,256,640]{2,1,0:T(8,128)(2,1)S(1)} %get-tuple-element.72.mix_ref, bf16[2,256,1024]{2,1,0:T(8,128)(2,1)S(1)} %copy-done.1, bf16[2,16,1024]{2,1,0:T(8,128)(2,1)S(1)} %get-tuple-element.63.head_ref, bf16[2,160,1024]{2,1,0:T(8,128)(2,1)S(1)} %collective-permute-done.11.front_ref.refs_7_), custom_call_target="tpu_custom_call" | custom-call | tf_op jit(solution)/shard_map/filter_sums/pallas_call | solution.py:441
  149.6 5.3 %collective-permute-done.20.back_ref = bf16[2,176,640]{2,1,0:T(8,128)(2,1)S(1)} collective-permute-done((bf16[2,176,640]{2,1,0:T(8,128)(2,1)S(1)}, bf16[2,176,640]{2,1,0:T(8,128)(2,1)S(1)}, u32[]{:S(2)}, u32[]{:S(2)}) %collective-permute-start.20) | collective-permute-done | bytes 450592 | tf_op jit(solution)/shard_map/ppermute | solution.py:26
  154.9 7.1 %input_grads.3 = (bf16[3,2,256,640]{3,2,1,0:T(8,128)(2,1)S(1)}, f32[5,24,128]{2,1,0:T(8,128)S(1)}) custom-call(f32[64,256]{1,0:T(8,128)S(1)} %concatenate.13.line_ref, bf16[2,256,640]{2,1,0:T(8,128)(2,1)S(1)} %get-tuple-element.72.mix_ref, bf16[2,256,640]{2,1,0:T(8,128)(2,1)S(1)} %get-tuple-element.73.query_ref, ...), custom_call_target="tpu_custom_call" | custom-call | tf_op jit(solution)/shard_map/input_grads/pallas_call | solution.py:560
  162.0 1.3 collective-permute-done.21
  163.4 2.4 %collective-permute-start.22 = (f32[8,24,128]{2,1,0:T(8,128)S(1)}, f32[8,24,128]{2,1,0:T(8,128)S(1)}, u32[]{:S(2)}, u32[]{:S(2)}) collective-permute-start(f32[8,24,128]{2,1,0:T(8,128)S(1)} %add.21), channel_id=1, source_target_pairs={{0,8},{4,12},{8,0},{12,4},{16,24},{20,28},{24,16},{28,20},{1,9},{5... | collective-permute-start | bytes 294920 | tf_op jit(solution)/shard_map/ppermute | solution.py:603
  165.7 2.4 %collective-permute-done.14.refs_10_ = bf16[2,128,1024]{2,1,0:T(8,128)(2,1)S(1)} collective-permute-done((bf16[2,128,1024]{2,1,0:T(8,128)(2,1)S(1)}, bf16[2,128,1024]{2,1,0:T(8,128)(2,1)S(1)}, u32[]{:S(2)}, u32[]{:S(2)}) %collective-permute-start.14) | collective-permute-done | bytes 524320 | tf_op jit(solution)/shard_map/ppermute | solution.py:616
  168.9 7.5 %block_output.3 = bf16[2,256,1024]{2,1,0:T(8,128)(2,1)} custom-call(s32[3]{0:T(128)} %pad_add_fusion.pos_ref, bf16[1536,1024]{1,0:T(8,128)(2,1)} %all-gather.2.cloned.1.call-done.refs_0_, bf16[1024,1024]{1,0:T(8,128)(2,1)} %refs_1_.3, bf16[320,1024]{1,0:T(8,128)(2,1)} %collective-permute-done.refs_1_.refs_2_, ...), custom_call_target="tpu_custom_call", output_to_operand_aliasing={{}: (13, {})} | custom-call | tf_op jit(solution)/shard_map/block_output/pallas_call | solution.py:327
  176.4 2.4 %collective-permute-start.23 = (f32[8,24,128]{2,1,0:T(8,128)S(1)}, f32[8,24,128]{2,1,0:T(8,128)S(1)}, u32[]{:S(2)}, u32[]{:S(2)}) collective-permute-start(f32[8,24,128]{2,1,0:T(8,128)S(1)} %add.22), channel_id=1, source_target_pairs={{0,4},{4,0},{8,12},{12,8},{16,20},{20,16},{24,28},{28,24},{1,5},{5... | collective-permute-start | bytes 294920 | tf_op jit(solution)/shard_map/ppermute | solution.py:603
  179.3 2.0 %copy.14 = bf16[2,256,3,1024]{3,1,2,0:T(8,128)(2,1)} copy(bf16[2,256,3,1024]{3,1,0,2:T(8,128)(2,1)S(1)} %maximum_bitcast_fusion) | data formatting | bytes 6291456
  (99 shorter events, 10.8 us)
Async XLA Ops:
  7.2 64.1 %all-gather.2.cloned.1.call-start = ((), (), s32[]{:S(2)}) async-start(), calls=%async_computation | async-start | bytes 3538944 | tf_op jit(solution)/shard_map/all_gather | solution.py:630
  11.0 27.3 %collective-permute-start = (bf16[320,1024]{1,0:T(8,128)(2,1)}, bf16[320,1024]{1,0:T(8,128)(2,1)}, u32[]{:S(2)}, u32[]{:S(2)}) collective-permute-start(bf16[320,1024]{1,0:T(8,128)(2,1)} %constant_dynamic-slice_fusion), channel_id=1, source_target_pairs={{0,4},{4,8},{8,12},{12,0},{1,5},{5,9},{9,13},{13,1},{2,6},{6,10},{... | collective-permute-start | bytes 1966088 | tf_op jit(solution)/shard_map/ppermute | solution.py:617
  14.9 2.2 %copy-start.4 = (f32[3,3,1024]{2,1,0:T(4,128)S(1)}, f32[3,3,1024]{2,1,0:T(4,128)}, u32[]{:S(2)}) copy-start(f32[3,3,1024]{2,1,0:T(4,128)} %w_ref.9) | copy-start | bytes 110596
  19.9 0.9 copy-start.20
  24.7 1.0 copy-start
  25.7 1.0 copy-start.2
  26.7 22.6 %copy-start.9 = (bf16[2,128,1024]{2,1,0:T(8,128)(2,1)}, bf16[2,128,1024]{2,1,0:T(8,128)(2,1)S(1)}, u32[]{:S(2)}) copy-start(bf16[2,128,1024]{2,1,0:T(8,128)(2,1)S(1)} %get-tuple-element.44.refs_8_) | copy-start | bytes 1572868
  38.4 32.3 %collective-permute-start.1 = (bf16[320,1024]{1,0:T(8,128)(2,1)}, bf16[320,1024]{1,0:T(8,128)(2,1)}, u32[]{:S(2)}, u32[]{:S(2)}) collective-permute-start(bf16[320,1024]{1,0:T(8,128)(2,1)} %collective-permute-done.refs_1_.refs_2_), channel_id=1, source_target_pairs={{0,4},{4,8},{8,12},{12,0},{1,5},{5,9},{9,13},{13,1},{2,6},{6,10},{... | collective-permute-start | bytes 1966088 | tf_op jit(solution)/shard_map/ppermute | solution.py:617
  46.2 13.9 %collective-permute-start.4 = (bf16[2,128,1024]{2,1,0:T(8,128)(2,1)S(1)}, bf16[2,128,1024]{2,1,0:T(8,128)(2,1)S(1)}, u32[]{:S(2)}, u32[]{:S(2)}) collective-permute-start(bf16[2,128,1024]{2,1,0:T(8,128)(2,1)S(1)} %get-tuple-element.44.refs_8_), channel_id=1, source_target_pairs={{0,3},{1,2},{2,1},{3,0},{4,7},{5,6},{6,5},{7,4},{8,11},{9,10},{10,... | collective-permute-start | bytes 1572872 | tf_op jit(solution)/shard_map/ppermute | solution.py:616
  48.7 16.9 %collective-permute-start.3 = (bf16[2,128,1024]{2,1,0:T(8,128)(2,1)S(1)}, bf16[2,128,1024]{2,1,0:T(8,128)(2,1)S(1)}, u32[]{:S(2)}, u32[]{:S(2)}) collective-permute-start(bf16[2,128,1024]{2,1,0:T(8,128)(2,1)S(1)} %get-tuple-element.44.refs_8_), channel_id=1, source_target_pairs={{0,2},{1,3},{2,0},{3,1},{4,6},{5,7},{6,4},{7,5},{8,10},{9,11},{10,... | collective-permute-start | bytes 1572872 | tf_op jit(solution)/shard_map/ppermute | solution.py:616
  49.2 16.4 %collective-permute-start.2 = (bf16[2,128,1024]{2,1,0:T(8,128)(2,1)S(1)}, bf16[2,128,1024]{2,1,0:T(8,128)(2,1)S(1)}, u32[]{:S(2)}, u32[]{:S(2)}) collective-permute-start(bf16[2,128,1024]{2,1,0:T(8,128)(2,1)S(1)} %get-tuple-element.44.refs_8_), channel_id=1, source_target_pairs={{0,1},{1,0},{2,3},{3,2},{4,5},{5,4},{6,7},{7,6},{8,9},{9,8},{10,11... | collective-permute-start | bytes 1572872 | tf_op jit(solution)/shard_map/ppermute | solution.py:616
  60.1 5.6 %copy-start.24 = (bf16[2,128,1024]{2,1,0:T(8,128)(2,1)}, bf16[2,128,1024]{2,1,0:T(8,128)(2,1)S(1)}, u32[]{:S(2)}) copy-start(bf16[2,128,1024]{2,1,0:T(8,128)(2,1)S(1)} %collective-permute-done.4.refs_11_) | copy-start | bytes 1572868
  65.6 5.1 %copy-start.25 = (bf16[2,128,1024]{2,1,0:T(8,128)(2,1)}, bf16[2,128,1024]{2,1,0:T(8,128)(2,1)S(1)}, u32[]{:S(2)}) copy-start(bf16[2,128,1024]{2,1,0:T(8,128)(2,1)S(1)} %collective-permute-done.3.refs_10_) | copy-start | bytes 1572868
  65.7 5.0 %copy-start.26 = (bf16[2,128,1024]{2,1,0:T(8,128)(2,1)}, bf16[2,128,1024]{2,1,0:T(8,128)(2,1)S(1)}, u32[]{:S(2)}) copy-start(bf16[2,128,1024]{2,1,0:T(8,128)(2,1)S(1)} %collective-permute-done.2.refs_9_) | copy-start | bytes 1572868
  70.7 16.5 %collective-permute-start.5 = (bf16[320,1024]{1,0:T(8,128)(2,1)}, bf16[320,1024]{1,0:T(8,128)(2,1)}, u32[]{:S(2)}, u32[]{:S(2)}) collective-permute-start(bf16[320,1024]{1,0:T(8,128)(2,1)} %collective-permute-done.1.refs_2_.refs_3_), channel_id=1, source_target_pairs={{0,4},{4,8},{8,12},{12,0},{1,5},{5,9},{9,13},{13,1},{2,6},{6,10},{... | collective-permute-start | bytes 1966088 | tf_op jit(solution)/shard_map/ppermute | solution.py:617
  71.3 19.8 %copy-start.21 = (bf16[2,160,1024]{2,1,0:T(8,128)(2,1)S(1)}, bf16[2,160,1024]{2,1,0:T(8,128)(2,1)}, u32[]{:S(2)}) copy-start(bf16[2,160,1024]{2,1,0:T(8,128)(2,1)} %copy-done.20) | copy-start | bytes 1966084
  77.7 9.4 %collective-permute-start.7 = (bf16[512,384]{1,0:T(8,128)(2,1)}, bf16[512,384]{1,0:T(8,128)(2,1)S(1)}, u32[]{:S(2)}, u32[]{:S(2)}) collective-permute-start(bf16[512,384]{1,0:T(8,128)(2,1)} %get-tuple-element.48), channel_id=1, source_target_pairs={{0,2},{1,3},{2,0},{3,1},{4,6},{5,7},{6,4},{7,5},{8,10},{9,11},{10,... | collective-permute-start | bytes 1179656 | tf_op jit(solution)/shard_map/ppermute | solution.py:616
  79.3 8.7 %collective-permute-start.6 = (bf16[512,384]{1,0:T(8,128)(2,1)}, bf16[512,384]{1,0:T(8,128)(2,1)S(1)}, u32[]{:S(2)}, u32[]{:S(2)}) collective-permute-start(bf16[512,384]{1,0:T(8,128)(2,1)} %get-tuple-element.47), channel_id=1, source_target_pairs={{0,1},{1,0},{2,3},{3,2},{4,5},{5,4},{6,7},{7,6},{8,9},{9,8},{10,11... | collective-permute-start | bytes 1179656 | tf_op jit(solution)/shard_map/ppermute | solution.py:616
  80.8 13.7 %collective-permute-start.8 = (bf16[320,1024]{1,0:T(8,128)(2,1)}, bf16[320,1024]{1,0:T(8,128)(2,1)S(1)}, u32[]{:S(2)}, u32[]{:S(2)}) collective-permute-start(bf16[320,1024]{1,0:T(8,128)(2,1)} %collective-permute-done.refs_1_.refs_2_), channel_id=1, source_target_pairs={{0,16},{16,0},{1,17},{17,1},{2,18},{18,2},{3,19},{19,3},{4,20},{20... | collective-permute-start | bytes 1966088 | tf_op jit(solution)/shard_map/ppermute | solution.py:618
  80.8 13.7 %collective-permute-start.9 = (bf16[320,1024]{1,0:T(8,128)(2,1)}, bf16[320,1024]{1,0:T(8,128)(2,1)S(1)}, u32[]{:S(2)}, u32[]{:S(2)}) collective-permute-start(bf16[320,1024]{1,0:T(8,128)(2,1)} %collective-permute-done.1.refs_2_.refs_3_), channel_id=1, source_target_pairs={{0,16},{16,0},{1,17},{17,1},{2,18},{18,2},{3,19},{19,3},{4,20},{20... | collective-permute-start | bytes 1966088 | tf_op jit(solution)/shard_map/ppermute | solution.py:618
  88.7 5.8 %collective-permute-start.10 = (bf16[320,1024]{1,0:T(8,128)(2,1)}, bf16[320,1024]{1,0:T(8,128)(2,1)}, u32[]{:S(2)}, u32[]{:S(2)}) collective-permute-start(bf16[320,1024]{1,0:T(8,128)(2,1)} %collective-permute-done.5.refs_3_.refs_4_), channel_id=1, source_target_pairs={{0,16},{16,0},{1,17},{17,1},{2,18},{18,2},{3,19},{19,3},{4,20},{20... | collective-permute-start | bytes 1966088 | tf_op jit(solution)/shard_map/ppermute | solution.py:618
  88.7 15.7 %collective-permute-start.12 = (bf16[512,384]{1,0:T(8,128)(2,1)}, bf16[512,384]{1,0:T(8,128)(2,1)S(1)}, u32[]{:S(2)}, u32[]{:S(2)}) collective-permute-start(bf16[512,384]{1,0:T(8,128)(2,1)} %get-tuple-element.54), channel_id=1, source_target_pairs={{0,3},{1,2},{2,1},{3,0},{4,7},{5,6},{6,5},{7,4},{8,11},{9,10},{10,... | collective-permute-start | bytes 1179656 | tf_op jit(solution)/shard_map/ppermute | solution.py:616
  91.1 17.7 %copy-start.1 = (bf16[2,256,1024]{2,1,0:T(8,128)(2,1)S(1)}, bf16[2,256,1024]{2,1,0:T(8,128)(2,1)}, u32[]{:S(2)}) copy-start(bf16[2,256,1024]{2,1,0:T(8,128)(2,1)} %copy-done) | copy-start | bytes 3145732
  91.1 17.7 %collective-permute-start.11 = (bf16[2,160,1024]{2,1,0:T(8,128)(2,1)S(1)}, bf16[2,160,1024]{2,1,0:T(8,128)(2,1)S(1)}, u32[]{:S(2)}, u32[]{:S(2)}) collective-permute-start(bf16[2,160,1024]{2,1,0:T(8,128)(2,1)S(1)} %copy-done.21), channel_id=1, source_target_pairs={{0,4},{4,8},{8,12},{1,5},{5,9},{9,13},{2,6},{6,10},{10,14},{3,7},{... | collective-permute-start | bytes 1966088 | tf_op jit(solution)/shard_map/ppermute | solution.py:26
  94.5 1.1 copy-start.23
  104.4 9.4 %copy-start.3 = (f32[2,128,1024]{2,1,0:T(8,128)S(1)}, f32[2,128,1024]{2,1,0:T(8,128)}, u32[]{:S(2)}) copy-start(f32[2,128,1024]{2,1,0:T(8,128)} %copy-done.2) | copy-start | bytes 3145732
  104.4 9.4 %copy-start.8 = (f32[512,384]{1,0:T(8,128)S(1)}, f32[512,384]{1,0:T(8,128)}, u32[]{:S(2)}) copy-start(f32[512,384]{1,0:T(8,128)} %get-tuple-element.57) | copy-start | bytes 2359300
  104.4 9.4 %copy-start.15 = (bf16[512,384]{1,0:T(8,128)(2,1)S(1)}, bf16[512,384]{1,0:T(8,128)(2,1)}, u32[]{:S(2)}) copy-start(bf16[512,384]{1,0:T(8,128)(2,1)} %copy-done.14) | copy-start | bytes 1179652
  104.4 9.4 %copy-start.17 = (bf16[512,384]{1,0:T(8,128)(2,1)S(1)}, bf16[512,384]{1,0:T(8,128)(2,1)}, u32[]{:S(2)}) copy-start(bf16[512,384]{1,0:T(8,128)(2,1)} %copy-done.16) | copy-start | bytes 1179652
  105.2 8.6 %copy-start.19 = (bf16[512,384]{1,0:T(8,128)(2,1)S(1)}, bf16[512,384]{1,0:T(8,128)(2,1)}, u32[]{:S(2)}) copy-start(bf16[512,384]{1,0:T(8,128)(2,1)} %copy-done.18) | copy-start | bytes 1179652
  105.2 28.3 %collective-permute-start.19 = (bf16[512,640]{1,0:T(8,128)(2,1)}, bf16[512,640]{1,0:T(8,128)(2,1)}, u32[]{:S(2)}, u32[]{:S(2)}) collective-permute-start(bf16[512,640]{1,0:T(8,128)(2,1)} %get-tuple-element.71), channel_id=1, source_target_pairs={{0,3},{1,2},{2,1},{3,0},{4,7},{5,6},{6,5},{7,4},{8,11},{9,10},{10,... | collective-permute-start | bytes 1966088 | tf_op jit(solution)/shard_map/ppermute | solution.py:616
  106.2 30.7 %collective-permute-start.18 = (bf16[512,640]{1,0:T(8,128)(2,1)}, bf16[512,640]{1,0:T(8,128)(2,1)}, u32[]{:S(2)}, u32[]{:S(2)}) collective-permute-start(bf16[512,640]{1,0:T(8,128)(2,1)} %get-tuple-element.69), channel_id=1, source_target_pairs={{0,2},{1,3},{2,0},{3,1},{4,6},{5,7},{6,4},{7,5},{8,10},{9,11},{10,... | collective-permute-start | bytes 1966088 | tf_op jit(solution)/shard_map/ppermute | solution.py:616
  107.2 29.7 %collective-permute-start.17 = (bf16[512,640]{1,0:T(8,128)(2,1)}, bf16[512,640]{1,0:T(8,128)(2,1)}, u32[]{:S(2)}, u32[]{:S(2)}) collective-permute-start(bf16[512,640]{1,0:T(8,128)(2,1)} %get-tuple-element.67), channel_id=1, source_target_pairs={{0,1},{1,0},{2,3},{3,2},{4,5},{5,4},{6,7},{7,6},{8,9},{9,8},{10,11... | collective-permute-start | bytes 1966088 | tf_op jit(solution)/shard_map/ppermute | solution.py:616
  113.8 4.5 %copy-start.29 = (bf16[64,128]{1,0:T(8,128)(2,1)S(1)}, bf16[64,128]{1,0:T(8,128)(2,1)}, u32[]{:S(2)}) copy-start(bf16[64,128]{1,0:T(8,128)(2,1)} %param.7) | copy-start | bytes 49156
  116.9 11.4 %collective-permute-start.16 = (bf16[2,176,384]{2,1,0:T(8,128)(2,1)}, bf16[2,176,384]{2,1,0:T(8,128)(2,1)S(1)}, u32[]{:S(2)}, u32[]{:S(2)}) collective-permute-start(bf16[2,176,384]{2,1,0:T(8,128)(2,1)} %get-tuple-element.61), channel_id=1, source_target_pairs={{4,0},{8,4},{12,8},{5,1},{9,5},{13,9},{6,2},{10,6},{14,10},{7,3},{... | collective-permute-start | bytes 811016 | tf_op jit(solution)/shard_map/ppermute | solution.py:26
  125.9 10.9 %copy-start.5 = (f32[512,640]{1,0:T(8,128)S(1)}, f32[512,640]{1,0:T(8,128)}, u32[]{:S(2)}) copy-start(f32[512,640]{1,0:T(8,128)} %get-tuple-element.55) | copy-start | bytes 3932164
  128.3 1.0 copy-start.13
  133.5 7.4 %copy-start.6 = (bf16[3,2,256,384]{3,2,1,0:T(8,128)(2,1)}, bf16[3,2,256,384]{3,2,1,0:T(8,128)(2,1)S(1)}, u32[]{:S(2)}) copy-start(bf16[3,2,256,384]{3,2,1,0:T(8,128)(2,1)S(1)} %get-tuple-element.64) | copy-start | bytes 3538948
  136.9 5.3 %copy-start.11 = (bf16[2,128,1024]{2,1,0:T(8,128)(2,1)S(1)}, bf16[2,128,1024]{2,1,0:T(8,128)(2,1)}, u32[]{:S(2)}) copy-start(bf16[2,128,1024]{2,1,0:T(8,128)(2,1)} %copy-done.10) | copy-start | bytes 1572868
  140.9 14.0 %collective-permute-start.20 = (bf16[2,176,640]{2,1,0:T(8,128)(2,1)S(1)}, bf16[2,176,640]{2,1,0:T(8,128)(2,1)S(1)}, u32[]{:S(2)}, u32[]{:S(2)}) collective-permute-start(bf16[2,176,640]{2,1,0:T(8,128)(2,1)S(1)} %get-tuple-element.74), channel_id=1, source_target_pairs={{4,0},{8,4},{12,8},{5,1},{9,5},{13,9},{6,2},{10,6},{14,10},{7,3},{... | collective-permute-start | bytes 1351688 | tf_op jit(solution)/shard_map/ppermute | solution.py:26
  142.2 23.5 %collective-permute-start.15 = (bf16[2,128,1024]{2,1,0:T(8,128)(2,1)S(1)}, bf16[2,128,1024]{2,1,0:T(8,128)(2,1)S(1)}, u32[]{:S(2)}, u32[]{:S(2)}) collective-permute-start(bf16[2,128,1024]{2,1,0:T(8,128)(2,1)S(1)} %copy-done.11), channel_id=1, source_target_pairs={{0,3},{1,2},{2,1},{3,0},{4,7},{5,6},{6,5},{7,4},{8,11},{9,10},{10,... | collective-permute-start | bytes 1572872 | tf_op jit(solution)/shard_map/ppermute | solution.py:616
  143.5 24.6 %collective-permute-start.14 = (bf16[2,128,1024]{2,1,0:T(8,128)(2,1)S(1)}, bf16[2,128,1024]{2,1,0:T(8,128)(2,1)S(1)}, u32[]{:S(2)}, u32[]{:S(2)}) collective-permute-start(bf16[2,128,1024]{2,1,0:T(8,128)(2,1)S(1)} %copy-done.11), channel_id=1, source_target_pairs={{0,2},{1,3},{2,0},{3,1},{4,6},{5,7},{6,4},{7,5},{8,10},{9,11},{10,... | collective-permute-start | bytes 1572872 | tf_op jit(solution)/shard_map/ppermute | solution.py:616
  144.5 24.4 %collective-permute-start.13 = (bf16[2,128,1024]{2,1,0:T(8,128)(2,1)S(1)}, bf16[2,128,1024]{2,1,0:T(8,128)(2,1)}, u32[]{:S(2)}, u32[]{:S(2)}) collective-permute-start(bf16[2,128,1024]{2,1,0:T(8,128)(2,1)S(1)} %copy-done.11), channel_id=1, source_target_pairs={{0,1},{1,0},{2,3},{3,2},{4,5},{5,4},{6,7},{7,6},{8,9},{9,8},{10,11... | collective-permute-start | bytes 1572872 | tf_op jit(solution)/shard_map/ppermute | solution.py:616
  162.0 1.4 collective-permute-start.21
  163.3 15.5 %copy-start.7 = (bf16[3,2,256,384]{3,2,1,0:T(8,128)(2,1)S(1)}, bf16[3,2,256,384]{3,2,1,0:T(8,128)(2,1)}, u32[]{:S(2)}) copy-start(bf16[3,2,256,384]{3,2,1,0:T(8,128)(2,1)} %copy-done.6) | copy-start | bytes 3538948
  163.4 13.1 %collective-permute-start.22 = (f32[8,24,128]{2,1,0:T(8,128)S(1)}, f32[8,24,128]{2,1,0:T(8,128)S(1)}, u32[]{:S(2)}, u32[]{:S(2)}) collective-permute-start(f32[8,24,128]{2,1,0:T(8,128)S(1)} %add.21), channel_id=1, source_target_pairs={{0,8},{4,12},{8,0},{12,4},{16,24},{20,28},{24,16},{28,20},{1,9},{5... | collective-permute-start | bytes 294920 | tf_op jit(solution)/shard_map/ppermute | solution.py:603
  165.7 2.4 %copy-start.27 = (bf16[2,128,1024]{2,1,0:T(8,128)(2,1)}, bf16[2,128,1024]{2,1,0:T(8,128)(2,1)S(1)}, u32[]{:S(2)}) copy-start(bf16[2,128,1024]{2,1,0:T(8,128)(2,1)S(1)} %collective-permute-done.15.refs_11_) | copy-start | bytes 1572868
  176.4 5.4 %collective-permute-start.23 = (f32[8,24,128]{2,1,0:T(8,128)S(1)}, f32[8,24,128]{2,1,0:T(8,128)S(1)}, u32[]{:S(2)}, u32[]{:S(2)}) collective-permute-start(f32[8,24,128]{2,1,0:T(8,128)S(1)} %add.22), channel_id=1, source_target_pairs={{0,4},{4,0},{8,12},{12,8},{16,20},{20,16},{24,28},{28,24},{1,5},{5... | collective-permute-start | bytes 294920 | tf_op jit(solution)/shard_map/ppermute | solution.py:603
  (7 other events, 5.5 us)
Sparse Core Ops, SparseCore 0:
  9.6 56.4 all-gather.1

commit v3 on v2

--- a/solution.py
+++ b/solution.py
@@ -258,9 +258,9 @@
         return copies(refs[1], refs[steps])
 
 
-def grad_kernel(weights, steps, pos_ref, cot_ref, *refs):
+def grad_kernel(weights, steps, ranges, pos_ref, cot_ref, *refs):
     held = len(weights.arrays)
-    outs, (buffer, sems) = refs[held : held + steps], refs[held + steps :]
+    outs, (buffer, sems) = refs[held:-2], refs[-2:]
     order = list(range(1, steps)) + [0]
     copies = {
         partner: weights.fetch(pos_ref, refs[:held], buffer, 0, sems, partner)
@@ -269,32 +269,45 @@
     for partner in order:
         for copy in copies[partner]:
             copy.wait()
-        outs[partner][...] = lax.dot_general(
+        part = lax.dot_general(
             cot_ref[...],
             buffer[partner],
             (((1,), (1,)), ((), ())),
             preferred_element_type=F32,
-        ).astype(outs[partner].dtype)
-
-
-def grad_parts(pos, cotangent, weights, steps):
-    rows, width = cotangent.shape
+        )
+        if partner == 0:
+            outs[0][...] = part.reshape(outs[0].shape)
+            continue
+        for r, (start, stop) in enumerate(ranges):
+            out_ref = outs[1 + r * (steps - 1) + partner - 1]
+            rows = outs[0].shape[1]
+            for s in range(out_ref.shape[0]):
+                out_ref[s] = part[s * rows + start : s * rows + stop].astype(BF16)
+
+
+def grad_parts(pos, cotangent, weights, steps, ranges):
+    seqs, rows, width = cotangent.shape
     span = weights.span
     inside = pl.BlockSpec(memory_space=pltpu.VMEM)
-    return pl.pallas_call(
-        functools.partial(grad_kernel, weights, steps),
+    shapes = [jax.ShapeDtypeStruct((seqs, rows, span), F32)]
+    for start, stop in ranges:
+        shapes += [jax.ShapeDtypeStruct((seqs, stop - start, span), BF16)] * (steps - 1)
+    found = pl.pallas_call(
+        functools.partial(grad_kernel, weights, steps, ranges),
         in_specs=[pl.BlockSpec(memory_space=pltpu.SMEM), inside]
-        + [pl.BlockSpec(memory_space=pl.ANY)] * len(weights.arrays),
-        out_specs=[inside] * steps,
-        out_shape=[jax.ShapeDtypeStruct((rows, span), F32)]
-        + [jax.ShapeDtypeStruct((rows, span), BF16)] * (steps - 1),
+        + [pl.BlockSpec(memory_space=pltpu.HBM)] * len(weights.arrays),
+        out_specs=[inside] * len(shapes),
+        out_shape=shapes,
         scratch_shapes=[
             pltpu.VMEM((steps, span, width), BF16),
             pltpu.SemaphoreType.DMA((steps, 2)),
         ],
-        compiler_params=params(56),
+        compiler_params=params(24),
         name="grad_parts",
-    )(pos, cotangent, *weights.arrays)
+    )(pos, cotangent.reshape(seqs * rows, width), *weights.arrays)
+    return found[0], [
+        found[1 + r * (steps - 1) : 1 + (r + 1) * (steps - 1)] for r in range(len(ranges))
+    ]
 
 
 def out_kernel(weights, steps, pos_ref, *refs):
@@ -321,7 +334,7 @@
     seqs, rows, depth = gated[0].shape
     width = weights[0].arrays[0].shape[1]
     inside = pl.BlockSpec(memory_space=pltpu.VMEM)
-    anywhere = pl.BlockSpec(memory_space=pl.ANY)
+    anywhere = pl.BlockSpec(memory_space=pltpu.HBM)
     arrays = [array for piece in weights for array in piece.arrays]
     before = [] if before is None else [before]
     return pl.pallas_call(
@@ -336,62 +349,74 @@
         scratch_shapes=[pltpu.VMEM((steps, depth, width), BF16)]
         + [pltpu.SemaphoreType.DMA((steps, 2))] * len(weights),
         input_output_aliases={1 + len(arrays) + steps: 0} if before else {},
-        compiler_params=params(56),
+        compiler_params=params(24),
         name="block_output",
     )(pos, *arrays, *gated, *before)
 
 
-def mix_grad_kernel(steps, *refs):
-    terms = refs[:steps]
-    low_ref, high_ref, x_ref, front_ref, w_ref, mix_ref, query_ref, pack_ref, pad = refs[steps:]
-    seqs, rows = x_ref.shape[1], low_ref.shape[1]
+def mix_grad_kernel(count, start, stop, *refs):
+    terms = refs[:count]
+    low_ref, high_ref, x_ref, front_ref, w_ref, mix_ref, query_ref = refs[count : count + 7]
+    pad = refs[-1]
+    seqs, half = x_ref.shape[1], low_ref.shape[1]
     for s in range(seqs):
-        query = convolve(x_ref, w_ref, pad, 0, s, front_rows(front_ref, 0, s, rows))
-        for b, mixed_ref in enumerate((low_ref, high_ref)):
-            at = slice(b * rows, (b + 1) * rows)
-            total = terms[0][s, at].astype(F32)
+        query = convolve(x_ref, w_ref, pad, 0, s, front_rows(front_ref, 0, s, half))
+        for first, mixed_ref in ((0, low_ref), (half, high_ref)):
+            begin, end = max(first, start), min(first + half, stop)
+            if begin >= end:
+                continue
+            at = slice(begin - start, end - start)
+            total = terms[0][s, begin:end]
             for term in terms[1:]:
                 total = total + term[s, at].astype(F32)
             gated_grad = total.astype(BF16).astype(F32)
-            mix_ref[s, at] = (gated_grad * query[at]).astype(BF16)
-            query_ref[s, at] = (gated_grad * mixed_ref[s]).astype(BF16)
-        pack_ref[s, :HALO] = mix_ref[s, :HALO]
-        pack_ref[s, HALO : HALO + EXTRA] = query_ref[s, :EXTRA]
-        heads = [x_ref[j, s, :EXTRA].astype(F32)[:8] for j in (1, 2)]
-        pack_ref[s, HALO + EXTRA :] = jnp.concatenate(heads, axis=0).astype(BF16)
-
-
-def mix_grads(terms, mixed, x, front, short_w, offset):
-    seqs, rows, width = terms[0].shape
+            mixed = mixed_ref[s, begin - first : end - first]
+            mix_ref[s, at] = (gated_grad * query[begin:end]).astype(BF16)
+            query_ref[s, at] = (gated_grad * mixed).astype(BF16)
+        if start == 0:
+            pack_ref = refs[count + 7]
+            pack_ref[s, :HALO] = mix_ref[s, :HALO]
+            pack_ref[s, HALO : HALO + EXTRA] = query_ref[s, :EXTRA]
+            heads = [x_ref[j, s, :EXTRA].astype(F32)[:8] for j in (1, 2)]
+            pack_ref[s, HALO + EXTRA :] = jnp.concatenate(heads, axis=0).astype(BF16)
+
+
+def mix_grads(own, terms, start, stop, mixed, x, front, short_w, offset):
+    seqs, rows, width = own.shape
     half = rows // 2
     first = offset // LANES
     local = lambda count: pl.BlockSpec((seqs, count, LANES), lambda i: (0, 0, i))
     wide = lambda count: pl.BlockSpec((seqs, count, LANES), lambda i: (0, 0, first + i))
+    counts = [stop - start] * 2 + [HALO + 2 * EXTRA] * (start == 0)
     return pl.pallas_call(
-        functools.partial(mix_grad_kernel, len(terms)),
+        functools.partial(mix_grad_kernel, 1 + len(terms), start, stop),
         grid=(width // LANES,),
-        in_specs=[local(rows)] * len(terms)
+        in_specs=[local(rows)]
+        + [local(stop - start)] * len(terms)
         + [wide(half), wide(half)]
         + [
             pl.BlockSpec((3, seqs, rows, LANES), lambda i: (0, 0, 0, first + i)),
             wide(front.shape[1]),
             pl.BlockSpec((3, 3, LANES), lambda i: (0, 0, first + i)),
         ],
-        out_specs=[local(rows), local(rows), local(HALO + 2 * EXTRA)],
-        out_shape=[
-            jax.ShapeDtypeStruct((seqs, rows, width), BF16),
-            jax.ShapeDtypeStruct((seqs, rows, width), BF16),
-            jax.ShapeDtypeStruct((seqs, HALO + 2 * EXTRA, width), BF16),
-        ],
+        out_specs=[local(count) for count in counts],
+        out_shape=[jax.ShapeDtypeStruct((seqs, count, width), BF16) for count in counts],
         scratch_shapes=[pltpu.VMEM((3 * seqs, rows + 8, LANES), F32)],
         compiler_params=params(),
         name="mix_grads",
-    )(*terms, *mixed, x, front, short_w)
-
-
-def filter_kernel(
-    group_size, mix_ref, product_ref, head_ref, front_ref, out_ref, left, columns
-):
+    )(own, *terms, *mixed, x, front, short_w)
+
+
+def join(parts, whole_ref):
+    at = 0
+    for part_ref in parts:
+        whole_ref[:, at : at + part_ref.shape[1]] = part_ref[...]
+        at += part_ref.shape[1]
+
+
+def filter_kernel(group_size, ranges, *refs):
+    product_ref, head_ref, front_ref, out_ref, left, columns, mix_ref = refs[ranges:]
+    join(refs[:ranges], mix_ref)
     seqs = mix_ref.shape[0]
     rows = out_ref.shape[1]
     groups = LANES // group_size
@@ -434,15 +459,18 @@
 
 
 def filter_sums(mix_grad, product, head, front, block_rows, offset, group_size):
-    seqs, rows, width = mix_grad.shape
+    seqs, rows, _ = product.shape
+    width = mix_grad[0].shape[2]
     first = offset // LANES
     groups = LANES // group_size
     blocks = rows // block_rows
     return pl.pallas_call(
-        functools.partial(filter_kernel, group_size),
+        functools.partial(filter_kernel, group_size, len(mix_grad)),
         grid=(width // LANES,),
         in_specs=[
-            pl.BlockSpec((seqs, rows, LANES), lambda i: (0, 0, i)),
+            pl.BlockSpec((seqs, part.shape[1], LANES), lambda i: (0, 0, i)) for part in mix_grad
+        ]
+        + [
             pl.BlockSpec((seqs, rows, LANES), lambda i: (0, 0, first + i)),
             pl.BlockSpec((seqs, EXTRA, LANES), lambda i: (0, 0, first + i)),
             pl.BlockSpec((seqs, front.shape[1], LANES), lambda i: (0, 0, first + i)),
@@ -452,30 +480,18 @@
         scratch_shapes=[
             pltpu.VMEM((blocks, groups * block_rows, seqs * LANES), BF16),
             pltpu.VMEM((blocks, 2 * block_rows, seqs * LANES), BF16),
+            pltpu.VMEM((seqs, rows, LANES), BF16),
         ],
         compiler_params=params(),
         name="filter_sums",
-    )(mix_grad, product, head, front)
-
-
-def input_grad_kernel(
-    group_size,
-    line_ref,
-    mix_ref,
-    query_ref,
-    back_ref,
-    x_ref,
-    front_ref,
-    w_ref,
-    filter_ref,
-    out_ref,
-    sums_ref,
-    band,
-    columns,
-    grads,
-    inputs,
-    edge,
-):
+    )(*mix_grad, product, head, front)
+
+
+def input_grad_kernel(group_size, ranges, *refs):
+    line_ref, back_ref, x_ref, front_ref, w_ref, filter_ref = refs[2 * ranges : 2 * ranges + 6]
+    out_ref, sums_ref, band, columns, grads, inputs, edge, mix_ref, query_ref = refs[2 * ranges + 6 :]
+    join(refs[:ranges], mix_ref)
+    join(refs[ranges : 2 * ranges], query_ref)
     seqs, rows = mix_ref.shape[0], mix_ref.shape[1]
     block = line_ref.shape[1] // 2
     groups = LANES // group_size
@@ -550,7 +566,8 @@
 def input_grads(
     line, mix_grad, query_grad, back, x, front, short_w, filter_part, offset, group_size
 ):
-    seqs, rows, width = mix_grad.shape
+    _, seqs, rows, _ = x.shape
+    width = back.shape[2]
     block = line.shape[1] // 2
     first = offset // LANES
     groups = LANES // group_size
@@ -558,12 +575,11 @@
     wide3 = lambda *sizes: pl.BlockSpec(sizes + (LANES,), lambda i: (0, 0, first + i))
     wide4 = lambda *sizes: pl.BlockSpec(sizes + (LANES,), lambda i: (0, 0, 0, first + i))
     return pl.pallas_call(
-        functools.partial(input_grad_kernel, group_size),
+        functools.partial(input_grad_kernel, group_size, len(mix_grad)),
         grid=(width // LANES,),
-        in_specs=[
+        in_specs=[local(part.shape[1]) for part in (*mix_grad, *query_grad)]
+        + [
             pl.BlockSpec((groups, 2 * block), lambda i: (first + i, 0)),
-            local(rows),
-            local(rows),
             local(HALO + 2 * EXTRA),
             wide4(3, seqs, rows),
             wide3(seqs, front.shape[1]),
@@ -584,10 +600,12 @@
             pltpu.VMEM((3 * seqs, rows + 8, LANES), F32),
             pltpu.VMEM((3 * seqs, rows + 8, LANES), F32),
             pltpu.VMEM((2 * seqs, 16, LANES), F32),
+            pltpu.VMEM((seqs, rows, LANES), BF16),
+            pltpu.VMEM((seqs, rows, LANES), BF16),
         ],
         compiler_params=params(),
         name="input_grads",
-    )(line, mix_grad, query_grad, back, x, front, short_w, filter_part)
+    )(*mix_grad, *query_grad, line, back, x, front, short_w, filter_part)
 
 
 def total_over(block, axes):
@@ -638,7 +656,6 @@
     causal = jnp.concatenate([empty[:, :1], filters[:, ::-1], empty[:, 1:]], axis=1)
     anticausal = jnp.concatenate([filters, empty], axis=1)
 
-    cotangent = grad_out.reshape(seqs * rows, width)
     product, pack = products(x, short_w, taps)
     mixed_high, gated_high = mix_high(causal, product, x, short_w, taps, group_size)
     high = [gated_high] + [to(gated_high, k) for k in partners[1:]]
@@ -647,35 +664,49 @@
         for _ in range(length - 3):
             near.append(around(after(near[-1], *high[1:])))
 
-    def send_parts(piece, ready, before):
-        parts = grad_parts(pos, after(cotangent, *ready), piece, members)
-        shape = (seqs, rows, piece.span)
-        parts = [after(block, *before) for block in parts]
-        sent = [parts[0]] + [to(parts[k], k) for k in partners[1:]]
-        return [block.reshape(shape) for block in sent]
-
-    all_terms = [send_parts(weights[0], high[1:], [])]
+    def send_parts(piece, ranges, ready, before):
+        own, parts = grad_parts(pos, after(grad_out, *ready), piece, members, ranges)
+        sent = [[after(block, *before) for block in blocks] for blocks in parts]
+        return own, [[to(block, k + 1) for k, block in enumerate(blocks)] for blocks in sent]
+
+    ranges = [[(0, rows)]]
+    own, got = send_parts(weights[0], ranges[0], high[1:], [])
+    owns, gots = [own], [got]
     if ring:
-        near[-1] = after(near[-1], *all_terms[0][1:3])
-        pack = after(pack, near[-1])
+        near[-1] = after(near[-1], *got[0][:2])
         weights.append(Passed(out_w, near, [swap(block) for block in near], cut))
-        all_terms.append(send_parts(weights[1], [], all_terms[0][1:]))
-
-    front = shift(pack, "ctx", 1)
+        ranges.append([(0, rows)])
+        own, got = send_parts(weights[1], ranges[1], [], got[0])
+        owns.append(own)
+        gots.append(got)
+
+    block_out = block_output(pos, weights, high, 1, 2, None)
+    front = shift(after(pack, owns[-1]), "ctx", 1)
+    front = after(front, block_out)
     mixed_low, gated_low, head = mix_low(causal, front, product, x, short_w, taps, group_size)
-    sent = after(gated_low, all_terms[-1][0])
+    sent = after(gated_low, owns[-1])
     low = [gated_low] + [to(sent, k) for k in partners[1:]]
-    block_out = block_output(pos, weights, high, 1, 2, None)
 
     outs, sums = [], []
     for p, piece in enumerate(weights):
-        terms = all_terms[p]
-        if p:
-            terms = [after(terms[0], outs[-1], block_out)] + terms[1:]
-        mix_grad, query_grad, pack = mix_grads(
-            terms, (mixed_low, mixed_high), x, front, short_w, piece.start
-        )
-        back = shift(pack, "ctx", -1)
+        mix_grad, query_grad, back = [], [], None
+        for (start, stop), terms in zip(ranges[p], gots[p]):
+            held = after(owns[p], outs[-1], block_out) if p else owns[p]
+            found = mix_grads(
+                held,
+                terms,
+                start,
+                stop,
+                (mixed_low, mixed_high),
+                x,
+                front,
+                short_w,
+                piece.start,
+            )
+            mix_grad.append(found[0])
+            query_grad.append(found[1])
+            if start == 0:
+                back = shift(found[2], "ctx", -1)
         back = after(back, *([] if p else [block_out]))
         folded = filter_sums(mix_grad, product, head, front, taps, piece.start, group_size)
         grad, part = input_grads(

time: 191 us -> 183 us (0.958)
  Pallas kernels: 64.6 us -> 54.7 us
  waiting for transfers between devices: 51.5 us -> 56.2 us
    ppermute x3, waiting for transfers between devices: 5.4 us -> 15.8 us  [shift(): return lax.ppermute(block, axis, route)]
    pallas_call x8, Pallas kernels: 38.8 us -> 32.6 us  [the longest x2 11.2 us: input_grads(): pl.pallas_call(functools.partial(input_grad_kernel, group_size, len(mix_g...]
    ppermute x12, waiting for transfers between devices: 21.8 us -> 17.3 us  [shards(): lax.ppermute(block, 'grp', [(i, i ^ k) for i in partners])]
    pallas_call x2, Pallas kernels: 15.1 us -> 11.4 us  [block_output(): pl.pallas_call(functools.partial(out_kernel, weights, steps), grid=(1,),...]
    unnamed x63 -> x45, local copies, waits for them, and re-layouts: 13.9 us -> 13.4 us
  transfers between devices with their start and end apart: 25 -> 25, of which waited for: 13 -> 14; matrix products, arithmetic and copies ran while one was open for 4% -> 4% of each run, Pallas kernels for 32% -> 29%
where the time goes in v3:
time: 183 us
  waiting for transfers between devices  56.2 us (31%)
  Pallas kernels  54.7 us (30%)
  starting transfers between devices  38.2 us (21%)
  local copies, waits for them, and re-layouts  18.1 us (10%)
  between operations  14.4 us (8%)
    ppermute x3, waiting for transfers between devices, shards(): lax.ppermute(block, 'ctx', [(i, (i + 1) % length) for i in range(length)])  21.5 us
    ppermute x12, waiting for transfers between devices, shards(): lax.ppermute(block, 'grp', [(i, i ^ k) for i in partners])  17.3 us
    ppermute x3, waiting for transfers between devices, shift(): return lax.ppermute(block, axis, route)  15.8 us
    ppermute x12, starting transfers between devices, shards(): lax.ppermute(block, 'grp', [(i, i ^ k) for i in partners])  15.4 us
    unnamed x45, local copies, waits for them, and re-layouts  13.4 us
    pallas_call x2, Pallas kernels, block_output(): pl.pallas_call(functools.partial(out_kernel, weights, steps), grid=(1,),...  11.4 us
    pallas_call x2, Pallas kernels, input_grads(): pl.pallas_call(functools.partial(input_grad_kernel, group_size, len(mix_g...  11.2 us
    ppermute x3, starting transfers between devices, shards(): lax.ppermute(block, 'ctx', [(i, (i + 1) % length) for i in range(length)])  11.2 us
  transfers between devices with their start and end apart: 25, of which 14 were waited for; matrix products, arithmetic and copies ran while one was open for 4% of the time, Pallas kernels for 29%

profile of v3, /device:TPU:0, one launch (start us, length us, event | category | flops | bytes accessed | tf_op | source)
XLA Modules:
  0.0 182.9 jit_solution(10379661893132532137)
XLA Ops:
  7.2 1.8 constant_dynamic-slice_fusion.1
  9.0 2.0 %constant_dynamic-slice_fusion = bf16[320,1024]{1,0:T(8,128)(2,1)} fusion(bf16[1024,1024]{1,0:T(8,128)(2,1)} %refs_1_.3, s32[]{:T(128)S(6)} %select_n.7), kind=kLoop, calls=%fused_computation.10 | loop fusion | bytes 1310724 | tf_op jit(solution)/shard_map/dynamic_slice | solution.py:646
  11.0 3.0 %collective-permute-start = (bf16[320,1024]{1,0:T(8,128)(2,1)}, bf16[320,1024]{1,0:T(8,128)(2,1)}, u32[]{:S(2)}, u32[]{:S(2)}) collective-permute-start(bf16[320,1024]{1,0:T(8,128)(2,1)} %constant_dynamic-slice_fusion), channel_id=1, source_target_pairs={{0,4},{4,8},{8,12},{12,0},{1,5},{5,9},{9,13},{13,1},{2,6},{6,10},{... | collective-permute-start | bytes 1966088 | tf_op jit(solution)/shard_map/ppermute | solution.py:635
  14.0 2.2 %copy.16 = bf16[2,256,3,1024]{3,1,0,2:T(8,128)(2,1)S(1)} copy(bf16[2,256,3,1024]{3,1,2,0:T(8,128)(2,1)} %param.5) | data formatting | bytes 6291456 | tf_op args[0]
  16.4 2.7 %products.1 = (bf16[2,256,1024]{2,1,0:T(8,128)(2,1)S(1)}, bf16[2,160,1024]{2,1,0:T(8,128)(2,1)S(1)}) custom-call(bf16[3,2,256,1024]{3,2,1,0:T(8,128)(2,1)S(1)} %bitcast.15, f32[3,3,1024]{2,1,0:T(4,128)S(1)} %copy-done.9), custom_call_target="tpu_custom_call" | custom-call | tf_op jit(solution)/shard_map/products/pallas_call | solution.py:81
  20.1 3.8 %mix_high.1 = (f32[2,128,1024]{2,1,0:T(8,128)S(1)}, bf16[2,128,1024]{2,1,0:T(8,128)(2,1)S(1)}) custom-call(f32[64,256]{1,0:T(8,128)S(1)} %maximum_maximum_fusion.line_ref, bf16[2,256,1024]{2,1,0:T(8,128)(2,1)S(1)} %get-tuple-element.41.low_ref.high_ref.product_ref.refs_1_, bf16[2,256,1024]{2,1,0:T(8,128)(2,1)S(1)} %get-tuple-element.41.low_ref.high_ref.product_ref.refs_1_, ...), custom_call_target="tpu_custom_call" | custom-call | tf_op jit(solution)/shard_map/mix_high/pallas_call | solution.py:126
  24.0 1.0 copy-done.2
  24.9 1.0 copy-done.7
  25.9 12.5 %collective-permute-done.refs_1_.refs_2_ = bf16[320,1024]{1,0:T(8,128)(2,1)} collective-permute-done((bf16[320,1024]{1,0:T(8,128)(2,1)}, bf16[320,1024]{1,0:T(8,128)(2,1)}, u32[]{:S(2)}, u32[]{:S(2)}) %collective-permute-start) | collective-permute-done | bytes 655392 | tf_op jit(solution)/shard_map/ppermute | solution.py:635
  38.4 7.8 %collective-permute-start.1 = (bf16[320,1024]{1,0:T(8,128)(2,1)}, bf16[320,1024]{1,0:T(8,128)(2,1)}, u32[]{:S(2)}, u32[]{:S(2)}) collective-permute-start(bf16[320,1024]{1,0:T(8,128)(2,1)} %collective-permute-done.refs_1_.refs_2_), channel_id=1, source_target_pairs={{0,4},{4,8},{8,12},{12,0},{1,5},{5,9},{9,13},{13,1},{2,6},{6,10},{... | collective-permute-start | bytes 1966088 | tf_op jit(solution)/shard_map/ppermute | solution.py:635
  46.2 1.5 collective-permute-start.2
  47.8 1.5 collective-permute-start.3
  50.5 8.6 %collective-permute-done.2.refs_9_ = bf16[2,128,1024]{2,1,0:T(8,128)(2,1)S(1)} collective-permute-done((bf16[2,128,1024]{2,1,0:T(8,128)(2,1)S(1)}, bf16[2,128,1024]{2,1,0:T(8,128)(2,1)S(1)}, u32[]{:S(2)}, u32[]{:S(2)}) %collective-permute-start.2) | collective-permute-done | bytes 524320 | tf_op jit(solution)/shard_map/ppermute | solution.py:634
  59.9 6.0 %collective-permute-done.3.refs_10_ = bf16[2,128,1024]{2,1,0:T(8,128)(2,1)S(1)} collective-permute-done((bf16[2,128,1024]{2,1,0:T(8,128)(2,1)S(1)}, bf16[2,128,1024]{2,1,0:T(8,128)(2,1)S(1)}, u32[]{:S(2)}, u32[]{:S(2)}) %collective-permute-start.3) | collective-permute-done | bytes 524320 | tf_op jit(solution)/shard_map/ppermute | solution.py:634
  66.7 0.9 copy-done.16
  67.6 3.1 %collective-permute-done.1.refs_2_.refs_3_ = bf16[320,1024]{1,0:T(8,128)(2,1)} collective-permute-done((bf16[320,1024]{1,0:T(8,128)(2,1)}, bf16[320,1024]{1,0:T(8,128)(2,1)}, u32[]{:S(2)}, u32[]{:S(2)}) %collective-permute-start.1) | collective-permute-done | bytes 655392 | tf_op jit(solution)/shard_map/ppermute | solution.py:635
  71.1 1.9 %copy-done = bf16[1536,1024]{1,0:T(8,128)(2,1)S(1)} copy-done((bf16[1536,1024]{1,0:T(8,128)(2,1)S(1)}, bf16[1536,1024]{1,0:T(8,128)(2,1)}, u32[]{:S(2)}) %copy-start) | copy-done | bytes 3145752
  73.0 1.2 copy-done.5
  74.2 3.8 %grad_parts.2 = (f32[2,256,384]{2,1,0:T(8,128)S(1)}, bf16[2,256,384]{2,1,0:T(8,128)(2,1)S(1)}, bf16[2,256,384]{2,1,0:T(8,128)(2,1)S(1)}, bf16[2,256,384]{2,1,0:T(8,128)(2,1)S(1)}) custom-call(s32[3]{0:T(128)S(1)} %pad_add_fusion.pos_ref, bf16[512,1024]{1,0:T(8,128)(2,1)S(1)} %bitcast.22, bf16[1536,1024]{1,0:T(8,128)(2,1)S(1)} %copy-done), custom_call_target="tpu_custom_call" | custom-call | tf_op jit(solution)/shard_map/grad_parts/pallas_call | solution.py:295
  78.0 1.2 collective-permute-start.6
  79.3 1.5 collective-permute-start.7
  81.3 5.9 %collective-permute-done.5.refs_3_.refs_4_ = bf16[320,1024]{1,0:T(8,128)(2,1)} collective-permute-done((bf16[320,1024]{1,0:T(8,128)(2,1)}, bf16[320,1024]{1,0:T(8,128)(2,1)}, u32[]{:S(2)}, u32[]{:S(2)}) %collective-permute-start.5) | collective-permute-done | bytes 655392 | tf_op jit(solution)/shard_map/ppermute | solution.py:635
  87.7 2.0 %collective-permute-start.15 = (bf16[2,256,384]{2,1,0:T(8,128)(2,1)S(1)}, bf16[2,256,384]{2,1,0:T(8,128)(2,1)S(1)}, u32[]{:S(2)}, u32[]{:S(2)}) collective-permute-start(bf16[2,256,384]{2,1,0:T(8,128)(2,1)S(1)} %get-tuple-element.57), channel_id=1, source_target_pairs={{0,3},{1,2},{2,1},{3,0},{4,7},{5,6},{6,5},{7,4},{8,11},{9,10},{10,... | collective-permute-start | bytes 1179656 | tf_op jit(solution)/shard_map/ppermute | solution.py:634
  90.0 7.2 %grad_parts.3 = (f32[2,256,640]{2,1,0:T(8,128)S(1)}, bf16[2,256,640]{2,1,0:T(8,128)(2,1)S(1)}, bf16[2,256,640]{2,1,0:T(8,128)(2,1)S(1)}, bf16[2,256,640]{2,1,0:T(8,128)(2,1)S(1)}) custom-call(s32[3]{0:T(128)S(1)} %pad_add_fusion.pos_ref, bf16[512,1024]{1,0:T(8,128)(2,1)S(1)} %bitcast.23, bf16[1024,1024]{1,0:T(8,128)(2,1)S(1)} %copy-done.4, ...), custom_call_target="tpu_custom_call" | custom-call | tf_op jit(solution)/shard_map/grad_parts/pallas_call | solution.py:295
  97.2 3.5 %collective-permute-start.11 = (bf16[2,160,1024]{2,1,0:T(8,128)(2,1)S(1)}, bf16[2,160,1024]{2,1,0:T(8,128)(2,1)S(1)}, u32[]{:S(2)}, u32[]{:S(2)}) collective-permute-start(bf16[2,160,1024]{2,1,0:T(8,128)(2,1)S(1)} %copy-done.19), channel_id=1, source_target_pairs={{0,4},{4,8},{8,12},{1,5},{5,9},{9,13},{2,6},{6,10},{10,14},{3,7},{... | collective-permute-start | bytes 1966088 | tf_op jit(solution)/shard_map/ppermute | solution.py:26
  100.8 2.6 %collective-permute-start.19 = (bf16[2,256,640]{2,1,0:T(8,128)(2,1)S(1)}, bf16[2,256,640]{2,1,0:T(8,128)(2,1)S(1)}, u32[]{:S(2)}, u32[]{:S(2)}) collective-permute-start(bf16[2,256,640]{2,1,0:T(8,128)(2,1)S(1)} %get-tuple-element.71), channel_id=1, source_target_pairs={{0,3},{1,2},{2,1},{3,0},{4,7},{5,6},{6,5},{7,4},{8,11},{9,10},{10,... | collective-permute-start | bytes 1966088 | tf_op jit(solution)/shard_map/ppermute | solution.py:634
  104.3 5.7 %block_output.2.refs_12_ = bf16[2,256,1024]{2,1,0:T(8,128)(2,1)} custom-call(s32[3]{0:T(128)S(1)} %pad_add_fusion.pos_ref, bf16[1536,1024]{1,0:T(8,128)(2,1)S(1)} %copy-done.1, bf16[1024,1024]{1,0:T(8,128)(2,1)S(1)} %copy-done.4, bf16[320,1024]{1,0:T(8,128)(2,1)} %collective-permute-done.refs_1_.refs_2_, ...), custom_call_target="tpu_custom_call" | custom-call | tf_op jit(solution)/shard_map/block_output/pallas_call | solution.py:340
  110.1 4.9 %collective-permute-done.11.front_ref.refs_7_.refs_3_.refs_5_ = bf16[2,160,1024]{2,1,0:T(8,128)(2,1)S(1)} collective-permute-done((bf16[2,160,1024]{2,1,0:T(8,128)(2,1)S(1)}, bf16[2,160,1024]{2,1,0:T(8,128)(2,1)S(1)}, u32[]{:S(2)}, u32[]{:S(2)}) %collective-permute-start.11) | collective-permute-done | bytes 655392 | tf_op jit(solution)/shard_map/ppermute | solution.py:26
  115.0 4.1 %mix_low.1 = (f32[2,128,1024]{2,1,0:T(8,128)S(1)}, bf16[2,128,1024]{2,1,0:T(8,128)(2,1)S(1)}, bf16[2,16,1024]{2,1,0:T(8,128)(2,1)S(1)}) custom-call(f32[64,256]{1,0:T(8,128)S(1)} %maximum_maximum_fusion.line_ref, bf16[2,160,1024]{2,1,0:T(8,128)(2,1)S(1)} %collective-permute-done.11.front_ref.refs_7_.refs_3_.refs_5_, bf16[2,256,1024]{2,1,0:T(8,128)(2,1)S(1)} %copy-done.3, ...), custom_call_target="tpu_custom_call" | custom-call | tf_op jit(solution)/shard_map/mix_low/pallas_call | solution.py:189
  119.2 1.5 mix_grads.2
  120.7 1.3 collective-permute-start.16
  122.0 2.3 %filter_sums.2.refs_7_ = f32[24,128]{1,0:T(8,128)S(1)} custom-call(bf16[2,256,384]{2,1,0:T(8,128)(2,1)S(1)} %get-tuple-element.59.refs_0_, bf16[2,256,1024]{2,1,0:T(8,128)(2,1)S(1)} %copy-done.3, bf16[2,16,1024]{2,1,0:T(8,128)(2,1)S(1)} %get-tuple-element.63.refs_2_, bf16[2,160,1024]{2,1,0:T(8,128)(2,1)S(1)} %collective-permute-done.11.front_ref.refs_7_.refs_3_.refs_5_), custom_call_target="tpu_custom_call" | custom-call | tf_op jit(solution)/shard_map/filter_sums/pallas_call | solution.py:467
  124.4 6.7 %collective-permute-done.16.refs_3_ = bf16[2,176,384]{2,1,0:T(8,128)(2,1)S(1)} collective-permute-done((bf16[2,176,384]{2,1,0:T(8,128)(2,1)S(1)}, bf16[2,176,384]{2,1,0:T(8,128)(2,1)S(1)}, u32[]{:S(2)}, u32[]{:S(2)}) %collective-permute-start.16) | collective-permute-done | bytes 270368 | tf_op jit(solution)/shard_map/ppermute | solution.py:26
  131.1 4.2 %input_grads.2 = (bf16[3,2,256,384]{3,2,1,0:T(8,128)(2,1)S(1)}, f32[3,24,128]{2,1,0:T(8,128)S(1)}) custom-call(bf16[2,256,384]{2,1,0:T(8,128)(2,1)S(1)} %get-tuple-element.59.refs_0_, bf16[2,256,384]{2,1,0:T(8,128)(2,1)S(1)} %get-tuple-element.60.refs_1_, f32[64,256]{1,0:T(8,128)S(1)} %concatenate.13.refs_2_, ...), custom_call_target="tpu_custom_call" | custom-call | tf_op jit(solution)/shard_map/input_grads/pallas_call | solution.py:577
  135.3 2.6 %mix_grads.3 = (bf16[2,256,640]{2,1,0:T(8,128)(2,1)S(1)}, bf16[2,256,640]{2,1,0:T(8,128)(2,1)S(1)}, bf16[2,176,640]{2,1,0:T(8,128)(2,1)S(1)}) custom-call(f32[2,256,640]{2,1,0:T(8,128)S(1)} %get-tuple-element.65.refs_0_, bf16[2,256,640]{2,1,0:T(8,128)(2,1)S(1)} %collective-permute-done.17.refs_1_, bf16[2,256,640]{2,1,0:T(8,128)(2,1)S(1)} %collective-permute-done.18.refs_2_, ...), custom_call_target="tpu_custom_call" | custom-call | tf_op jit(solution)/shard_map/mix_grads/pallas_call | solution.py:391
  137.9 1.3 collective-permute-start.20
  139.2 1.4 collective-permute-start.12
  140.6 1.6 collective-permute-start.13
  142.8 3.9 %filter_sums.3.refs_7_ = f32[40,128]{1,0:T(8,128)S(1)} custom-call(bf16[2,256,640]{2,1,0:T(8,128)(2,1)S(1)} %get-tuple-element.72.refs_0_, bf16[2,256,1024]{2,1,0:T(8,128)(2,1)S(1)} %copy-done.3, bf16[2,16,1024]{2,1,0:T(8,128)(2,1)S(1)} %get-tuple-element.63.refs_2_, bf16[2,160,1024]{2,1,0:T(8,128)(2,1)S(1)} %collective-permute-done.11.front_ref.refs_7_.refs_3_.refs_5_), custom_call_target="tpu_custom_call" | custom-call | tf_op jit(solution)/shard_map/filter_sums/pallas_call | solution.py:467
  146.7 4.1 %collective-permute-done.20.refs_3_ = bf16[2,176,640]{2,1,0:T(8,128)(2,1)S(1)} collective-permute-done((bf16[2,176,640]{2,1,0:T(8,128)(2,1)S(1)}, bf16[2,176,640]{2,1,0:T(8,128)(2,1)S(1)}, u32[]{:S(2)}, u32[]{:S(2)}) %collective-permute-start.20) | collective-permute-done | bytes 450592 | tf_op jit(solution)/shard_map/ppermute | solution.py:26
  150.8 7.0 %input_grads.3 = (bf16[3,2,256,640]{3,2,1,0:T(8,128)(2,1)S(1)}, f32[5,24,128]{2,1,0:T(8,128)S(1)}) custom-call(bf16[2,256,640]{2,1,0:T(8,128)(2,1)S(1)} %get-tuple-element.72.refs_0_, bf16[2,256,640]{2,1,0:T(8,128)(2,1)S(1)} %get-tuple-element.73.refs_1_, f32[64,256]{1,0:T(8,128)S(1)} %concatenate.13.refs_2_, ...), custom_call_target="tpu_custom_call" | custom-call | tf_op jit(solution)/shard_map/input_grads/pallas_call | solution.py:577
  157.9 1.3 collective-permute-done.21
  159.3 2.7 %collective-permute-start.22 = (f32[8,24,128]{2,1,0:T(8,128)S(1)}, f32[8,24,128]{2,1,0:T(8,128)S(1)}, u32[]{:S(2)}, u32[]{:S(2)}) collective-permute-start(f32[8,24,128]{2,1,0:T(8,128)S(1)} %add.21), channel_id=1, source_target_pairs={{0,8},{4,12},{8,0},{12,4},{16,24},{20,28},{24,16},{28,20},{1,9},{5... | collective-permute-start | bytes 294920 | tf_op jit(solution)/shard_map/ppermute | solution.py:621
  162.0 1.3 collective-permute-done.13.refs_10_
  163.3 0.9 collective-permute-done.14.refs_11_
  164.2 5.7 %block_output.3 = bf16[2,256,1024]{2,1,0:T(8,128)(2,1)} custom-call(s32[3]{0:T(128)S(1)} %pad_add_fusion.pos_ref, bf16[1536,1024]{1,0:T(8,128)(2,1)S(1)} %copy-done.1, bf16[1024,1024]{1,0:T(8,128)(2,1)S(1)} %copy-done.4, bf16[320,1024]{1,0:T(8,128)(2,1)} %collective-permute-done.refs_1_.refs_2_, ...), custom_call_target="tpu_custom_call", output_to_operand_aliasing={{}: (13, {})} | custom-call | tf_op jit(solution)/shard_map/block_output/pallas_call | solution.py:340
  169.9 2.2 %collective-permute-start.23 = (f32[8,24,128]{2,1,0:T(8,128)S(1)}, f32[8,24,128]{2,1,0:T(8,128)S(1)}, u32[]{:S(2)}, u32[]{:S(2)}) collective-permute-start(f32[8,24,128]{2,1,0:T(8,128)S(1)} %add.22), channel_id=1, source_target_pairs={{0,4},{4,0},{8,12},{12,8},{16,20},{20,16},{24,28},{28,24},{1,5},{5... | collective-permute-start | bytes 294920 | tf_op jit(solution)/shard_map/ppermute | solution.py:621
  172.6 2.0 %copy.14 = bf16[2,256,3,1024]{3,1,2,0:T(8,128)(2,1)} copy(bf16[2,256,3,1024]{3,1,0,2:T(8,128)(2,1)S(1)} %maximum_bitcast_fusion) | data formatting | bytes 6291456
  (81 shorter events, 9.4 us)
Async XLA Ops:
  7.2 63.9 %all-gather.2.cloned.1.call-start = ((), (), s32[]{:S(2)}) async-start(), calls=%async_computation | async-start | bytes 3538944 | tf_op jit(solution)/shard_map/all_gather | solution.py:648
  11.0 5.2 %copy-start.20 = (bf16[64,128]{1,0:T(8,128)(2,1)S(1)}, bf16[64,128]{1,0:T(8,128)(2,1)}, u32[]{:S(2)}) copy-start(bf16[64,128]{1,0:T(8,128)(2,1)} %param.7) | copy-start | bytes 49156
  11.0 5.4 %copy-start.9 = (f32[3,3,1024]{2,1,0:T(4,128)S(1)}, f32[3,3,1024]{2,1,0:T(4,128)}, u32[]{:S(2)}) copy-start(f32[3,3,1024]{2,1,0:T(4,128)} %refs_6_.3) | copy-start | bytes 110596
  11.0 27.4 %collective-permute-start = (bf16[320,1024]{1,0:T(8,128)(2,1)}, bf16[320,1024]{1,0:T(8,128)(2,1)}, u32[]{:S(2)}, u32[]{:S(2)}) collective-permute-start(bf16[320,1024]{1,0:T(8,128)(2,1)} %constant_dynamic-slice_fusion), channel_id=1, source_target_pairs={{0,4},{4,8},{8,12},{12,0},{1,5},{5,9},{9,13},{13,1},{2,6},{6,10},{... | collective-permute-start | bytes 1966088 | tf_op jit(solution)/shard_map/ppermute | solution.py:635
  19.2 0.8 copy-start.18
  24.0 1.0 copy-start.2
  24.9 1.0 copy-start.7
  38.4 32.3 %collective-permute-start.1 = (bf16[320,1024]{1,0:T(8,128)(2,1)}, bf16[320,1024]{1,0:T(8,128)(2,1)}, u32[]{:S(2)}, u32[]{:S(2)}) collective-permute-start(bf16[320,1024]{1,0:T(8,128)(2,1)} %collective-permute-done.refs_1_.refs_2_), channel_id=1, source_target_pairs={{0,4},{4,8},{8,12},{12,0},{1,5},{5,9},{9,13},{13,1},{2,6},{6,10},{... | collective-permute-start | bytes 1966088 | tf_op jit(solution)/shard_map/ppermute | solution.py:635
  46.2 12.9 %collective-permute-start.2 = (bf16[2,128,1024]{2,1,0:T(8,128)(2,1)S(1)}, bf16[2,128,1024]{2,1,0:T(8,128)(2,1)S(1)}, u32[]{:S(2)}, u32[]{:S(2)}) collective-permute-start(bf16[2,128,1024]{2,1,0:T(8,128)(2,1)S(1)} %get-tuple-element.44.refs_8_), channel_id=1, source_target_pairs={{0,1},{1,0},{2,3},{3,2},{4,5},{5,4},{6,7},{7,6},{8,9},{9,8},{10,11... | collective-permute-start | bytes 1572872 | tf_op jit(solution)/shard_map/ppermute | solution.py:634
  47.8 18.1 %collective-permute-start.3 = (bf16[2,128,1024]{2,1,0:T(8,128)(2,1)S(1)}, bf16[2,128,1024]{2,1,0:T(8,128)(2,1)S(1)}, u32[]{:S(2)}, u32[]{:S(2)}) collective-permute-start(bf16[2,128,1024]{2,1,0:T(8,128)(2,1)S(1)} %get-tuple-element.44.refs_8_), channel_id=1, source_target_pairs={{0,2},{1,3},{2,0},{3,1},{4,6},{5,7},{6,4},{7,5},{8,10},{9,11},{10,... | collective-permute-start | bytes 1572872 | tf_op jit(solution)/shard_map/ppermute | solution.py:634
  49.3 17.5 %collective-permute-start.4 = (bf16[2,128,1024]{2,1,0:T(8,128)(2,1)S(1)}, bf16[2,128,1024]{2,1,0:T(8,128)(2,1)S(1)}, u32[]{:S(2)}, u32[]{:S(2)}) collective-permute-start(bf16[2,128,1024]{2,1,0:T(8,128)(2,1)S(1)} %get-tuple-element.44.refs_8_), channel_id=1, source_target_pairs={{0,3},{1,2},{2,1},{3,0},{4,7},{5,6},{6,5},{7,4},{8,11},{9,10},{10,... | collective-permute-start | bytes 1572872 | tf_op jit(solution)/shard_map/ppermute | solution.py:634
  49.7 0.8 copy-start.10
  59.1 0.8 copy-start.12
  65.9 0.8 copy-start.14
  66.7 0.9 copy-start.16
  70.7 16.5 %collective-permute-start.5 = (bf16[320,1024]{1,0:T(8,128)(2,1)}, bf16[320,1024]{1,0:T(8,128)(2,1)}, u32[]{:S(2)}, u32[]{:S(2)}) collective-permute-start(bf16[320,1024]{1,0:T(8,128)(2,1)} %collective-permute-done.1.refs_2_.refs_3_), channel_id=1, source_target_pairs={{0,4},{4,8},{8,12},{12,0},{1,5},{5,9},{9,13},{13,1},{2,6},{6,10},{... | collective-permute-start | bytes 1966088 | tf_op jit(solution)/shard_map/ppermute | solution.py:635
  71.1 1.9 %copy-start = (bf16[1536,1024]{1,0:T(8,128)(2,1)S(1)}, bf16[1536,1024]{1,0:T(8,128)(2,1)}, u32[]{:S(2)}) copy-start(bf16[1536,1024]{1,0:T(8,128)(2,1)} %all-gather.2.cloned.1.call-done.refs_0_) | copy-start | bytes 9437188
  73.0 1.2 copy-start.5
  74.2 15.8 %copy-start.4 = (bf16[1024,1024]{1,0:T(8,128)(2,1)S(1)}, bf16[1024,1024]{1,0:T(8,128)(2,1)}, u32[]{:S(2)}) copy-start(bf16[1024,1024]{1,0:T(8,128)(2,1)} %refs_1_.3) | copy-start | bytes 6291460
  74.2 15.8 %copy-start.6 = (bf16[2,256,1024]{2,1,0:T(8,128)(2,1)S(1)}, bf16[2,256,1024]{2,1,0:T(8,128)(2,1)}, u32[]{:S(2)}) copy-start(bf16[2,256,1024]{2,1,0:T(8,128)(2,1)} %param.9) | copy-start | bytes 3145732
  78.0 9.2 %collective-permute-start.6 = (bf16[2,256,384]{2,1,0:T(8,128)(2,1)S(1)}, bf16[2,256,384]{2,1,0:T(8,128)(2,1)S(1)}, u32[]{:S(2)}, u32[]{:S(2)}) collective-permute-start(bf16[2,256,384]{2,1,0:T(8,128)(2,1)S(1)} %get-tuple-element.47), channel_id=1, source_target_pairs={{0,1},{1,0},{2,3},{3,2},{4,5},{5,4},{6,7},{7,6},{8,9},{9,8},{10,11... | collective-permute-start | bytes 1179656 | tf_op jit(solution)/shard_map/ppermute | solution.py:634
  79.3 8.4 %collective-permute-start.7 = (bf16[2,256,384]{2,1,0:T(8,128)(2,1)S(1)}, bf16[2,256,384]{2,1,0:T(8,128)(2,1)S(1)}, u32[]{:S(2)}, u32[]{:S(2)}) collective-permute-start(bf16[2,256,384]{2,1,0:T(8,128)(2,1)S(1)} %get-tuple-element.48), channel_id=1, source_target_pairs={{0,2},{1,3},{2,0},{3,1},{4,6},{5,7},{6,4},{7,5},{8,10},{9,11},{10,... | collective-permute-start | bytes 1179656 | tf_op jit(solution)/shard_map/ppermute | solution.py:634
  80.8 8.9 %collective-permute-start.8 = (bf16[320,1024]{1,0:T(8,128)(2,1)}, bf16[320,1024]{1,0:T(8,128)(2,1)S(1)}, u32[]{:S(2)}, u32[]{:S(2)}) collective-permute-start(bf16[320,1024]{1,0:T(8,128)(2,1)} %collective-permute-done.refs_1_.refs_2_), channel_id=1, source_target_pairs={{0,16},{16,0},{1,17},{17,1},{2,18},{18,2},{3,19},{19,3},{4,20},{20... | collective-permute-start | bytes 1966088 | tf_op jit(solution)/shard_map/ppermute | solution.py:636
  80.8 8.9 %collective-permute-start.9 = (bf16[320,1024]{1,0:T(8,128)(2,1)}, bf16[320,1024]{1,0:T(8,128)(2,1)S(1)}, u32[]{:S(2)}, u32[]{:S(2)}) collective-permute-start(bf16[320,1024]{1,0:T(8,128)(2,1)} %collective-permute-done.1.refs_2_.refs_3_), channel_id=1, source_target_pairs={{0,16},{16,0},{1,17},{17,1},{2,18},{18,2},{3,19},{19,3},{4,20},{20... | collective-permute-start | bytes 1966088 | tf_op jit(solution)/shard_map/ppermute | solution.py:636
  87.7 2.3 %collective-permute-start.10 = (bf16[320,1024]{1,0:T(8,128)(2,1)}, bf16[320,1024]{1,0:T(8,128)(2,1)S(1)}, u32[]{:S(2)}, u32[]{:S(2)}) collective-permute-start(bf16[320,1024]{1,0:T(8,128)(2,1)} %collective-permute-done.5.refs_3_.refs_4_), channel_id=1, source_target_pairs={{0,16},{16,0},{1,17},{17,1},{2,18},{18,2},{3,19},{19,3},{4,20},{20... | collective-permute-start | bytes 1966088 | tf_op jit(solution)/shard_map/ppermute | solution.py:636
  87.7 13.1 %collective-permute-start.15 = (bf16[2,256,384]{2,1,0:T(8,128)(2,1)S(1)}, bf16[2,256,384]{2,1,0:T(8,128)(2,1)S(1)}, u32[]{:S(2)}, u32[]{:S(2)}) collective-permute-start(bf16[2,256,384]{2,1,0:T(8,128)(2,1)S(1)} %get-tuple-element.57), channel_id=1, source_target_pairs={{0,3},{1,2},{2,1},{3,0},{4,7},{5,6},{6,5},{7,4},{8,11},{9,10},{10,... | collective-permute-start | bytes 1179656 | tf_op jit(solution)/shard_map/ppermute | solution.py:634
  90.0 7.2 %copy-start.19 = (bf16[2,160,1024]{2,1,0:T(8,128)(2,1)S(1)}, bf16[2,160,1024]{2,1,0:T(8,128)(2,1)}, u32[]{:S(2)}) copy-start(bf16[2,160,1024]{2,1,0:T(8,128)(2,1)} %copy-done.18) | copy-start | bytes 1966084
  90.0 14.3 %copy-start.1 = (bf16[1536,1024]{1,0:T(8,128)(2,1)S(1)}, bf16[1536,1024]{1,0:T(8,128)(2,1)}, u32[]{:S(2)}) copy-start(bf16[1536,1024]{1,0:T(8,128)(2,1)} %all-gather.2.cloned.1.call-done.refs_0_) | copy-start | bytes 9437188
  90.0 14.3 %copy-start.11 = (bf16[2,128,1024]{2,1,0:T(8,128)(2,1)S(1)}, bf16[2,128,1024]{2,1,0:T(8,128)(2,1)}, u32[]{:S(2)}) copy-start(bf16[2,128,1024]{2,1,0:T(8,128)(2,1)} %copy-done.10) | copy-start | bytes 1572868
  90.0 14.3 %copy-start.13 = (bf16[2,128,1024]{2,1,0:T(8,128)(2,1)S(1)}, bf16[2,128,1024]{2,1,0:T(8,128)(2,1)}, u32[]{:S(2)}) copy-start(bf16[2,128,1024]{2,1,0:T(8,128)(2,1)} %copy-done.12) | copy-start | bytes 1572868
  90.0 14.3 %copy-start.15 = (bf16[2,128,1024]{2,1,0:T(8,128)(2,1)S(1)}, bf16[2,128,1024]{2,1,0:T(8,128)(2,1)}, u32[]{:S(2)}) copy-start(bf16[2,128,1024]{2,1,0:T(8,128)(2,1)} %copy-done.14) | copy-start | bytes 1572868
  90.0 14.3 %copy-start.17 = (bf16[2,128,1024]{2,1,0:T(8,128)(2,1)S(1)}, bf16[2,128,1024]{2,1,0:T(8,128)(2,1)}, u32[]{:S(2)}) copy-start(bf16[2,128,1024]{2,1,0:T(8,128)(2,1)} %copy-done.16) | copy-start | bytes 1572868
  97.2 17.8 %collective-permute-start.11 = (bf16[2,160,1024]{2,1,0:T(8,128)(2,1)S(1)}, bf16[2,160,1024]{2,1,0:T(8,128)(2,1)S(1)}, u32[]{:S(2)}, u32[]{:S(2)}) collective-permute-start(bf16[2,160,1024]{2,1,0:T(8,128)(2,1)S(1)} %copy-done.19), channel_id=1, source_target_pairs={{0,4},{4,8},{8,12},{1,5},{5,9},{9,13},{2,6},{6,10},{10,14},{3,7},{... | collective-permute-start | bytes 1966088 | tf_op jit(solution)/shard_map/ppermute | solution.py:26
  100.8 34.6 %collective-permute-start.19 = (bf16[2,256,640]{2,1,0:T(8,128)(2,1)S(1)}, bf16[2,256,640]{2,1,0:T(8,128)(2,1)S(1)}, u32[]{:S(2)}, u32[]{:S(2)}) collective-permute-start(bf16[2,256,640]{2,1,0:T(8,128)(2,1)S(1)} %get-tuple-element.71), channel_id=1, source_target_pairs={{0,3},{1,2},{2,1},{3,0},{4,7},{5,6},{6,5},{7,4},{8,11},{9,10},{10,... | collective-permute-start | bytes 1966088 | tf_op jit(solution)/shard_map/ppermute | solution.py:634
  103.3 32.0 %collective-permute-start.18 = (bf16[2,256,640]{2,1,0:T(8,128)(2,1)S(1)}, bf16[2,256,640]{2,1,0:T(8,128)(2,1)S(1)}, u32[]{:S(2)}, u32[]{:S(2)}) collective-permute-start(bf16[2,256,640]{2,1,0:T(8,128)(2,1)S(1)} %get-tuple-element.69), channel_id=1, source_target_pairs={{0,2},{1,3},{2,0},{3,1},{4,6},{5,7},{6,4},{7,5},{8,10},{9,11},{10,... | collective-permute-start | bytes 1966088 | tf_op jit(solution)/shard_map/ppermute | solution.py:634
  103.7 11.3 %copy-start.3 = (bf16[2,256,1024]{2,1,0:T(8,128)(2,1)S(1)}, bf16[2,256,1024]{2,1,0:T(8,128)(2,1)}, u32[]{:S(2)}) copy-start(bf16[2,256,1024]{2,1,0:T(8,128)(2,1)} %copy-done.2) | copy-start | bytes 3145732
  103.7 31.6 %collective-permute-start.17 = (bf16[2,256,640]{2,1,0:T(8,128)(2,1)S(1)}, bf16[2,256,640]{2,1,0:T(8,128)(2,1)S(1)}, u32[]{:S(2)}, u32[]{:S(2)}) collective-permute-start(bf16[2,256,640]{2,1,0:T(8,128)(2,1)S(1)} %get-tuple-element.67), channel_id=1, source_target_pairs={{0,1},{1,0},{2,3},{3,2},{4,5},{5,4},{6,7},{7,6},{8,9},{9,8},{10,11... | collective-permute-start | bytes 1966088 | tf_op jit(solution)/shard_map/ppermute | solution.py:634
  110.1 9.1 %copy-start.8 = (f32[2,128,1024]{2,1,0:T(8,128)S(1)}, f32[2,128,1024]{2,1,0:T(8,128)}, u32[]{:S(2)}) copy-start(f32[2,128,1024]{2,1,0:T(8,128)} %copy-done.7) | copy-start | bytes 3145732
  120.7 10.4 %collective-permute-start.16 = (bf16[2,176,384]{2,1,0:T(8,128)(2,1)S(1)}, bf16[2,176,384]{2,1,0:T(8,128)(2,1)S(1)}, u32[]{:S(2)}, u32[]{:S(2)}) collective-permute-start(bf16[2,176,384]{2,1,0:T(8,128)(2,1)S(1)} %get-tuple-element.61), channel_id=1, source_target_pairs={{4,0},{8,4},{12,8},{5,1},{9,5},{13,9},{6,2},{10,6},{14,10},{7,3},{... | collective-permute-start | bytes 811016 | tf_op jit(solution)/shard_map/ppermute | solution.py:26
  137.9 12.9 %collective-permute-start.20 = (bf16[2,176,640]{2,1,0:T(8,128)(2,1)S(1)}, bf16[2,176,640]{2,1,0:T(8,128)(2,1)S(1)}, u32[]{:S(2)}, u32[]{:S(2)}) collective-permute-start(bf16[2,176,640]{2,1,0:T(8,128)(2,1)S(1)} %get-tuple-element.74), channel_id=1, source_target_pairs={{4,0},{8,4},{12,8},{5,1},{9,5},{13,9},{6,2},{10,6},{14,10},{7,3},{... | collective-permute-start | bytes 1351688 | tf_op jit(solution)/shard_map/ppermute | solution.py:26
  139.2 22.8 %collective-permute-start.12 = (bf16[2,128,1024]{2,1,0:T(8,128)(2,1)S(1)}, bf16[2,128,1024]{2,1,0:T(8,128)(2,1)S(1)}, u32[]{:S(2)}, u32[]{:S(2)}) collective-permute-start(bf16[2,128,1024]{2,1,0:T(8,128)(2,1)S(1)} %get-tuple-element.55.refs_8_), channel_id=1, source_target_pairs={{0,1},{1,0},{2,3},{3,2},{4,5},{5,4},{6,7},{7,6},{8,9},{9,8},{10,11... | collective-permute-start | bytes 1572872 | tf_op jit(solution)/shard_map/ppermute | solution.py:634
  140.6 22.6 %collective-permute-start.13 = (bf16[2,128,1024]{2,1,0:T(8,128)(2,1)S(1)}, bf16[2,128,1024]{2,1,0:T(8,128)(2,1)S(1)}, u32[]{:S(2)}, u32[]{:S(2)}) collective-permute-start(bf16[2,128,1024]{2,1,0:T(8,128)(2,1)S(1)} %get-tuple-element.55.refs_8_), channel_id=1, source_target_pairs={{0,2},{1,3},{2,0},{3,1},{4,6},{5,7},{6,4},{7,5},{8,10},{9,11},{10,... | collective-permute-start | bytes 1572872 | tf_op jit(solution)/shard_map/ppermute | solution.py:634
  142.3 21.9 %collective-permute-start.14 = (bf16[2,128,1024]{2,1,0:T(8,128)(2,1)S(1)}, bf16[2,128,1024]{2,1,0:T(8,128)(2,1)S(1)}, u32[]{:S(2)}, u32[]{:S(2)}) collective-permute-start(bf16[2,128,1024]{2,1,0:T(8,128)(2,1)S(1)} %get-tuple-element.55.refs_8_), channel_id=1, source_target_pairs={{0,3},{1,2},{2,1},{3,0},{4,7},{5,6},{6,5},{7,4},{8,11},{9,10},{10,... | collective-permute-start | bytes 1572872 | tf_op jit(solution)/shard_map/ppermute | solution.py:634
  157.9 1.4 collective-permute-start.21
  159.3 10.6 %collective-permute-start.22 = (f32[8,24,128]{2,1,0:T(8,128)S(1)}, f32[8,24,128]{2,1,0:T(8,128)S(1)}, u32[]{:S(2)}, u32[]{:S(2)}) collective-permute-start(f32[8,24,128]{2,1,0:T(8,128)S(1)} %add.21), channel_id=1, source_target_pairs={{0,8},{4,12},{8,0},{12,4},{16,24},{20,28},{24,16},{28,20},{1,9},{5... | collective-permute-start | bytes 294920 | tf_op jit(solution)/shard_map/ppermute | solution.py:621
  169.9 4.8 %collective-permute-start.23 = (f32[8,24,128]{2,1,0:T(8,128)S(1)}, f32[8,24,128]{2,1,0:T(8,128)S(1)}, u32[]{:S(2)}, u32[]{:S(2)}) collective-permute-start(f32[8,24,128]{2,1,0:T(8,128)S(1)} %add.22), channel_id=1, source_target_pairs={{0,4},{4,0},{8,12},{12,8},{16,20},{20,16},{24,28},{28,24},{1,5},{5... | collective-permute-start | bytes 294920 | tf_op jit(solution)/shard_map/ppermute | solution.py:621
Sparse Core Ops, SparseCore 0:
  9.6 56.4 all-gather.1

commit v4 on v3

--- a/solution.py
+++ b/solution.py
@@ -645,10 +645,11 @@
         half = (stop - start) // cores
         return lax.dynamic_slice_in_dim(out_w, start + core * half, half, axis=0)
 
-    first = lax.all_gather(own_half(0, cut), ("ctx", "dp"), axis=0, tiled=True)
-    weights = [Gathered(first, members, 0)]
     if ring:
-        near = [around(own_half(cut, depth))]
+        early, near = [around(own_half(0, cut))], [around(own_half(cut, depth))]
+    else:
+        whole = lax.all_gather(own_half(0, depth), ("ctx", "dp"), axis=0, tiled=True)
+        weights = [Gathered(whole, members, 0)]
 
     x = jnp.transpose(projected, (2, 0, 1, 3))
     filters = medium_h.astype(F32)
@@ -660,9 +661,12 @@
     mixed_high, gated_high = mix_high(causal, product, x, short_w, taps, group_size)
     high = [gated_high] + [to(gated_high, k) for k in partners[1:]]
     if ring:
+        early.append(around(after(early[-1], mixed_high)))
         near.append(around(after(near[-1], mixed_high)))
         for _ in range(length - 3):
+            early.append(around(early[-1]))
             near.append(around(after(near[-1], *high[1:])))
+        weights = [Passed(out_w, early, [swap(block) for block in early], 0)]
 
     def send_parts(piece, ranges, ready, before):
         own, parts = grad_parts(pos, after(grad_out, *ready), piece, members, ranges)

time: 183 us -> 172 us (0.940)
  between operations: 14.4 us -> 1.02 us
  starting transfers between devices: 38.2 us -> 33.4 us
  waiting for transfers between devices: 56.2 us -> 59.8 us
  Pallas kernels: 54.7 us -> 56.8 us
    ppermute x3 -> x6, starting transfers between devices: 11.2 us -> 6.25 us  [shards(): lax.ppermute(block, 'ctx', [(i, (i + 1) % length) for i in range(length)])]
    ppermute x3 -> x6, waiting for transfers between devices: 21.5 us -> 25.4 us  [shards(): lax.ppermute(block, 'ctx', [(i, (i + 1) % length) for i in range(length)])]
    unnamed x45 -> x49, local copies, waits for them, and re-layouts: 13.4 us -> 13.9 us
  transfers between devices with their start and end apart: 25 -> 30, of which waited for: 14 -> 16; matrix products, arithmetic and copies ran while one was open for 4% -> 4% of each run, Pallas kernels for 29% -> 32%
where the time goes in v4:
time: 172 us
  waiting for transfers between devices  59.8 us (35%)
  Pallas kernels  56.8 us (33%)
  starting transfers between devices  33.4 us (19%)
  local copies, waits for them, and re-layouts  19.2 us (11%)
    ppermute x6, waiting for transfers between devices, shards(): lax.ppermute(block, 'ctx', [(i, (i + 1) % length) for i in range(length)])  25.4 us
    ppermute x12, waiting for transfers between devices, shards(): lax.ppermute(block, 'grp', [(i, i ^ k) for i in partners])  16.9 us
    ppermute x12, starting transfers between devices, shards(): lax.ppermute(block, 'grp', [(i, i ^ k) for i in partners])  16.6 us
    ppermute x3, waiting for transfers between devices, shift(): return lax.ppermute(block, axis, route)  14.4 us
    unnamed x49, local copies, waits for them, and re-layouts  13.9 us
    pallas_call x2, Pallas kernels, block_output(): pl.pallas_call(functools.partial(out_kernel, weights, steps), grid=(1,),...  12.6 us
    pallas_call x2, Pallas kernels, grad_parts(): pl.pallas_call(functools.partial(grad_kernel, weights, steps, ranges), in...  11.9 us
    pallas_call x2, Pallas kernels, input_grads(): pl.pallas_call(functools.partial(input_grad_kernel, group_size, len(mix_g...  11.3 us
  transfers between devices with their start and end apart: 30, of which 16 were waited for; matrix products, arithmetic and copies ran while one was open for 4% of the time, Pallas kernels for 32%

profile of v4, /device:TPU:0, one launch (start us, length us, event | category | flops | bytes accessed | tf_op | source)
XLA Modules:
  0.0 171.6 jit_solution(18154124446402442086)
XLA Ops:
  0.6 1.8 %constant_dynamic-slice_fusion.1 = bf16[192,1024]{1,0:T(8,128)(2,1)} fusion(bf16[1024,1024]{1,0:T(8,128)(2,1)} %refs_7_.3, s32[]{:T(128)S(6)} %select_n.6), kind=kLoop, calls=%fused_computation.11 | loop fusion | bytes 786436 | tf_op jit(solution)/shard_map/dynamic_slice | solution.py:646
  2.4 3.0 %collective-permute-start = (bf16[192,1024]{1,0:T(8,128)(2,1)}, bf16[192,1024]{1,0:T(8,128)(2,1)S(1)}, u32[]{:S(2)}, u32[]{:S(2)}) collective-permute-start(bf16[192,1024]{1,0:T(8,128)(2,1)} %constant_dynamic-slice_fusion.1), channel_id=1, source_target_pairs={{0,4},{4,8},{8,12},{12,0},{1,5},{5,9},{9,13},{13,1},{2,6},{6,10},{... | collective-permute-start | bytes 1179656 | tf_op jit(solution)/shard_map/ppermute | solution.py:635
  5.4 2.0 %constant_dynamic-slice_fusion = bf16[320,1024]{1,0:T(8,128)(2,1)} fusion(bf16[1024,1024]{1,0:T(8,128)(2,1)} %refs_7_.3, s32[]{:T(128)S(6)} %select_n.7), kind=kLoop, calls=%fused_computation.10 | loop fusion | bytes 1310724 | tf_op jit(solution)/shard_map/dynamic_slice | solution.py:646
  7.4 1.6 collective-permute-start.6
  9.0 2.2 %copy.16 = bf16[2,256,3,1024]{3,1,0,2:T(8,128)(2,1)S(1)} copy(bf16[2,256,3,1024]{3,1,2,0:T(8,128)(2,1)} %param.5) | data formatting | bytes 6291456 | tf_op args[0]
  12.8 2.7 %products.1 = (bf16[2,256,1024]{2,1,0:T(8,128)(2,1)S(1)}, bf16[2,160,1024]{2,1,0:T(8,128)(2,1)S(1)}) custom-call(bf16[3,2,256,1024]{3,2,1,0:T(8,128)(2,1)S(1)} %bitcast.15, f32[3,3,1024]{2,1,0:T(4,128)S(1)} %copy-done.7), custom_call_target="tpu_custom_call" | custom-call | tf_op jit(solution)/shard_map/products/pallas_call | solution.py:81
  16.5 3.8 %mix_high.1 = (f32[2,128,1024]{2,1,0:T(8,128)S(1)}, bf16[2,128,1024]{2,1,0:T(8,128)(2,1)S(1)}) custom-call(f32[64,256]{1,0:T(8,128)S(1)} %maximum_maximum_fusion.line_ref, bf16[2,256,1024]{2,1,0:T(8,128)(2,1)S(1)} %get-tuple-element.42.low_ref.high_ref.product_ref.refs_1_, bf16[2,256,1024]{2,1,0:T(8,128)(2,1)S(1)} %get-tuple-element.42.low_ref.high_ref.product_ref.refs_1_, ...), custom_call_target="tpu_custom_call" | custom-call | tf_op jit(solution)/shard_map/mix_high/pallas_call | solution.py:126
  22.3 1.6 collective-permute-start.1
  23.9 2.4 %collective-permute-start.10 = (bf16[2,128,1024]{2,1,0:T(8,128)(2,1)S(1)}, bf16[2,128,1024]{2,1,0:T(8,128)(2,1)S(1)}, u32[]{:S(2)}, u32[]{:S(2)}) collective-permute-start(bf16[2,128,1024]{2,1,0:T(8,128)(2,1)S(1)} %get-tuple-element.46.refs_14_), channel_id=1, source_target_pairs={{0,3},{1,2},{2,1},{3,0},{4,7},{5,6},{6,5},{7,4},{8,11},{9,10},{10,... | collective-permute-start | bytes 1572872 | tf_op jit(solution)/shard_map/ppermute | solution.py:634
  26.9 4.9 %collective-permute-done.6.refs_1_.refs_8_ = bf16[320,1024]{1,0:T(8,128)(2,1)} collective-permute-done((bf16[320,1024]{1,0:T(8,128)(2,1)}, bf16[320,1024]{1,0:T(8,128)(2,1)}, u32[]{:S(2)}, u32[]{:S(2)}) %collective-permute-start.6) | collective-permute-done | bytes 655392 | tf_op jit(solution)/shard_map/ppermute | solution.py:635
  31.8 8.4 %collective-permute-done.1.refs_2_ = bf16[192,1024]{1,0:T(8,128)(2,1)} collective-permute-done((bf16[192,1024]{1,0:T(8,128)(2,1)S(1)}, bf16[192,1024]{1,0:T(8,128)(2,1)}, u32[]{:S(2)}, u32[]{:S(2)}) %collective-permute-start.1) | collective-permute-done | bytes 393248 | tf_op jit(solution)/shard_map/ppermute | solution.py:635
  40.2 1.7 %collective-permute-start.9 = (bf16[2,128,1024]{2,1,0:T(8,128)(2,1)S(1)}, bf16[2,128,1024]{2,1,0:T(8,128)(2,1)S(1)}, u32[]{:S(2)}, u32[]{:S(2)}) collective-permute-start(bf16[2,128,1024]{2,1,0:T(8,128)(2,1)S(1)} %get-tuple-element.46.refs_14_), channel_id=1, source_target_pairs={{0,2},{1,3},{2,0},{3,1},{4,6},{5,7},{6,4},{7,5},{8,10},{9,11},{10,... | collective-permute-start | bytes 1572872 | tf_op jit(solution)/shard_map/ppermute | solution.py:634
  43.6 5.3 %collective-permute-done.8.refs_15_ = bf16[2,128,1024]{2,1,0:T(8,128)(2,1)S(1)} collective-permute-done((bf16[2,128,1024]{2,1,0:T(8,128)(2,1)S(1)}, bf16[2,128,1024]{2,1,0:T(8,128)(2,1)S(1)}, u32[]{:S(2)}, u32[]{:S(2)}) %collective-permute-start.8) | collective-permute-done | bytes 524320 | tf_op jit(solution)/shard_map/ppermute | solution.py:634
  49.7 12.1 %collective-permute-done.2.refs_3_ = bf16[192,1024]{1,0:T(8,128)(2,1)} collective-permute-done((bf16[192,1024]{1,0:T(8,128)(2,1)}, bf16[192,1024]{1,0:T(8,128)(2,1)}, u32[]{:S(2)}, u32[]{:S(2)}) %collective-permute-start.2) | collective-permute-done | bytes 393248 | tf_op jit(solution)/shard_map/ppermute | solution.py:635
  62.7 1.2 collective-permute-done.5.refs_6_
  63.9 1.6 copy-done
  65.5 1.2 copy-done.6
  66.7 4.7 %grad_parts.2 = (f32[2,256,384]{2,1,0:T(8,128)S(1)}, bf16[2,256,384]{2,1,0:T(8,128)(2,1)S(1)}, bf16[2,256,384]{2,1,0:T(8,128)(2,1)S(1)}, bf16[2,256,384]{2,1,0:T(8,128)(2,1)S(1)}) custom-call(s32[3]{0:T(128)S(1)} %pad_add_fusion.pos_ref, bf16[512,1024]{1,0:T(8,128)(2,1)S(1)} %bitcast.22, bf16[1024,1024]{1,0:T(8,128)(2,1)S(1)} %copy-done, ...), custom_call_target="tpu_custom_call" | custom-call | tf_op jit(solution)/shard_map/grad_parts/pallas_call | solution.py:295
  71.4 1.3 collective-permute-start.12
  72.7 1.8 %collective-permute-start.13 = (bf16[2,256,384]{2,1,0:T(8,128)(2,1)S(1)}, bf16[2,256,384]{2,1,0:T(8,128)(2,1)S(1)}, u32[]{:S(2)}, u32[]{:S(2)}) collective-permute-start(bf16[2,256,384]{2,1,0:T(8,128)(2,1)S(1)} %get-tuple-element.50), channel_id=1, source_target_pairs={{0,2},{1,3},{2,0},{3,1},{4,6},{5,7},{6,4},{7,5},{8,10},{9,11},{10,... | collective-permute-start | bytes 1179656 | tf_op jit(solution)/shard_map/ppermute | solution.py:634
  75.0 7.6 %collective-permute-done.12.refs_1_ = bf16[2,256,384]{2,1,0:T(8,128)(2,1)S(1)} collective-permute-done((bf16[2,256,384]{2,1,0:T(8,128)(2,1)S(1)}, bf16[2,256,384]{2,1,0:T(8,128)(2,1)S(1)}, u32[]{:S(2)}, u32[]{:S(2)}) %collective-permute-start.12) | collective-permute-done | bytes 393248 | tf_op jit(solution)/shard_map/ppermute | solution.py:634
  83.7 1.8 %collective-permute-start.21 = (bf16[2,256,384]{2,1,0:T(8,128)(2,1)S(1)}, bf16[2,256,384]{2,1,0:T(8,128)(2,1)S(1)}, u32[]{:S(2)}, u32[]{:S(2)}) collective-permute-start(bf16[2,256,384]{2,1,0:T(8,128)(2,1)S(1)} %get-tuple-element.59), channel_id=1, source_target_pairs={{0,3},{1,2},{2,1},{3,0},{4,7},{5,6},{6,5},{7,4},{8,11},{9,10},{10,... | collective-permute-start | bytes 1179656 | tf_op jit(solution)/shard_map/ppermute | solution.py:634
  86.0 7.2 %grad_parts.3 = (f32[2,256,640]{2,1,0:T(8,128)S(1)}, bf16[2,256,640]{2,1,0:T(8,128)(2,1)S(1)}, bf16[2,256,640]{2,1,0:T(8,128)(2,1)S(1)}, bf16[2,256,640]{2,1,0:T(8,128)(2,1)S(1)}) custom-call(s32[3]{0:T(128)S(1)} %pad_add_fusion.pos_ref, bf16[512,1024]{1,0:T(8,128)(2,1)S(1)} %bitcast.23, bf16[1024,1024]{1,0:T(8,128)(2,1)S(1)} %copy-done, ...), custom_call_target="tpu_custom_call" | custom-call | tf_op jit(solution)/shard_map/grad_parts/pallas_call | solution.py:295
  93.2 2.2 %collective-permute-start.17 = (bf16[2,160,1024]{2,1,0:T(8,128)(2,1)S(1)}, bf16[2,160,1024]{2,1,0:T(8,128)(2,1)S(1)}, u32[]{:S(2)}, u32[]{:S(2)}) collective-permute-start(bf16[2,160,1024]{2,1,0:T(8,128)(2,1)S(1)} %copy-done.20), channel_id=1, source_target_pairs={{0,4},{4,8},{8,12},{1,5},{5,9},{9,13},{2,6},{6,10},{10,14},{3,7},{... | collective-permute-start | bytes 1966088 | tf_op jit(solution)/shard_map/ppermute | solution.py:26
  96.1 1.8 %collective-permute-start.25 = (bf16[2,256,640]{2,1,0:T(8,128)(2,1)S(1)}, bf16[2,256,640]{2,1,0:T(8,128)(2,1)S(1)}, u32[]{:S(2)}, u32[]{:S(2)}) collective-permute-start(bf16[2,256,640]{2,1,0:T(8,128)(2,1)S(1)} %get-tuple-element.73), channel_id=1, source_target_pairs={{0,3},{1,2},{2,1},{3,0},{4,7},{5,6},{6,5},{7,4},{8,11},{9,10},{10,... | collective-permute-start | bytes 1966088 | tf_op jit(solution)/shard_map/ppermute | solution.py:634
  98.3 1.3 collective-permute-start.23
  99.6 6.3 %block_output.2.refs_18_ = bf16[2,256,1024]{2,1,0:T(8,128)(2,1)} custom-call(s32[3]{0:T(128)S(1)} %pad_add_fusion.pos_ref, bf16[1024,1024]{1,0:T(8,128)(2,1)S(1)} %copy-done.1, bf16[192,1024]{1,0:T(8,128)(2,1)S(1)} %collective-permute-done.refs_1_, bf16[192,1024]{1,0:T(8,128)(2,1)} %collective-permute-done.1.refs_2_, ...), custom_call_target="tpu_custom_call" | custom-call | tf_op jit(solution)/shard_map/block_output/pallas_call | solution.py:340
  106.0 3.7 %collective-permute-done.17.front_ref.refs_7_.refs_3_.refs_5_ = bf16[2,160,1024]{2,1,0:T(8,128)(2,1)S(1)} collective-permute-done((bf16[2,160,1024]{2,1,0:T(8,128)(2,1)S(1)}, bf16[2,160,1024]{2,1,0:T(8,128)(2,1)S(1)}, u32[]{:S(2)}, u32[]{:S(2)}) %collective-permute-start.17) | collective-permute-done | bytes 655392 | tf_op jit(solution)/shard_map/ppermute | solution.py:26
  109.6 4.1 %mix_low.1 = (f32[2,128,1024]{2,1,0:T(8,128)S(1)}, bf16[2,128,1024]{2,1,0:T(8,128)(2,1)S(1)}, bf16[2,16,1024]{2,1,0:T(8,128)(2,1)S(1)}) custom-call(f32[64,256]{1,0:T(8,128)S(1)} %copy-done.10, bf16[2,160,1024]{2,1,0:T(8,128)(2,1)S(1)} %collective-permute-done.17.front_ref.refs_7_.refs_3_.refs_5_, bf16[2,256,1024]{2,1,0:T(8,128)(2,1)S(1)} %copy-done.3, ...), custom_call_target="tpu_custom_call" | custom-call | tf_op jit(solution)/shard_map/mix_low/pallas_call | solution.py:189
  113.8 1.5 mix_grads.2
  115.3 1.3 collective-permute-start.22
  116.6 2.3 %filter_sums.2.refs_7_ = f32[24,128]{1,0:T(8,128)S(1)} custom-call(bf16[2,256,384]{2,1,0:T(8,128)(2,1)S(1)} %get-tuple-element.61.refs_0_, bf16[2,256,1024]{2,1,0:T(8,128)(2,1)S(1)} %copy-done.3, bf16[2,16,1024]{2,1,0:T(8,128)(2,1)S(1)} %get-tuple-element.65.refs_2_, bf16[2,160,1024]{2,1,0:T(8,128)(2,1)S(1)} %collective-permute-done.17.front_ref.refs_7_.refs_3_.refs_5_), custom_call_target="tpu_custom_call" | custom-call | tf_op jit(solution)/shard_map/filter_sums/pallas_call | solution.py:467
  119.0 6.7 %collective-permute-done.22.refs_3_ = bf16[2,176,384]{2,1,0:T(8,128)(2,1)S(1)} collective-permute-done((bf16[2,176,384]{2,1,0:T(8,128)(2,1)S(1)}, bf16[2,176,384]{2,1,0:T(8,128)(2,1)S(1)}, u32[]{:S(2)}, u32[]{:S(2)}) %collective-permute-start.22) | collective-permute-done | bytes 270368 | tf_op jit(solution)/shard_map/ppermute | solution.py:26
  125.7 4.2 %input_grads.2 = (bf16[3,2,256,384]{3,2,1,0:T(8,128)(2,1)S(1)}, f32[3,24,128]{2,1,0:T(8,128)S(1)}) custom-call(bf16[2,256,384]{2,1,0:T(8,128)(2,1)S(1)} %get-tuple-element.61.refs_0_, bf16[2,256,384]{2,1,0:T(8,128)(2,1)S(1)} %get-tuple-element.62.refs_1_, f32[64,256]{1,0:T(8,128)S(1)} %concatenate.13.refs_2_, ...), custom_call_target="tpu_custom_call" | custom-call | tf_op jit(solution)/shard_map/input_grads/pallas_call | solution.py:577
  129.9 2.6 %mix_grads.3 = (bf16[2,256,640]{2,1,0:T(8,128)(2,1)S(1)}, bf16[2,256,640]{2,1,0:T(8,128)(2,1)S(1)}, bf16[2,176,640]{2,1,0:T(8,128)(2,1)S(1)}) custom-call(f32[2,256,640]{2,1,0:T(8,128)S(1)} %get-tuple-element.67.refs_0_, bf16[2,256,640]{2,1,0:T(8,128)(2,1)S(1)} %collective-permute-done.23.refs_1_, bf16[2,256,640]{2,1,0:T(8,128)(2,1)S(1)} %collective-permute-done.24.refs_2_, ...), custom_call_target="tpu_custom_call" | custom-call | tf_op jit(solution)/shard_map/mix_grads/pallas_call | solution.py:391
  132.5 1.3 collective-permute-start.26
  133.8 1.2 collective-permute-start.18
  135.0 1.1 collective-permute-start.19
  136.1 1.2 collective-permute-start.20
  137.4 3.9 %filter_sums.3.refs_7_ = f32[40,128]{1,0:T(8,128)S(1)} custom-call(bf16[2,256,640]{2,1,0:T(8,128)(2,1)S(1)} %get-tuple-element.74.refs_0_, bf16[2,256,1024]{2,1,0:T(8,128)(2,1)S(1)} %copy-done.3, bf16[2,16,1024]{2,1,0:T(8,128)(2,1)S(1)} %get-tuple-element.65.refs_2_, bf16[2,160,1024]{2,1,0:T(8,128)(2,1)S(1)} %collective-permute-done.17.front_ref.refs_7_.refs_3_.refs_5_), custom_call_target="tpu_custom_call" | custom-call | tf_op jit(solution)/shard_map/filter_sums/pallas_call | solution.py:467
  141.3 4.0 %collective-permute-done.26.refs_3_ = bf16[2,176,640]{2,1,0:T(8,128)(2,1)S(1)} collective-permute-done((bf16[2,176,640]{2,1,0:T(8,128)(2,1)S(1)}, bf16[2,176,640]{2,1,0:T(8,128)(2,1)S(1)}, u32[]{:S(2)}, u32[]{:S(2)}) %collective-permute-start.26) | collective-permute-done | bytes 450592 | tf_op jit(solution)/shard_map/ppermute | solution.py:26
  145.3 7.0 %input_grads.3 = (bf16[3,2,256,640]{3,2,1,0:T(8,128)(2,1)S(1)}, f32[5,24,128]{2,1,0:T(8,128)S(1)}) custom-call(bf16[2,256,640]{2,1,0:T(8,128)(2,1)S(1)} %get-tuple-element.74.refs_0_, bf16[2,256,640]{2,1,0:T(8,128)(2,1)S(1)} %get-tuple-element.75.refs_1_, f32[64,256]{1,0:T(8,128)S(1)} %concatenate.13.refs_2_, ...), custom_call_target="tpu_custom_call" | custom-call | tf_op jit(solution)/shard_map/input_grads/pallas_call | solution.py:577
  152.4 1.3 collective-permute-done.27
  153.8 2.7 %collective-permute-start.28 = (f32[8,24,128]{2,1,0:T(8,128)S(1)}, f32[8,24,128]{2,1,0:T(8,128)S(1)}, u32[]{:S(2)}, u32[]{:S(2)}) collective-permute-start(f32[8,24,128]{2,1,0:T(8,128)S(1)} %add.21), channel_id=1, source_target_pairs={{0,8},{4,12},{8,0},{12,4},{16,24},{20,28},{24,16},{28,20},{1,9},{5... | collective-permute-start | bytes 294920 | tf_op jit(solution)/shard_map/ppermute | solution.py:621
  157.1 1.6 collective-permute-done.20.refs_17_
  158.7 6.3 %block_output.3 = bf16[2,256,1024]{2,1,0:T(8,128)(2,1)} custom-call(s32[3]{0:T(128)S(1)} %pad_add_fusion.pos_ref, bf16[1024,1024]{1,0:T(8,128)(2,1)S(1)} %copy-done.1, bf16[192,1024]{1,0:T(8,128)(2,1)S(1)} %collective-permute-done.refs_1_, bf16[192,1024]{1,0:T(8,128)(2,1)} %collective-permute-done.1.refs_2_, ...), custom_call_target="tpu_custom_call", output_to_operand_aliasing={{}: (19, {})} | custom-call | tf_op jit(solution)/shard_map/block_output/pallas_call | solution.py:340
  165.1 2.5 %collective-permute-start.29 = (f32[8,24,128]{2,1,0:T(8,128)S(1)}, f32[8,24,128]{2,1,0:T(8,128)S(1)}, u32[]{:S(2)}, u32[]{:S(2)}) collective-permute-start(f32[8,24,128]{2,1,0:T(8,128)S(1)} %add.22), channel_id=1, source_target_pairs={{0,4},{4,0},{8,12},{12,8},{16,20},{20,16},{24,28},{28,24},{1,5},{5... | collective-permute-start | bytes 294920 | tf_op jit(solution)/shard_map/ppermute | solution.py:621
  168.0 2.0 %copy.14 = bf16[2,256,3,1024]{3,1,2,0:T(8,128)(2,1)} copy(bf16[2,256,3,1024]{3,1,0,2:T(8,128)(2,1)S(1)} %maximum_bitcast_fusion) | data formatting | bytes 6291456
  (94 shorter events, 14.3 us)
Async XLA Ops:
  2.4 19.9 %collective-permute-start = (bf16[192,1024]{1,0:T(8,128)(2,1)}, bf16[192,1024]{1,0:T(8,128)(2,1)S(1)}, u32[]{:S(2)}, u32[]{:S(2)}) collective-permute-start(bf16[192,1024]{1,0:T(8,128)(2,1)} %constant_dynamic-slice_fusion.1), channel_id=1, source_target_pairs={{0,4},{4,8},{8,12},{12,0},{1,5},{5,9},{9,13},{13,1},{2,6},{6,10},{... | collective-permute-start | bytes 1179656 | tf_op jit(solution)/shard_map/ppermute | solution.py:635
  7.4 3.8 %copy-start.22 = (bf16[64,128]{1,0:T(8,128)(2,1)S(1)}, bf16[64,128]{1,0:T(8,128)(2,1)}, u32[]{:S(2)}) copy-start(bf16[64,128]{1,0:T(8,128)(2,1)} %param.7) | copy-start | bytes 49156
  7.4 24.4 %collective-permute-start.6 = (bf16[320,1024]{1,0:T(8,128)(2,1)}, bf16[320,1024]{1,0:T(8,128)(2,1)}, u32[]{:S(2)}, u32[]{:S(2)}) collective-permute-start(bf16[320,1024]{1,0:T(8,128)(2,1)} %constant_dynamic-slice_fusion), channel_id=1, source_target_pairs={{0,4},{4,8},{8,12},{12,0},{1,5},{5,9},{9,13},{13,1},{2,6},{6,10},{... | collective-permute-start | bytes 1966088 | tf_op jit(solution)/shard_map/ppermute | solution.py:635
  12.8 3.6 %copy-start.21 = (f32[64,128]{1,0:T(8,128)S(1)}, f32[64,128]{1,0:T(8,128)}, u32[]{:S(2)}) copy-start(f32[64,128]{1,0:T(8,128)} %rev.6) | copy-start | bytes 98308
  15.5 0.8 copy-start.19
  16.4 25.5 %copy-start.9 = (f32[64,256]{1,0:T(8,128)}, f32[64,256]{1,0:T(8,128)S(1)}, u32[]{:S(2)}) copy-start(f32[64,256]{1,0:T(8,128)S(1)} %maximum_maximum_fusion.line_ref) | copy-start | bytes 196612
  20.3 1.0 copy-start.2
  21.3 1.0 copy-start.4
  22.3 17.9 %collective-permute-start.1 = (bf16[192,1024]{1,0:T(8,128)(2,1)S(1)}, bf16[192,1024]{1,0:T(8,128)(2,1)}, u32[]{:S(2)}, u32[]{:S(2)}) collective-permute-start(bf16[192,1024]{1,0:T(8,128)(2,1)S(1)} %collective-permute-done.refs_1_), channel_id=1, source_target_pairs={{0,4},{4,8},{8,12},{12,0},{1,5},{5,9},{9,13},{13,1},{2,6},{6,10},{... | collective-permute-start | bytes 1179656 | tf_op jit(solution)/shard_map/ppermute | solution.py:635
  23.9 18.9 %collective-permute-start.10 = (bf16[2,128,1024]{2,1,0:T(8,128)(2,1)S(1)}, bf16[2,128,1024]{2,1,0:T(8,128)(2,1)S(1)}, u32[]{:S(2)}, u32[]{:S(2)}) collective-permute-start(bf16[2,128,1024]{2,1,0:T(8,128)(2,1)S(1)} %get-tuple-element.46.refs_14_), channel_id=1, source_target_pairs={{0,3},{1,2},{2,1},{3,0},{4,7},{5,6},{6,5},{7,4},{8,11},{9,10},{10,... | collective-permute-start | bytes 1572872 | tf_op jit(solution)/shard_map/ppermute | solution.py:634
  26.3 22.6 %collective-permute-start.8 = (bf16[2,128,1024]{2,1,0:T(8,128)(2,1)S(1)}, bf16[2,128,1024]{2,1,0:T(8,128)(2,1)S(1)}, u32[]{:S(2)}, u32[]{:S(2)}) collective-permute-start(bf16[2,128,1024]{2,1,0:T(8,128)(2,1)S(1)} %get-tuple-element.46.refs_14_), channel_id=1, source_target_pairs={{0,1},{1,0},{2,3},{3,2},{4,5},{5,4},{6,7},{7,6},{8,9},{9,8},{10,11... | collective-permute-start | bytes 1572872 | tf_op jit(solution)/shard_map/ppermute | solution.py:634
  31.8 30.9 %collective-permute-start.7 = (bf16[320,1024]{1,0:T(8,128)(2,1)}, bf16[320,1024]{1,0:T(8,128)(2,1)}, u32[]{:S(2)}, u32[]{:S(2)}) collective-permute-start(bf16[320,1024]{1,0:T(8,128)(2,1)} %collective-permute-done.6.refs_1_.refs_8_), channel_id=1, source_target_pairs={{0,4},{4,8},{8,12},{12,0},{1,5},{5,9},{9,13},{13,1},{2,6},{6,10},{... | collective-permute-start | bytes 1966088 | tf_op jit(solution)/shard_map/ppermute | solution.py:635
  40.2 21.6 %collective-permute-start.2 = (bf16[192,1024]{1,0:T(8,128)(2,1)}, bf16[192,1024]{1,0:T(8,128)(2,1)}, u32[]{:S(2)}, u32[]{:S(2)}) collective-permute-start(bf16[192,1024]{1,0:T(8,128)(2,1)} %collective-permute-done.1.refs_2_), channel_id=1, source_target_pairs={{0,4},{4,8},{8,12},{12,0},{1,5},{5,9},{9,13},{13,1},{2,6},{6,10},{... | collective-permute-start | bytes 1179656 | tf_op jit(solution)/shard_map/ppermute | solution.py:635
  40.2 21.6 %collective-permute-start.9 = (bf16[2,128,1024]{2,1,0:T(8,128)(2,1)S(1)}, bf16[2,128,1024]{2,1,0:T(8,128)(2,1)S(1)}, u32[]{:S(2)}, u32[]{:S(2)}) collective-permute-start(bf16[2,128,1024]{2,1,0:T(8,128)(2,1)S(1)} %get-tuple-element.46.refs_14_), channel_id=1, source_target_pairs={{0,2},{1,3},{2,0},{3,1},{4,6},{5,7},{6,4},{7,5},{8,10},{9,11},{10,... | collective-permute-start | bytes 1572872 | tf_op jit(solution)/shard_map/ppermute | solution.py:634
  43.6 19.2 %collective-permute-start.3 = (bf16[192,1024]{1,0:T(8,128)(2,1)S(1)}, bf16[192,1024]{1,0:T(8,128)(2,1)}, u32[]{:S(2)}, u32[]{:S(2)}) collective-permute-start(bf16[192,1024]{1,0:T(8,128)(2,1)S(1)} %collective-permute-done.refs_1_), channel_id=1, source_target_pairs={{0,16},{16,0},{1,17},{17,1},{2,18},{18,2},{3,19},{19,3},{4,20},{20... | collective-permute-start | bytes 1179656 | tf_op jit(solution)/shard_map/ppermute | solution.py:636
  49.7 13.0 %collective-permute-start.4 = (bf16[192,1024]{1,0:T(8,128)(2,1)}, bf16[192,1024]{1,0:T(8,128)(2,1)}, u32[]{:S(2)}, u32[]{:S(2)}) collective-permute-start(bf16[192,1024]{1,0:T(8,128)(2,1)} %collective-permute-done.1.refs_2_), channel_id=1, source_target_pairs={{0,16},{16,0},{1,17},{17,1},{2,18},{18,2},{3,19},{19,3},{4,20},{20... | collective-permute-start | bytes 1179656 | tf_op jit(solution)/shard_map/ppermute | solution.py:636
  61.8 2.1 %collective-permute-start.5 = (bf16[192,1024]{1,0:T(8,128)(2,1)}, bf16[192,1024]{1,0:T(8,128)(2,1)}, u32[]{:S(2)}, u32[]{:S(2)}) collective-permute-start(bf16[192,1024]{1,0:T(8,128)(2,1)} %collective-permute-done.2.refs_3_), channel_id=1, source_target_pairs={{0,16},{16,0},{1,17},{17,1},{2,18},{18,2},{3,19},{19,3},{4,20},{20... | collective-permute-start | bytes 1179656 | tf_op jit(solution)/shard_map/ppermute | solution.py:636
  62.7 21.0 %collective-permute-start.11 = (bf16[320,1024]{1,0:T(8,128)(2,1)}, bf16[320,1024]{1,0:T(8,128)(2,1)}, u32[]{:S(2)}, u32[]{:S(2)}) collective-permute-start(bf16[320,1024]{1,0:T(8,128)(2,1)} %collective-permute-done.7.refs_2_.refs_9_), channel_id=1, source_target_pairs={{0,4},{4,8},{8,12},{12,0},{1,5},{5,9},{9,13},{13,1},{2,6},{6,10},{... | collective-permute-start | bytes 1966088 | tf_op jit(solution)/shard_map/ppermute | solution.py:635
  63.9 1.6 copy-start
  65.5 1.2 copy-start.6
  71.4 11.2 %collective-permute-start.12 = (bf16[2,256,384]{2,1,0:T(8,128)(2,1)S(1)}, bf16[2,256,384]{2,1,0:T(8,128)(2,1)S(1)}, u32[]{:S(2)}, u32[]{:S(2)}) collective-permute-start(bf16[2,256,384]{2,1,0:T(8,128)(2,1)S(1)} %get-tuple-element.49), channel_id=1, source_target_pairs={{0,1},{1,0},{2,3},{3,2},{4,5},{5,4},{6,7},{7,6},{8,9},{9,8},{10,11... | collective-permute-start | bytes 1179656 | tf_op jit(solution)/shard_map/ppermute | solution.py:634
  72.7 10.9 %collective-permute-start.13 = (bf16[2,256,384]{2,1,0:T(8,128)(2,1)S(1)}, bf16[2,256,384]{2,1,0:T(8,128)(2,1)S(1)}, u32[]{:S(2)}, u32[]{:S(2)}) collective-permute-start(bf16[2,256,384]{2,1,0:T(8,128)(2,1)S(1)} %get-tuple-element.50), channel_id=1, source_target_pairs={{0,2},{1,3},{2,0},{3,1},{4,6},{5,7},{6,4},{7,5},{8,10},{9,11},{10,... | collective-permute-start | bytes 1179656 | tf_op jit(solution)/shard_map/ppermute | solution.py:634
  74.5 10.9 %collective-permute-start.14 = (bf16[320,1024]{1,0:T(8,128)(2,1)}, bf16[320,1024]{1,0:T(8,128)(2,1)S(1)}, u32[]{:S(2)}, u32[]{:S(2)}) collective-permute-start(bf16[320,1024]{1,0:T(8,128)(2,1)} %collective-permute-done.6.refs_1_.refs_8_), channel_id=1, source_target_pairs={{0,16},{16,0},{1,17},{17,1},{2,18},{18,2},{3,19},{19,3},{4,20},{20... | collective-permute-start | bytes 1966088 | tf_op jit(solution)/shard_map/ppermute | solution.py:636
  74.5 10.9 %collective-permute-start.15 = (bf16[320,1024]{1,0:T(8,128)(2,1)}, bf16[320,1024]{1,0:T(8,128)(2,1)S(1)}, u32[]{:S(2)}, u32[]{:S(2)}) collective-permute-start(bf16[320,1024]{1,0:T(8,128)(2,1)} %collective-permute-done.7.refs_2_.refs_9_), channel_id=1, source_target_pairs={{0,16},{16,0},{1,17},{17,1},{2,18},{18,2},{3,19},{19,3},{4,20},{20... | collective-permute-start | bytes 1966088 | tf_op jit(solution)/shard_map/ppermute | solution.py:636
  83.7 2.3 %collective-permute-start.16 = (bf16[320,1024]{1,0:T(8,128)(2,1)}, bf16[320,1024]{1,0:T(8,128)(2,1)S(1)}, u32[]{:S(2)}, u32[]{:S(2)}) collective-permute-start(bf16[320,1024]{1,0:T(8,128)(2,1)} %collective-permute-done.11.refs_3_.refs_10_), channel_id=1, source_target_pairs={{0,16},{16,0},{1,17},{17,1},{2,18},{18,2},{3,19},{19,3},{4,20},{20... | collective-permute-start | bytes 1966088 | tf_op jit(solution)/shard_map/ppermute | solution.py:636
  83.7 12.4 %collective-permute-start.21 = (bf16[2,256,384]{2,1,0:T(8,128)(2,1)S(1)}, bf16[2,256,384]{2,1,0:T(8,128)(2,1)S(1)}, u32[]{:S(2)}, u32[]{:S(2)}) collective-permute-start(bf16[2,256,384]{2,1,0:T(8,128)(2,1)S(1)} %get-tuple-element.59), channel_id=1, source_target_pairs={{0,3},{1,2},{2,1},{3,0},{4,7},{5,6},{6,5},{7,4},{8,11},{9,10},{10,... | collective-permute-start | bytes 1179656 | tf_op jit(solution)/shard_map/ppermute | solution.py:634
  86.0 7.2 %copy-start.20 = (bf16[2,160,1024]{2,1,0:T(8,128)(2,1)S(1)}, bf16[2,160,1024]{2,1,0:T(8,128)(2,1)}, u32[]{:S(2)}) copy-start(bf16[2,160,1024]{2,1,0:T(8,128)(2,1)} %copy-done.19) | copy-start | bytes 1966084
  86.0 13.6 %copy-start.1 = (bf16[1024,1024]{1,0:T(8,128)(2,1)S(1)}, bf16[1024,1024]{1,0:T(8,128)(2,1)}, u32[]{:S(2)}) copy-start(bf16[1024,1024]{1,0:T(8,128)(2,1)} %refs_7_.3) | copy-start | bytes 6291460
  86.0 13.6 %copy-start.12 = (bf16[2,128,1024]{2,1,0:T(8,128)(2,1)S(1)}, bf16[2,128,1024]{2,1,0:T(8,128)(2,1)}, u32[]{:S(2)}) copy-start(bf16[2,128,1024]{2,1,0:T(8,128)(2,1)} %copy-done.11) | copy-start | bytes 1572868
  86.0 13.6 %copy-start.14 = (bf16[2,128,1024]{2,1,0:T(8,128)(2,1)S(1)}, bf16[2,128,1024]{2,1,0:T(8,128)(2,1)}, u32[]{:S(2)}) copy-start(bf16[2,128,1024]{2,1,0:T(8,128)(2,1)} %copy-done.13) | copy-start | bytes 1572868
  86.0 13.6 %copy-start.16 = (bf16[2,128,1024]{2,1,0:T(8,128)(2,1)S(1)}, bf16[2,128,1024]{2,1,0:T(8,128)(2,1)}, u32[]{:S(2)}) copy-start(bf16[2,128,1024]{2,1,0:T(8,128)(2,1)} %copy-done.15) | copy-start | bytes 1572868
  86.0 13.6 %copy-start.18 = (bf16[2,128,1024]{2,1,0:T(8,128)(2,1)S(1)}, bf16[2,128,1024]{2,1,0:T(8,128)(2,1)}, u32[]{:S(2)}) copy-start(bf16[2,128,1024]{2,1,0:T(8,128)(2,1)} %copy-done.17) | copy-start | bytes 1572868
  93.2 16.4 %collective-permute-start.17 = (bf16[2,160,1024]{2,1,0:T(8,128)(2,1)S(1)}, bf16[2,160,1024]{2,1,0:T(8,128)(2,1)S(1)}, u32[]{:S(2)}, u32[]{:S(2)}) collective-permute-start(bf16[2,160,1024]{2,1,0:T(8,128)(2,1)S(1)} %copy-done.20), channel_id=1, source_target_pairs={{0,4},{4,8},{8,12},{1,5},{5,9},{9,13},{2,6},{6,10},{10,14},{3,7},{... | collective-permute-start | bytes 1966088 | tf_op jit(solution)/shard_map/ppermute | solution.py:26
  96.1 33.8 %collective-permute-start.25 = (bf16[2,256,640]{2,1,0:T(8,128)(2,1)S(1)}, bf16[2,256,640]{2,1,0:T(8,128)(2,1)S(1)}, u32[]{:S(2)}, u32[]{:S(2)}) collective-permute-start(bf16[2,256,640]{2,1,0:T(8,128)(2,1)S(1)} %get-tuple-element.73), channel_id=1, source_target_pairs={{0,3},{1,2},{2,1},{3,0},{4,7},{5,6},{6,5},{7,4},{8,11},{9,10},{10,... | collective-permute-start | bytes 1966088 | tf_op jit(solution)/shard_map/ppermute | solution.py:634
  97.9 32.0 %collective-permute-start.24 = (bf16[2,256,640]{2,1,0:T(8,128)(2,1)S(1)}, bf16[2,256,640]{2,1,0:T(8,128)(2,1)S(1)}, u32[]{:S(2)}, u32[]{:S(2)}) collective-permute-start(bf16[2,256,640]{2,1,0:T(8,128)(2,1)S(1)} %get-tuple-element.71), channel_id=1, source_target_pairs={{0,2},{1,3},{2,0},{3,1},{4,6},{5,7},{6,4},{7,5},{8,10},{9,11},{10,... | collective-permute-start | bytes 1966088 | tf_op jit(solution)/shard_map/ppermute | solution.py:634
  98.3 11.3 %copy-start.3 = (bf16[2,256,1024]{2,1,0:T(8,128)(2,1)S(1)}, bf16[2,256,1024]{2,1,0:T(8,128)(2,1)}, u32[]{:S(2)}) copy-start(bf16[2,256,1024]{2,1,0:T(8,128)(2,1)} %copy-done.2) | copy-start | bytes 3145732
  98.3 11.3 %copy-start.8 = (f32[3,3,1024]{2,1,0:T(4,128)S(1)}, f32[3,3,1024]{2,1,0:T(4,128)}, u32[]{:S(2)}) copy-start(f32[3,3,1024]{2,1,0:T(4,128)} %refs_6_.3) | copy-start | bytes 110596
  98.3 11.3 %copy-start.10 = (f32[64,256]{1,0:T(8,128)S(1)}, f32[64,256]{1,0:T(8,128)}, u32[]{:S(2)}) copy-start(f32[64,256]{1,0:T(8,128)} %copy-done.9) | copy-start | bytes 196612
  98.3 31.6 %collective-permute-start.23 = (bf16[2,256,640]{2,1,0:T(8,128)(2,1)S(1)}, bf16[2,256,640]{2,1,0:T(8,128)(2,1)S(1)}, u32[]{:S(2)}, u32[]{:S(2)}) collective-permute-start(bf16[2,256,640]{2,1,0:T(8,128)(2,1)S(1)} %get-tuple-element.69), channel_id=1, source_target_pairs={{0,1},{1,0},{2,3},{3,2},{4,5},{5,4},{6,7},{7,6},{8,9},{9,8},{10,11... | collective-permute-start | bytes 1966088 | tf_op jit(solution)/shard_map/ppermute | solution.py:634
  105.9 7.8 %copy-start.5 = (f32[2,128,1024]{2,1,0:T(8,128)S(1)}, f32[2,128,1024]{2,1,0:T(8,128)}, u32[]{:S(2)}) copy-start(f32[2,128,1024]{2,1,0:T(8,128)} %copy-done.4) | copy-start | bytes 3145732
  115.3 10.3 %collective-permute-start.22 = (bf16[2,176,384]{2,1,0:T(8,128)(2,1)S(1)}, bf16[2,176,384]{2,1,0:T(8,128)(2,1)S(1)}, u32[]{:S(2)}, u32[]{:S(2)}) collective-permute-start(bf16[2,176,384]{2,1,0:T(8,128)(2,1)S(1)} %get-tuple-element.63), channel_id=1, source_target_pairs={{4,0},{8,4},{12,8},{5,1},{9,5},{13,9},{6,2},{10,6},{14,10},{7,3},{... | collective-permute-start | bytes 811016 | tf_op jit(solution)/shard_map/ppermute | solution.py:26
  132.5 12.8 %collective-permute-start.26 = (bf16[2,176,640]{2,1,0:T(8,128)(2,1)S(1)}, bf16[2,176,640]{2,1,0:T(8,128)(2,1)S(1)}, u32[]{:S(2)}, u32[]{:S(2)}) collective-permute-start(bf16[2,176,640]{2,1,0:T(8,128)(2,1)S(1)} %get-tuple-element.76), channel_id=1, source_target_pairs={{4,0},{8,4},{12,8},{5,1},{9,5},{13,9},{6,2},{10,6},{14,10},{7,3},{... | collective-permute-start | bytes 1351688 | tf_op jit(solution)/shard_map/ppermute | solution.py:26
  133.8 22.7 %collective-permute-start.18 = (bf16[2,128,1024]{2,1,0:T(8,128)(2,1)S(1)}, bf16[2,128,1024]{2,1,0:T(8,128)(2,1)S(1)}, u32[]{:S(2)}, u32[]{:S(2)}) collective-permute-start(bf16[2,128,1024]{2,1,0:T(8,128)(2,1)S(1)} %get-tuple-element.57.refs_14_), channel_id=1, source_target_pairs={{0,1},{1,0},{2,3},{3,2},{4,5},{5,4},{6,7},{7,6},{8,9},{9,8},{10,11... | collective-permute-start | bytes 1572872 | tf_op jit(solution)/shard_map/ppermute | solution.py:634
  135.0 22.1 %collective-permute-start.19 = (bf16[2,128,1024]{2,1,0:T(8,128)(2,1)S(1)}, bf16[2,128,1024]{2,1,0:T(8,128)(2,1)S(1)}, u32[]{:S(2)}, u32[]{:S(2)}) collective-permute-start(bf16[2,128,1024]{2,1,0:T(8,128)(2,1)S(1)} %get-tuple-element.57.refs_14_), channel_id=1, source_target_pairs={{0,2},{1,3},{2,0},{3,1},{4,6},{5,7},{6,4},{7,5},{8,10},{9,11},{10,... | collective-permute-start | bytes 1572872 | tf_op jit(solution)/shard_map/ppermute | solution.py:634
  136.1 22.6 %collective-permute-start.20 = (bf16[2,128,1024]{2,1,0:T(8,128)(2,1)S(1)}, bf16[2,128,1024]{2,1,0:T(8,128)(2,1)S(1)}, u32[]{:S(2)}, u32[]{:S(2)}) collective-permute-start(bf16[2,128,1024]{2,1,0:T(8,128)(2,1)S(1)} %get-tuple-element.57.refs_14_), channel_id=1, source_target_pairs={{0,3},{1,2},{2,1},{3,0},{4,7},{5,6},{6,5},{7,4},{8,11},{9,10},{10,... | collective-permute-start | bytes 1572872 | tf_op jit(solution)/shard_map/ppermute | solution.py:634
  152.4 1.4 collective-permute-start.27
  153.8 11.3 %collective-permute-start.28 = (f32[8,24,128]{2,1,0:T(8,128)S(1)}, f32[8,24,128]{2,1,0:T(8,128)S(1)}, u32[]{:S(2)}, u32[]{:S(2)}) collective-permute-start(f32[8,24,128]{2,1,0:T(8,128)S(1)} %add.21), channel_id=1, source_target_pairs={{0,8},{4,12},{8,0},{12,4},{16,24},{20,28},{24,16},{28,20},{1,9},{5... | collective-permute-start | bytes 294920 | tf_op jit(solution)/shard_map/ppermute | solution.py:621
  165.1 5.1 %collective-permute-start.29 = (f32[8,24,128]{2,1,0:T(8,128)S(1)}, f32[8,24,128]{2,1,0:T(8,128)S(1)}, u32[]{:S(2)}, u32[]{:S(2)}) collective-permute-start(f32[8,24,128]{2,1,0:T(8,128)S(1)} %add.22), channel_id=1, source_target_pairs={{0,4},{4,0},{8,12},{12,8},{16,20},{20,16},{24,28},{28,24},{1,5},{5... | collective-permute-start | bytes 294920 | tf_op jit(solution)/shard_map/ppermute | solution.py:621
  (5 other events, 4.0 us)

commit v5 on v4

--- a/solution.py
+++ b/solution.py
@@ -685,7 +685,7 @@
         gots.append(got)
 
     block_out = block_output(pos, weights, high, 1, 2, None)
-    front = shift(after(pack, owns[-1]), "ctx", 1)
+    front = shift(after(pack, owns[0]), "ctx", 1)
     front = after(front, block_out)
     mixed_low, gated_low, head = mix_low(causal, front, product, x, short_w, taps, group_size)
     sent = after(gated_low, owns[-1])

time: 172 us -> 170 us (0.988)
    ppermute x3, waiting for transfers between devices: 14.4 us -> 10.7 us  [shift(): return lax.ppermute(block, axis, route)]
    ppermute x12, waiting for transfers between devices: 16.9 us -> 20.1 us  [shards(): lax.ppermute(block, 'grp', [(i, i ^ k) for i in partners])]
  transfers between devices with their start and end apart: 30 -> 30, of which waited for: 16 -> 15; matrix products, arithmetic and copies ran while one was open for 4% -> 4% of each run, Pallas kernels for 32% -> 32%
where the time goes in v5:
time: 170 us
  waiting for transfers between devices  58.7 us (35%)
  Pallas kernels  56.8 us (33%)
  starting transfers between devices  32.6 us (19%)
  local copies, waits for them, and re-layouts  19.2 us (11%)
    ppermute x6, waiting for transfers between devices, shards(): lax.ppermute(block, 'ctx', [(i, (i + 1) % length) for i in range(length)])  25.4 us
    ppermute x12, waiting for transfers between devices, shards(): lax.ppermute(block, 'grp', [(i, i ^ k) for i in partners])  20.1 us
    ppermute x12, starting transfers between devices, shards(): lax.ppermute(block, 'grp', [(i, i ^ k) for i in partners])  16.6 us
    unnamed x49, local copies, waits for them, and re-layouts  13.9 us
    pallas_call x2, Pallas kernels, block_output(): pl.pallas_call(functools.partial(out_kernel, weights, steps), grid=(1,),...  12.6 us
    pallas_call x2, Pallas kernels, grad_parts(): pl.pallas_call(functools.partial(grad_kernel, weights, steps, ranges), in...  11.9 us
    pallas_call x2, Pallas kernels, input_grads(): pl.pallas_call(functools.partial(input_grad_kernel, group_size, len(mix_g...  11.3 us
    ppermute x3, waiting for transfers between devices, shift(): return lax.ppermute(block, axis, route)  10.7 us
  transfers between devices with their start and end apart: 30, of which 15 were waited for; matrix products, arithmetic and copies ran while one was open for 4% of the time, Pallas kernels for 32%

profile of v5, /device:TPU:0, one launch (start us, length us, event | category | flops | bytes accessed | tf_op | source)
XLA Modules:
  0.0 169.7 jit_solution(17320429341995951312)
XLA Ops:
  0.6 1.8 %constant_dynamic-slice_fusion.1 = bf16[192,1024]{1,0:T(8,128)(2,1)} fusion(bf16[1024,1024]{1,0:T(8,128)(2,1)} %refs_7_.3, s32[]{:T(128)S(6)} %select_n.6), kind=kLoop, calls=%fused_computation.11 | loop fusion | bytes 786436 | tf_op jit(solution)/shard_map/dynamic_slice | solution.py:646
  2.4 3.0 %collective-permute-start = (bf16[192,1024]{1,0:T(8,128)(2,1)}, bf16[192,1024]{1,0:T(8,128)(2,1)S(1)}, u32[]{:S(2)}, u32[]{:S(2)}) collective-permute-start(bf16[192,1024]{1,0:T(8,128)(2,1)} %constant_dynamic-slice_fusion.1), channel_id=1, source_target_pairs={{0,4},{4,8},{8,12},{12,0},{1,5},{5,9},{9,13},{13,1},{2,6},{6,10},{... | collective-permute-start | bytes 1179656 | tf_op jit(solution)/shard_map/ppermute | solution.py:635
  5.4 2.0 %constant_dynamic-slice_fusion = bf16[320,1024]{1,0:T(8,128)(2,1)} fusion(bf16[1024,1024]{1,0:T(8,128)(2,1)} %refs_7_.3, s32[]{:T(128)S(6)} %select_n.7), kind=kLoop, calls=%fused_computation.10 | loop fusion | bytes 1310724 | tf_op jit(solution)/shard_map/dynamic_slice | solution.py:646
  7.4 1.6 collective-permute-start.6
  9.0 2.2 %copy.16 = bf16[2,256,3,1024]{3,1,0,2:T(8,128)(2,1)S(1)} copy(bf16[2,256,3,1024]{3,1,2,0:T(8,128)(2,1)} %param.5) | data formatting | bytes 6291456 | tf_op args[0]
  12.8 2.7 %products.1 = (bf16[2,256,1024]{2,1,0:T(8,128)(2,1)S(1)}, bf16[2,160,1024]{2,1,0:T(8,128)(2,1)S(1)}) custom-call(bf16[3,2,256,1024]{3,2,1,0:T(8,128)(2,1)S(1)} %bitcast.15, f32[3,3,1024]{2,1,0:T(4,128)S(1)} %copy-done.7), custom_call_target="tpu_custom_call" | custom-call | tf_op jit(solution)/shard_map/products/pallas_call | solution.py:81
  16.5 3.8 %mix_high.1 = (f32[2,128,1024]{2,1,0:T(8,128)S(1)}, bf16[2,128,1024]{2,1,0:T(8,128)(2,1)S(1)}) custom-call(f32[64,256]{1,0:T(8,128)S(1)} %maximum_maximum_fusion.line_ref, bf16[2,256,1024]{2,1,0:T(8,128)(2,1)S(1)} %get-tuple-element.42.low_ref.high_ref.product_ref.refs_1_, bf16[2,256,1024]{2,1,0:T(8,128)(2,1)S(1)} %get-tuple-element.42.low_ref.high_ref.product_ref.refs_1_, ...), custom_call_target="tpu_custom_call" | custom-call | tf_op jit(solution)/shard_map/mix_high/pallas_call | solution.py:126
  22.3 1.6 collective-permute-start.1
  23.9 2.4 %collective-permute-start.10 = (bf16[2,128,1024]{2,1,0:T(8,128)(2,1)S(1)}, bf16[2,128,1024]{2,1,0:T(8,128)(2,1)S(1)}, u32[]{:S(2)}, u32[]{:S(2)}) collective-permute-start(bf16[2,128,1024]{2,1,0:T(8,128)(2,1)S(1)} %get-tuple-element.46.refs_14_), channel_id=1, source_target_pairs={{0,3},{1,2},{2,1},{3,0},{4,7},{5,6},{6,5},{7,4},{8,11},{9,10},{10,... | collective-permute-start | bytes 1572872 | tf_op jit(solution)/shard_map/ppermute | solution.py:634
  26.9 4.9 %collective-permute-done.6.refs_8_.refs_1_ = bf16[320,1024]{1,0:T(8,128)(2,1)} collective-permute-done((bf16[320,1024]{1,0:T(8,128)(2,1)}, bf16[320,1024]{1,0:T(8,128)(2,1)}, u32[]{:S(2)}, u32[]{:S(2)}) %collective-permute-start.6) | collective-permute-done | bytes 655392 | tf_op jit(solution)/shard_map/ppermute | solution.py:635
  31.8 8.4 %collective-permute-done.1.refs_2_ = bf16[192,1024]{1,0:T(8,128)(2,1)} collective-permute-done((bf16[192,1024]{1,0:T(8,128)(2,1)S(1)}, bf16[192,1024]{1,0:T(8,128)(2,1)}, u32[]{:S(2)}, u32[]{:S(2)}) %collective-permute-start.1) | collective-permute-done | bytes 393248 | tf_op jit(solution)/shard_map/ppermute | solution.py:635
  40.2 1.7 %collective-permute-start.9 = (bf16[2,128,1024]{2,1,0:T(8,128)(2,1)S(1)}, bf16[2,128,1024]{2,1,0:T(8,128)(2,1)S(1)}, u32[]{:S(2)}, u32[]{:S(2)}) collective-permute-start(bf16[2,128,1024]{2,1,0:T(8,128)(2,1)S(1)} %get-tuple-element.46.refs_14_), channel_id=1, source_target_pairs={{0,2},{1,3},{2,0},{3,1},{4,6},{5,7},{6,4},{7,5},{8,10},{9,11},{10,... | collective-permute-start | bytes 1572872 | tf_op jit(solution)/shard_map/ppermute | solution.py:634
  43.6 5.3 %collective-permute-done.8.refs_15_ = bf16[2,128,1024]{2,1,0:T(8,128)(2,1)S(1)} collective-permute-done((bf16[2,128,1024]{2,1,0:T(8,128)(2,1)S(1)}, bf16[2,128,1024]{2,1,0:T(8,128)(2,1)S(1)}, u32[]{:S(2)}, u32[]{:S(2)}) %collective-permute-start.8) | collective-permute-done | bytes 524320 | tf_op jit(solution)/shard_map/ppermute | solution.py:634
  49.7 12.1 %collective-permute-done.2.refs_3_ = bf16[192,1024]{1,0:T(8,128)(2,1)} collective-permute-done((bf16[192,1024]{1,0:T(8,128)(2,1)}, bf16[192,1024]{1,0:T(8,128)(2,1)}, u32[]{:S(2)}, u32[]{:S(2)}) %collective-permute-start.2) | collective-permute-done | bytes 393248 | tf_op jit(solution)/shard_map/ppermute | solution.py:635
  62.7 1.2 collective-permute-done.5.refs_6_
  63.9 1.6 copy-done
  65.5 1.2 copy-done.6
  66.7 4.7 %grad_parts.2 = (f32[2,256,384]{2,1,0:T(8,128)S(1)}, bf16[2,256,384]{2,1,0:T(8,128)(2,1)S(1)}, bf16[2,256,384]{2,1,0:T(8,128)(2,1)S(1)}, bf16[2,256,384]{2,1,0:T(8,128)(2,1)S(1)}) custom-call(s32[3]{0:T(128)S(1)} %pad_add_fusion.pos_ref, bf16[512,1024]{1,0:T(8,128)(2,1)S(1)} %bitcast.22, bf16[1024,1024]{1,0:T(8,128)(2,1)S(1)} %copy-done, ...), custom_call_target="tpu_custom_call" | custom-call | tf_op jit(solution)/shard_map/grad_parts/pallas_call | solution.py:295
  71.5 1.3 collective-permute-start.12
  72.7 1.8 %collective-permute-start.13 = (bf16[2,256,384]{2,1,0:T(8,128)(2,1)S(1)}, bf16[2,256,384]{2,1,0:T(8,128)(2,1)S(1)}, u32[]{:S(2)}, u32[]{:S(2)}) collective-permute-start(bf16[2,256,384]{2,1,0:T(8,128)(2,1)S(1)} %get-tuple-element.50), channel_id=1, source_target_pairs={{0,2},{1,3},{2,0},{3,1},{4,6},{5,7},{6,4},{7,5},{8,10},{9,11},{10,... | collective-permute-start | bytes 1179656 | tf_op jit(solution)/shard_map/ppermute | solution.py:634
  75.0 7.6 %collective-permute-done.12.refs_1_ = bf16[2,256,384]{2,1,0:T(8,128)(2,1)S(1)} collective-permute-done((bf16[2,256,384]{2,1,0:T(8,128)(2,1)S(1)}, bf16[2,256,384]{2,1,0:T(8,128)(2,1)S(1)}, u32[]{:S(2)}, u32[]{:S(2)}) %collective-permute-start.12) | collective-permute-done | bytes 393248 | tf_op jit(solution)/shard_map/ppermute | solution.py:634
  83.7 1.8 %collective-permute-start.21 = (bf16[2,256,384]{2,1,0:T(8,128)(2,1)S(1)}, bf16[2,256,384]{2,1,0:T(8,128)(2,1)S(1)}, u32[]{:S(2)}, u32[]{:S(2)}) collective-permute-start(bf16[2,256,384]{2,1,0:T(8,128)(2,1)S(1)} %get-tuple-element.59), channel_id=1, source_target_pairs={{0,3},{1,2},{2,1},{3,0},{4,7},{5,6},{6,5},{7,4},{8,11},{9,10},{10,... | collective-permute-start | bytes 1179656 | tf_op jit(solution)/shard_map/ppermute | solution.py:634
  85.4 2.1 %collective-permute-start.17 = (bf16[2,160,1024]{2,1,0:T(8,128)(2,1)S(1)}, bf16[2,160,1024]{2,1,0:T(8,128)(2,1)S(1)}, u32[]{:S(2)}, u32[]{:S(2)}) collective-permute-start(bf16[2,160,1024]{2,1,0:T(8,128)(2,1)S(1)} %copy-done.20), channel_id=1, source_target_pairs={{0,4},{4,8},{8,12},{1,5},{5,9},{9,13},{2,6},{6,10},{10,14},{3,7},{... | collective-permute-start | bytes 1966088 | tf_op jit(solution)/shard_map/ppermute | solution.py:26
  87.6 7.2 %grad_parts.3 = (f32[2,256,640]{2,1,0:T(8,128)S(1)}, bf16[2,256,640]{2,1,0:T(8,128)(2,1)S(1)}, bf16[2,256,640]{2,1,0:T(8,128)(2,1)S(1)}, bf16[2,256,640]{2,1,0:T(8,128)(2,1)S(1)}) custom-call(s32[3]{0:T(128)S(1)} %pad_add_fusion.pos_ref, bf16[512,1024]{1,0:T(8,128)(2,1)S(1)} %bitcast.23, bf16[1024,1024]{1,0:T(8,128)(2,1)S(1)} %copy-done, ...), custom_call_target="tpu_custom_call" | custom-call | tf_op jit(solution)/shard_map/grad_parts/pallas_call | solution.py:295
  94.8 1.3 collective-permute-done.21.refs_3_
  96.1 1.8 %collective-permute-start.25 = (bf16[2,256,640]{2,1,0:T(8,128)(2,1)S(1)}, bf16[2,256,640]{2,1,0:T(8,128)(2,1)S(1)}, u32[]{:S(2)}, u32[]{:S(2)}) collective-permute-start(bf16[2,256,640]{2,1,0:T(8,128)(2,1)S(1)} %get-tuple-element.73), channel_id=1, source_target_pairs={{0,3},{1,2},{2,1},{3,0},{4,7},{5,6},{6,5},{7,4},{8,11},{9,10},{10,... | collective-permute-start | bytes 1966088 | tf_op jit(solution)/shard_map/ppermute | solution.py:634
  98.3 1.3 collective-permute-start.23
  99.6 6.3 %block_output.2.refs_18_ = bf16[2,256,1024]{2,1,0:T(8,128)(2,1)} custom-call(s32[3]{0:T(128)S(1)} %pad_add_fusion.pos_ref, bf16[1024,1024]{1,0:T(8,128)(2,1)S(1)} %copy-done.1, bf16[192,1024]{1,0:T(8,128)(2,1)S(1)} %collective-permute-done.refs_1_, bf16[192,1024]{1,0:T(8,128)(2,1)} %collective-permute-done.1.refs_2_, ...), custom_call_target="tpu_custom_call" | custom-call | tf_op jit(solution)/shard_map/block_output/pallas_call | solution.py:340
  106.0 4.1 %mix_low.1 = (f32[2,128,1024]{2,1,0:T(8,128)S(1)}, bf16[2,128,1024]{2,1,0:T(8,128)(2,1)S(1)}, bf16[2,16,1024]{2,1,0:T(8,128)(2,1)S(1)}) custom-call(f32[64,256]{1,0:T(8,128)S(1)} %copy-done.10, bf16[2,160,1024]{2,1,0:T(8,128)(2,1)S(1)} %collective-permute-done.17.front_ref.refs_7_.refs_3_.refs_5_, bf16[2,256,1024]{2,1,0:T(8,128)(2,1)S(1)} %copy-done.3, ...), custom_call_target="tpu_custom_call" | custom-call | tf_op jit(solution)/shard_map/mix_low/pallas_call | solution.py:189
  110.2 1.5 mix_grads.2
  111.7 1.3 collective-permute-start.22
  113.0 2.3 %filter_sums.2.refs_7_ = f32[24,128]{1,0:T(8,128)S(1)} custom-call(bf16[2,256,384]{2,1,0:T(8,128)(2,1)S(1)} %get-tuple-element.61.refs_0_, bf16[2,256,1024]{2,1,0:T(8,128)(2,1)S(1)} %copy-done.3, bf16[2,16,1024]{2,1,0:T(8,128)(2,1)S(1)} %get-tuple-element.65.refs_2_, bf16[2,160,1024]{2,1,0:T(8,128)(2,1)S(1)} %collective-permute-done.17.front_ref.refs_7_.refs_3_.refs_5_), custom_call_target="tpu_custom_call" | custom-call | tf_op jit(solution)/shard_map/filter_sums/pallas_call | solution.py:467
  115.4 5.6 %collective-permute-done.22.refs_3_ = bf16[2,176,384]{2,1,0:T(8,128)(2,1)S(1)} collective-permute-done((bf16[2,176,384]{2,1,0:T(8,128)(2,1)S(1)}, bf16[2,176,384]{2,1,0:T(8,128)(2,1)S(1)}, u32[]{:S(2)}, u32[]{:S(2)}) %collective-permute-start.22) | collective-permute-done | bytes 270368 | tf_op jit(solution)/shard_map/ppermute | solution.py:26
  120.9 4.2 %input_grads.2 = (bf16[3,2,256,384]{3,2,1,0:T(8,128)(2,1)S(1)}, f32[3,24,128]{2,1,0:T(8,128)S(1)}) custom-call(bf16[2,256,384]{2,1,0:T(8,128)(2,1)S(1)} %get-tuple-element.61.refs_0_, bf16[2,256,384]{2,1,0:T(8,128)(2,1)S(1)} %get-tuple-element.62.refs_1_, f32[64,256]{1,0:T(8,128)S(1)} %concatenate.13.refs_2_, ...), custom_call_target="tpu_custom_call" | custom-call | tf_op jit(solution)/shard_map/input_grads/pallas_call | solution.py:577
  125.2 2.2 %collective-permute-done.24.refs_2_ = bf16[2,256,640]{2,1,0:T(8,128)(2,1)S(1)} collective-permute-done((bf16[2,256,640]{2,1,0:T(8,128)(2,1)S(1)}, bf16[2,256,640]{2,1,0:T(8,128)(2,1)S(1)}, u32[]{:S(2)}, u32[]{:S(2)}) %collective-permute-start.24) | collective-permute-done | bytes 655392 | tf_op jit(solution)/shard_map/ppermute | solution.py:634
  127.7 2.6 %mix_grads.3 = (bf16[2,256,640]{2,1,0:T(8,128)(2,1)S(1)}, bf16[2,256,640]{2,1,0:T(8,128)(2,1)S(1)}, bf16[2,176,640]{2,1,0:T(8,128)(2,1)S(1)}) custom-call(f32[2,256,640]{2,1,0:T(8,128)S(1)} %get-tuple-element.67.refs_0_, bf16[2,256,640]{2,1,0:T(8,128)(2,1)S(1)} %collective-permute-done.23.refs_1_, bf16[2,256,640]{2,1,0:T(8,128)(2,1)S(1)} %collective-permute-done.24.refs_2_, ...), custom_call_target="tpu_custom_call" | custom-call | tf_op jit(solution)/shard_map/mix_grads/pallas_call | solution.py:391
  130.3 1.3 collective-permute-start.26
  132.3 1.4 collective-permute-start.19
  133.7 1.5 collective-permute-start.20
  135.2 3.9 %filter_sums.3.refs_7_ = f32[40,128]{1,0:T(8,128)S(1)} custom-call(bf16[2,256,640]{2,1,0:T(8,128)(2,1)S(1)} %get-tuple-element.74.refs_0_, bf16[2,256,1024]{2,1,0:T(8,128)(2,1)S(1)} %copy-done.3, bf16[2,16,1024]{2,1,0:T(8,128)(2,1)S(1)} %get-tuple-element.65.refs_2_, bf16[2,160,1024]{2,1,0:T(8,128)(2,1)S(1)} %collective-permute-done.17.front_ref.refs_7_.refs_3_.refs_5_), custom_call_target="tpu_custom_call" | custom-call | tf_op jit(solution)/shard_map/filter_sums/pallas_call | solution.py:467
  139.1 5.1 %collective-permute-done.26.refs_3_ = bf16[2,176,640]{2,1,0:T(8,128)(2,1)S(1)} collective-permute-done((bf16[2,176,640]{2,1,0:T(8,128)(2,1)S(1)}, bf16[2,176,640]{2,1,0:T(8,128)(2,1)S(1)}, u32[]{:S(2)}, u32[]{:S(2)}) %collective-permute-start.26) | collective-permute-done | bytes 450592 | tf_op jit(solution)/shard_map/ppermute | solution.py:26
  144.1 7.0 %input_grads.3 = (bf16[3,2,256,640]{3,2,1,0:T(8,128)(2,1)S(1)}, f32[5,24,128]{2,1,0:T(8,128)S(1)}) custom-call(bf16[2,256,640]{2,1,0:T(8,128)(2,1)S(1)} %get-tuple-element.74.refs_0_, bf16[2,256,640]{2,1,0:T(8,128)(2,1)S(1)} %get-tuple-element.75.refs_1_, f32[64,256]{1,0:T(8,128)S(1)} %concatenate.13.refs_2_, ...), custom_call_target="tpu_custom_call" | custom-call | tf_op jit(solution)/shard_map/input_grads/pallas_call | solution.py:577
  151.3 1.3 collective-permute-done.27
  152.6 2.0 %collective-permute-start.28 = (f32[8,24,128]{2,1,0:T(8,128)S(1)}, f32[8,24,128]{2,1,0:T(8,128)S(1)}, u32[]{:S(2)}, u32[]{:S(2)}) collective-permute-start(f32[8,24,128]{2,1,0:T(8,128)S(1)} %add.21), channel_id=1, source_target_pairs={{0,8},{4,12},{8,0},{12,4},{16,24},{20,28},{24,16},{28,20},{1,9},{5... | collective-permute-start | bytes 294920 | tf_op jit(solution)/shard_map/ppermute | solution.py:621
  154.6 2.3 %collective-permute-done.19.refs_16_ = bf16[2,128,1024]{2,1,0:T(8,128)(2,1)S(1)} collective-permute-done((bf16[2,128,1024]{2,1,0:T(8,128)(2,1)S(1)}, bf16[2,128,1024]{2,1,0:T(8,128)(2,1)S(1)}, u32[]{:S(2)}, u32[]{:S(2)}) %collective-permute-start.19) | collective-permute-done | bytes 524320 | tf_op jit(solution)/shard_map/ppermute | solution.py:634
  156.9 6.3 %block_output.3 = bf16[2,256,1024]{2,1,0:T(8,128)(2,1)} custom-call(s32[3]{0:T(128)S(1)} %pad_add_fusion.pos_ref, bf16[1024,1024]{1,0:T(8,128)(2,1)S(1)} %copy-done.1, bf16[192,1024]{1,0:T(8,128)(2,1)S(1)} %collective-permute-done.refs_1_, bf16[192,1024]{1,0:T(8,128)(2,1)} %collective-permute-done.1.refs_2_, ...), custom_call_target="tpu_custom_call", output_to_operand_aliasing={{}: (19, {})} | custom-call | tf_op jit(solution)/shard_map/block_output/pallas_call | solution.py:340
  163.2 2.5 %collective-permute-start.29 = (f32[8,24,128]{2,1,0:T(8,128)S(1)}, f32[8,24,128]{2,1,0:T(8,128)S(1)}, u32[]{:S(2)}, u32[]{:S(2)}) collective-permute-start(f32[8,24,128]{2,1,0:T(8,128)S(1)} %add.22), channel_id=1, source_target_pairs={{0,4},{4,0},{8,12},{12,8},{16,20},{20,16},{24,28},{28,24},{1,5},{5... | collective-permute-start | bytes 294920 | tf_op jit(solution)/shard_map/ppermute | solution.py:621
  166.2 2.0 %copy.14 = bf16[2,256,3,1024]{3,1,2,0:T(8,128)(2,1)} copy(bf16[2,256,3,1024]{3,1,0,2:T(8,128)(2,1)S(1)} %maximum_bitcast_fusion) | data formatting | bytes 6291456
  (94 shorter events, 13.4 us)
Async XLA Ops:
  2.4 19.9 %collective-permute-start = (bf16[192,1024]{1,0:T(8,128)(2,1)}, bf16[192,1024]{1,0:T(8,128)(2,1)S(1)}, u32[]{:S(2)}, u32[]{:S(2)}) collective-permute-start(bf16[192,1024]{1,0:T(8,128)(2,1)} %constant_dynamic-slice_fusion.1), channel_id=1, source_target_pairs={{0,4},{4,8},{8,12},{12,0},{1,5},{5,9},{9,13},{13,1},{2,6},{6,10},{... | collective-permute-start | bytes 1179656 | tf_op jit(solution)/shard_map/ppermute | solution.py:635
  7.4 3.8 %copy-start.22 = (bf16[64,128]{1,0:T(8,128)(2,1)S(1)}, bf16[64,128]{1,0:T(8,128)(2,1)}, u32[]{:S(2)}) copy-start(bf16[64,128]{1,0:T(8,128)(2,1)} %param.7) | copy-start | bytes 49156
  7.4 24.4 %collective-permute-start.6 = (bf16[320,1024]{1,0:T(8,128)(2,1)}, bf16[320,1024]{1,0:T(8,128)(2,1)}, u32[]{:S(2)}, u32[]{:S(2)}) collective-permute-start(bf16[320,1024]{1,0:T(8,128)(2,1)} %constant_dynamic-slice_fusion), channel_id=1, source_target_pairs={{0,4},{4,8},{8,12},{12,0},{1,5},{5,9},{9,13},{13,1},{2,6},{6,10},{... | collective-permute-start | bytes 1966088 | tf_op jit(solution)/shard_map/ppermute | solution.py:635
  12.8 3.6 %copy-start.21 = (f32[64,128]{1,0:T(8,128)S(1)}, f32[64,128]{1,0:T(8,128)}, u32[]{:S(2)}) copy-start(f32[64,128]{1,0:T(8,128)} %rev.6) | copy-start | bytes 98308
  15.5 0.8 copy-start.19
  16.4 25.5 %copy-start.9 = (f32[64,256]{1,0:T(8,128)}, f32[64,256]{1,0:T(8,128)S(1)}, u32[]{:S(2)}) copy-start(f32[64,256]{1,0:T(8,128)S(1)} %maximum_maximum_fusion.line_ref) | copy-start | bytes 196612
  20.3 1.0 copy-start.2
  21.3 1.0 copy-start.4
  22.3 17.9 %collective-permute-start.1 = (bf16[192,1024]{1,0:T(8,128)(2,1)S(1)}, bf16[192,1024]{1,0:T(8,128)(2,1)}, u32[]{:S(2)}, u32[]{:S(2)}) collective-permute-start(bf16[192,1024]{1,0:T(8,128)(2,1)S(1)} %collective-permute-done.refs_1_), channel_id=1, source_target_pairs={{0,4},{4,8},{8,12},{12,0},{1,5},{5,9},{9,13},{13,1},{2,6},{6,10},{... | collective-permute-start | bytes 1179656 | tf_op jit(solution)/shard_map/ppermute | solution.py:635
  23.9 18.9 %collective-permute-start.10 = (bf16[2,128,1024]{2,1,0:T(8,128)(2,1)S(1)}, bf16[2,128,1024]{2,1,0:T(8,128)(2,1)S(1)}, u32[]{:S(2)}, u32[]{:S(2)}) collective-permute-start(bf16[2,128,1024]{2,1,0:T(8,128)(2,1)S(1)} %get-tuple-element.46.refs_14_), channel_id=1, source_target_pairs={{0,3},{1,2},{2,1},{3,0},{4,7},{5,6},{6,5},{7,4},{8,11},{9,10},{10,... | collective-permute-start | bytes 1572872 | tf_op jit(solution)/shard_map/ppermute | solution.py:634
  26.3 22.6 %collective-permute-start.8 = (bf16[2,128,1024]{2,1,0:T(8,128)(2,1)S(1)}, bf16[2,128,1024]{2,1,0:T(8,128)(2,1)S(1)}, u32[]{:S(2)}, u32[]{:S(2)}) collective-permute-start(bf16[2,128,1024]{2,1,0:T(8,128)(2,1)S(1)} %get-tuple-element.46.refs_14_), channel_id=1, source_target_pairs={{0,1},{1,0},{2,3},{3,2},{4,5},{5,4},{6,7},{7,6},{8,9},{9,8},{10,11... | collective-permute-start | bytes 1572872 | tf_op jit(solution)/shard_map/ppermute | solution.py:634
  31.8 30.9 %collective-permute-start.7 = (bf16[320,1024]{1,0:T(8,128)(2,1)}, bf16[320,1024]{1,0:T(8,128)(2,1)}, u32[]{:S(2)}, u32[]{:S(2)}) collective-permute-start(bf16[320,1024]{1,0:T(8,128)(2,1)} %collective-permute-done.6.refs_8_.refs_1_), channel_id=1, source_target_pairs={{0,4},{4,8},{8,12},{12,0},{1,5},{5,9},{9,13},{13,1},{2,6},{6,10},{... | collective-permute-start | bytes 1966088 | tf_op jit(solution)/shard_map/ppermute | solution.py:635
  40.2 21.6 %collective-permute-start.2 = (bf16[192,1024]{1,0:T(8,128)(2,1)}, bf16[192,1024]{1,0:T(8,128)(2,1)}, u32[]{:S(2)}, u32[]{:S(2)}) collective-permute-start(bf16[192,1024]{1,0:T(8,128)(2,1)} %collective-permute-done.1.refs_2_), channel_id=1, source_target_pairs={{0,4},{4,8},{8,12},{12,0},{1,5},{5,9},{9,13},{13,1},{2,6},{6,10},{... | collective-permute-start | bytes 1179656 | tf_op jit(solution)/shard_map/ppermute | solution.py:635
  40.2 21.6 %collective-permute-start.9 = (bf16[2,128,1024]{2,1,0:T(8,128)(2,1)S(1)}, bf16[2,128,1024]{2,1,0:T(8,128)(2,1)S(1)}, u32[]{:S(2)}, u32[]{:S(2)}) collective-permute-start(bf16[2,128,1024]{2,1,0:T(8,128)(2,1)S(1)} %get-tuple-element.46.refs_14_), channel_id=1, source_target_pairs={{0,2},{1,3},{2,0},{3,1},{4,6},{5,7},{6,4},{7,5},{8,10},{9,11},{10,... | collective-permute-start | bytes 1572872 | tf_op jit(solution)/shard_map/ppermute | solution.py:634
  43.6 19.2 %collective-permute-start.3 = (bf16[192,1024]{1,0:T(8,128)(2,1)S(1)}, bf16[192,1024]{1,0:T(8,128)(2,1)}, u32[]{:S(2)}, u32[]{:S(2)}) collective-permute-start(bf16[192,1024]{1,0:T(8,128)(2,1)S(1)} %collective-permute-done.refs_1_), channel_id=1, source_target_pairs={{0,16},{16,0},{1,17},{17,1},{2,18},{18,2},{3,19},{19,3},{4,20},{20... | collective-permute-start | bytes 1179656 | tf_op jit(solution)/shard_map/ppermute | solution.py:636
  49.7 13.0 %collective-permute-start.4 = (bf16[192,1024]{1,0:T(8,128)(2,1)}, bf16[192,1024]{1,0:T(8,128)(2,1)}, u32[]{:S(2)}, u32[]{:S(2)}) collective-permute-start(bf16[192,1024]{1,0:T(8,128)(2,1)} %collective-permute-done.1.refs_2_), channel_id=1, source_target_pairs={{0,16},{16,0},{1,17},{17,1},{2,18},{18,2},{3,19},{19,3},{4,20},{20... | collective-permute-start | bytes 1179656 | tf_op jit(solution)/shard_map/ppermute | solution.py:636
  61.8 2.1 %collective-permute-start.5 = (bf16[192,1024]{1,0:T(8,128)(2,1)}, bf16[192,1024]{1,0:T(8,128)(2,1)}, u32[]{:S(2)}, u32[]{:S(2)}) collective-permute-start(bf16[192,1024]{1,0:T(8,128)(2,1)} %collective-permute-done.2.refs_3_), channel_id=1, source_target_pairs={{0,16},{16,0},{1,17},{17,1},{2,18},{18,2},{3,19},{19,3},{4,20},{20... | collective-permute-start | bytes 1179656 | tf_op jit(solution)/shard_map/ppermute | solution.py:636
  62.7 21.0 %collective-permute-start.11 = (bf16[320,1024]{1,0:T(8,128)(2,1)}, bf16[320,1024]{1,0:T(8,128)(2,1)}, u32[]{:S(2)}, u32[]{:S(2)}) collective-permute-start(bf16[320,1024]{1,0:T(8,128)(2,1)} %collective-permute-done.7.refs_9_.refs_2_), channel_id=1, source_target_pairs={{0,4},{4,8},{8,12},{12,0},{1,5},{5,9},{9,13},{13,1},{2,6},{6,10},{... | collective-permute-start | bytes 1966088 | tf_op jit(solution)/shard_map/ppermute | solution.py:635
  63.9 1.6 copy-start
  65.5 1.2 copy-start.6
  66.7 18.7 %copy-start.20 = (bf16[2,160,1024]{2,1,0:T(8,128)(2,1)S(1)}, bf16[2,160,1024]{2,1,0:T(8,128)(2,1)}, u32[]{:S(2)}) copy-start(bf16[2,160,1024]{2,1,0:T(8,128)(2,1)} %copy-done.19) | copy-start | bytes 1966084
  71.5 11.2 %collective-permute-start.12 = (bf16[2,256,384]{2,1,0:T(8,128)(2,1)S(1)}, bf16[2,256,384]{2,1,0:T(8,128)(2,1)S(1)}, u32[]{:S(2)}, u32[]{:S(2)}) collective-permute-start(bf16[2,256,384]{2,1,0:T(8,128)(2,1)S(1)} %get-tuple-element.49), channel_id=1, source_target_pairs={{0,1},{1,0},{2,3},{3,2},{4,5},{5,4},{6,7},{7,6},{8,9},{9,8},{10,11... | collective-permute-start | bytes 1179656 | tf_op jit(solution)/shard_map/ppermute | solution.py:634
  72.7 10.9 %collective-permute-start.13 = (bf16[2,256,384]{2,1,0:T(8,128)(2,1)S(1)}, bf16[2,256,384]{2,1,0:T(8,128)(2,1)S(1)}, u32[]{:S(2)}, u32[]{:S(2)}) collective-permute-start(bf16[2,256,384]{2,1,0:T(8,128)(2,1)S(1)} %get-tuple-element.50), channel_id=1, source_target_pairs={{0,2},{1,3},{2,0},{3,1},{4,6},{5,7},{6,4},{7,5},{8,10},{9,11},{10,... | collective-permute-start | bytes 1179656 | tf_op jit(solution)/shard_map/ppermute | solution.py:634
  74.5 13.0 %collective-permute-start.14 = (bf16[320,1024]{1,0:T(8,128)(2,1)}, bf16[320,1024]{1,0:T(8,128)(2,1)S(1)}, u32[]{:S(2)}, u32[]{:S(2)}) collective-permute-start(bf16[320,1024]{1,0:T(8,128)(2,1)} %collective-permute-done.6.refs_8_.refs_1_), channel_id=1, source_target_pairs={{0,16},{16,0},{1,17},{17,1},{2,18},{18,2},{3,19},{19,3},{4,20},{20... | collective-permute-start | bytes 1966088 | tf_op jit(solution)/shard_map/ppermute | solution.py:636
  74.5 13.0 %collective-permute-start.15 = (bf16[320,1024]{1,0:T(8,128)(2,1)}, bf16[320,1024]{1,0:T(8,128)(2,1)S(1)}, u32[]{:S(2)}, u32[]{:S(2)}) collective-permute-start(bf16[320,1024]{1,0:T(8,128)(2,1)} %collective-permute-done.7.refs_9_.refs_2_), channel_id=1, source_target_pairs={{0,16},{16,0},{1,17},{17,1},{2,18},{18,2},{3,19},{19,3},{4,20},{20... | collective-permute-start | bytes 1966088 | tf_op jit(solution)/shard_map/ppermute | solution.py:636
  83.7 3.9 %collective-permute-start.16 = (bf16[320,1024]{1,0:T(8,128)(2,1)}, bf16[320,1024]{1,0:T(8,128)(2,1)S(1)}, u32[]{:S(2)}, u32[]{:S(2)}) collective-permute-start(bf16[320,1024]{1,0:T(8,128)(2,1)} %collective-permute-done.11.refs_10_.refs_3_), channel_id=1, source_target_pairs={{0,16},{16,0},{1,17},{17,1},{2,18},{18,2},{3,19},{19,3},{4,20},{20... | collective-permute-start | bytes 1966088 | tf_op jit(solution)/shard_map/ppermute | solution.py:636
  83.7 12.4 %collective-permute-start.21 = (bf16[2,256,384]{2,1,0:T(8,128)(2,1)S(1)}, bf16[2,256,384]{2,1,0:T(8,128)(2,1)S(1)}, u32[]{:S(2)}, u32[]{:S(2)}) collective-permute-start(bf16[2,256,384]{2,1,0:T(8,128)(2,1)S(1)} %get-tuple-element.59), channel_id=1, source_target_pairs={{0,3},{1,2},{2,1},{3,0},{4,7},{5,6},{6,5},{7,4},{8,11},{9,10},{10,... | collective-permute-start | bytes 1179656 | tf_op jit(solution)/shard_map/ppermute | solution.py:634
  85.4 20.5 %collective-permute-start.17 = (bf16[2,160,1024]{2,1,0:T(8,128)(2,1)S(1)}, bf16[2,160,1024]{2,1,0:T(8,128)(2,1)S(1)}, u32[]{:S(2)}, u32[]{:S(2)}) collective-permute-start(bf16[2,160,1024]{2,1,0:T(8,128)(2,1)S(1)} %copy-done.20), channel_id=1, source_target_pairs={{0,4},{4,8},{8,12},{1,5},{5,9},{9,13},{2,6},{6,10},{10,14},{3,7},{... | collective-permute-start | bytes 1966088 | tf_op jit(solution)/shard_map/ppermute | solution.py:26
  87.6 12.0 %copy-start.1 = (bf16[1024,1024]{1,0:T(8,128)(2,1)S(1)}, bf16[1024,1024]{1,0:T(8,128)(2,1)}, u32[]{:S(2)}) copy-start(bf16[1024,1024]{1,0:T(8,128)(2,1)} %refs_7_.3) | copy-start | bytes 6291460
  87.6 12.0 %copy-start.12 = (bf16[2,128,1024]{2,1,0:T(8,128)(2,1)S(1)}, bf16[2,128,1024]{2,1,0:T(8,128)(2,1)}, u32[]{:S(2)}) copy-start(bf16[2,128,1024]{2,1,0:T(8,128)(2,1)} %copy-done.11) | copy-start | bytes 1572868
  87.6 12.0 %copy-start.14 = (bf16[2,128,1024]{2,1,0:T(8,128)(2,1)S(1)}, bf16[2,128,1024]{2,1,0:T(8,128)(2,1)}, u32[]{:S(2)}) copy-start(bf16[2,128,1024]{2,1,0:T(8,128)(2,1)} %copy-done.13) | copy-start | bytes 1572868
  87.6 12.0 %copy-start.16 = (bf16[2,128,1024]{2,1,0:T(8,128)(2,1)S(1)}, bf16[2,128,1024]{2,1,0:T(8,128)(2,1)}, u32[]{:S(2)}) copy-start(bf16[2,128,1024]{2,1,0:T(8,128)(2,1)} %copy-done.15) | copy-start | bytes 1572868
  87.6 12.0 %copy-start.18 = (bf16[2,128,1024]{2,1,0:T(8,128)(2,1)S(1)}, bf16[2,128,1024]{2,1,0:T(8,128)(2,1)}, u32[]{:S(2)}) copy-start(bf16[2,128,1024]{2,1,0:T(8,128)(2,1)} %copy-done.17) | copy-start | bytes 1572868
  96.1 29.1 %collective-permute-start.25 = (bf16[2,256,640]{2,1,0:T(8,128)(2,1)S(1)}, bf16[2,256,640]{2,1,0:T(8,128)(2,1)S(1)}, u32[]{:S(2)}, u32[]{:S(2)}) collective-permute-start(bf16[2,256,640]{2,1,0:T(8,128)(2,1)S(1)} %get-tuple-element.73), channel_id=1, source_target_pairs={{0,3},{1,2},{2,1},{3,0},{4,7},{5,6},{6,5},{7,4},{8,11},{9,10},{10,... | collective-permute-start | bytes 1966088 | tf_op jit(solution)/shard_map/ppermute | solution.py:634
  97.9 29.5 %collective-permute-start.24 = (bf16[2,256,640]{2,1,0:T(8,128)(2,1)S(1)}, bf16[2,256,640]{2,1,0:T(8,128)(2,1)S(1)}, u32[]{:S(2)}, u32[]{:S(2)}) collective-permute-start(bf16[2,256,640]{2,1,0:T(8,128)(2,1)S(1)} %get-tuple-element.71), channel_id=1, source_target_pairs={{0,2},{1,3},{2,0},{3,1},{4,6},{5,7},{6,4},{7,5},{8,10},{9,11},{10,... | collective-permute-start | bytes 1966088 | tf_op jit(solution)/shard_map/ppermute | solution.py:634
  98.3 7.7 %copy-start.3 = (bf16[2,256,1024]{2,1,0:T(8,128)(2,1)S(1)}, bf16[2,256,1024]{2,1,0:T(8,128)(2,1)}, u32[]{:S(2)}) copy-start(bf16[2,256,1024]{2,1,0:T(8,128)(2,1)} %copy-done.2) | copy-start | bytes 3145732
  98.3 7.7 %copy-start.8 = (f32[3,3,1024]{2,1,0:T(4,128)S(1)}, f32[3,3,1024]{2,1,0:T(4,128)}, u32[]{:S(2)}) copy-start(f32[3,3,1024]{2,1,0:T(4,128)} %refs_6_.3) | copy-start | bytes 110596
  98.3 7.7 %copy-start.10 = (f32[64,256]{1,0:T(8,128)S(1)}, f32[64,256]{1,0:T(8,128)}, u32[]{:S(2)}) copy-start(f32[64,256]{1,0:T(8,128)} %copy-done.9) | copy-start | bytes 196612
  98.3 29.4 %collective-permute-start.23 = (bf16[2,256,640]{2,1,0:T(8,128)(2,1)S(1)}, bf16[2,256,640]{2,1,0:T(8,128)(2,1)S(1)}, u32[]{:S(2)}, u32[]{:S(2)}) collective-permute-start(bf16[2,256,640]{2,1,0:T(8,128)(2,1)S(1)} %get-tuple-element.69), channel_id=1, source_target_pairs={{0,1},{1,0},{2,3},{3,2},{4,5},{5,4},{6,7},{7,6},{8,9},{9,8},{10,11... | collective-permute-start | bytes 1966088 | tf_op jit(solution)/shard_map/ppermute | solution.py:634
  105.9 4.2 %copy-start.5 = (f32[2,128,1024]{2,1,0:T(8,128)S(1)}, f32[2,128,1024]{2,1,0:T(8,128)}, u32[]{:S(2)}) copy-start(f32[2,128,1024]{2,1,0:T(8,128)} %copy-done.4) | copy-start | bytes 3145732
  111.7 9.2 %collective-permute-start.22 = (bf16[2,176,384]{2,1,0:T(8,128)(2,1)S(1)}, bf16[2,176,384]{2,1,0:T(8,128)(2,1)S(1)}, u32[]{:S(2)}, u32[]{:S(2)}) collective-permute-start(bf16[2,176,384]{2,1,0:T(8,128)(2,1)S(1)} %get-tuple-element.63), channel_id=1, source_target_pairs={{4,0},{8,4},{12,8},{5,1},{9,5},{13,9},{6,2},{10,6},{14,10},{7,3},{... | collective-permute-start | bytes 811016 | tf_op jit(solution)/shard_map/ppermute | solution.py:26
  130.3 13.8 %collective-permute-start.26 = (bf16[2,176,640]{2,1,0:T(8,128)(2,1)S(1)}, bf16[2,176,640]{2,1,0:T(8,128)(2,1)S(1)}, u32[]{:S(2)}, u32[]{:S(2)}) collective-permute-start(bf16[2,176,640]{2,1,0:T(8,128)(2,1)S(1)} %get-tuple-element.76), channel_id=1, source_target_pairs={{4,0},{8,4},{12,8},{5,1},{9,5},{13,9},{6,2},{10,6},{14,10},{7,3},{... | collective-permute-start | bytes 1351688 | tf_op jit(solution)/shard_map/ppermute | solution.py:26
  131.6 23.0 %collective-permute-start.18 = (bf16[2,128,1024]{2,1,0:T(8,128)(2,1)S(1)}, bf16[2,128,1024]{2,1,0:T(8,128)(2,1)S(1)}, u32[]{:S(2)}, u32[]{:S(2)}) collective-permute-start(bf16[2,128,1024]{2,1,0:T(8,128)(2,1)S(1)} %get-tuple-element.58.refs_14_), channel_id=1, source_target_pairs={{0,1},{1,0},{2,3},{3,2},{4,5},{5,4},{6,7},{7,6},{8,9},{9,8},{10,11... | collective-permute-start | bytes 1572872 | tf_op jit(solution)/shard_map/ppermute | solution.py:634
  132.3 24.6 %collective-permute-start.19 = (bf16[2,128,1024]{2,1,0:T(8,128)(2,1)S(1)}, bf16[2,128,1024]{2,1,0:T(8,128)(2,1)S(1)}, u32[]{:S(2)}, u32[]{:S(2)}) collective-permute-start(bf16[2,128,1024]{2,1,0:T(8,128)(2,1)S(1)} %get-tuple-element.58.refs_14_), channel_id=1, source_target_pairs={{0,2},{1,3},{2,0},{3,1},{4,6},{5,7},{6,4},{7,5},{8,10},{9,11},{10,... | collective-permute-start | bytes 1572872 | tf_op jit(solution)/shard_map/ppermute | solution.py:634
  133.7 23.2 %collective-permute-start.20 = (bf16[2,128,1024]{2,1,0:T(8,128)(2,1)S(1)}, bf16[2,128,1024]{2,1,0:T(8,128)(2,1)S(1)}, u32[]{:S(2)}, u32[]{:S(2)}) collective-permute-start(bf16[2,128,1024]{2,1,0:T(8,128)(2,1)S(1)} %get-tuple-element.58.refs_14_), channel_id=1, source_target_pairs={{0,3},{1,2},{2,1},{3,0},{4,7},{5,6},{6,5},{7,4},{8,11},{9,10},{10,... | collective-permute-start | bytes 1572872 | tf_op jit(solution)/shard_map/ppermute | solution.py:634
  151.2 1.4 collective-permute-start.27
  152.6 10.6 %collective-permute-start.28 = (f32[8,24,128]{2,1,0:T(8,128)S(1)}, f32[8,24,128]{2,1,0:T(8,128)S(1)}, u32[]{:S(2)}, u32[]{:S(2)}) collective-permute-start(f32[8,24,128]{2,1,0:T(8,128)S(1)} %add.21), channel_id=1, source_target_pairs={{0,8},{4,12},{8,0},{12,4},{16,24},{20,28},{24,16},{28,20},{1,9},{5... | collective-permute-start | bytes 294920 | tf_op jit(solution)/shard_map/ppermute | solution.py:621
  163.2 5.1 %collective-permute-start.29 = (f32[8,24,128]{2,1,0:T(8,128)S(1)}, f32[8,24,128]{2,1,0:T(8,128)S(1)}, u32[]{:S(2)}, u32[]{:S(2)}) collective-permute-start(f32[8,24,128]{2,1,0:T(8,128)S(1)} %add.22), channel_id=1, source_target_pairs={{0,4},{4,0},{8,12},{12,8},{16,20},{20,16},{24,28},{28,24},{1,5},{5... | collective-permute-start | bytes 294920 | tf_op jit(solution)/shard_map/ppermute | solution.py:621
  (5 other events, 4.0 us)

commit v6 on v5

--- a/solution.py
+++ b/solution.py
@@ -677,7 +677,7 @@
     own, got = send_parts(weights[0], ranges[0], high[1:], [])
     owns, gots = [own], [got]
     if ring:
-        near[-1] = after(near[-1], *got[0][:2])
+        near[-1] = after(near[-1], got[0][2])
         weights.append(Passed(out_w, near, [swap(block) for block in near], cut))
         ranges.append([(0, rows)])
         own, got = send_parts(weights[1], ranges[1], [], got[0])

time: 170 us -> 170 us (level)
  transfers between devices with their start and end apart: 30 -> 30, of which waited for: 15 -> 14; matrix products, arithmetic and copies ran while one was open for 4% -> 4% of each run, Pallas kernels for 32% -> 32%
where the time goes in v6:
time: 170 us; the launch traced here: 169 us
  waiting for transfers between devices  58.2 us (34%)
  Pallas kernels  56.8 us (33%)
  starting transfers between devices  32.8 us (19%)
  local copies, waits for them, and re-layouts  19.2 us (11%)
    ppermute x6, waiting for transfers between devices, shards(): lax.ppermute(block, 'ctx', [(i, (i + 1) % length) for i in range(length)])  25.4 us
    ppermute x12, waiting for transfers between devices, shards(): lax.ppermute(block, 'grp', [(i, i ^ k) for i in partners])  19.4 us
    ppermute x12, starting transfers between devices, shards(): lax.ppermute(block, 'grp', [(i, i ^ k) for i in partners])  17.3 us
    unnamed x49, local copies, waits for them, and re-layouts  13.9 us
    pallas_call x2, Pallas kernels, block_output(): pl.pallas_call(functools.partial(out_kernel, weights, steps), grid=(1,),...  12.6 us
    pallas_call x2, Pallas kernels, grad_parts(): pl.pallas_call(functools.partial(grad_kernel, weights, steps, ranges), in...  11.9 us
    pallas_call x2, Pallas kernels, input_grads(): pl.pallas_call(functools.partial(input_grad_kernel, group_size, len(mix_g...  11.2 us
    ppermute x3, waiting for transfers between devices, shift(): return lax.ppermute(block, axis, route)  10.8 us
  transfers between devices with their start and end apart: 30, of which 14 were waited for; matrix products, arithmetic and copies ran while one was open for 4% of the time, Pallas kernels for 32%

profile of v6, /device:TPU:0, one launch (start us, length us, event | category | flops | bytes accessed | tf_op | source)
XLA Modules:
  0.0 169.4 jit_solution(18319294530230500202)
XLA Ops:
  0.6 1.8 %constant_dynamic-slice_fusion.1 = bf16[192,1024]{1,0:T(8,128)(2,1)} fusion(bf16[1024,1024]{1,0:T(8,128)(2,1)} %refs_7_.3, s32[]{:T(128)S(6)} %select_n.6), kind=kLoop, calls=%fused_computation.11 | loop fusion | bytes 786436 | tf_op jit(solution)/shard_map/dynamic_slice | solution.py:646
  2.4 3.0 %collective-permute-start = (bf16[192,1024]{1,0:T(8,128)(2,1)}, bf16[192,1024]{1,0:T(8,128)(2,1)S(1)}, u32[]{:S(2)}, u32[]{:S(2)}) collective-permute-start(bf16[192,1024]{1,0:T(8,128)(2,1)} %constant_dynamic-slice_fusion.1), channel_id=1, source_target_pairs={{0,4},{4,8},{8,12},{12,0},{1,5},{5,9},{9,13},{13,1},{2,6},{6,10},{... | collective-permute-start | bytes 1179656 | tf_op jit(solution)/shard_map/ppermute | solution.py:635
  5.4 2.0 %constant_dynamic-slice_fusion = bf16[320,1024]{1,0:T(8,128)(2,1)} fusion(bf16[1024,1024]{1,0:T(8,128)(2,1)} %refs_7_.3, s32[]{:T(128)S(6)} %select_n.7), kind=kLoop, calls=%fused_computation.10 | loop fusion | bytes 1310724 | tf_op jit(solution)/shard_map/dynamic_slice | solution.py:646
  7.4 1.6 collective-permute-start.6
  9.0 2.2 %copy.16 = bf16[2,256,3,1024]{3,1,0,2:T(8,128)(2,1)S(1)} copy(bf16[2,256,3,1024]{3,1,2,0:T(8,128)(2,1)} %param.5) | data formatting | bytes 6291456 | tf_op args[0]
  12.8 2.7 %products.1 = (bf16[2,256,1024]{2,1,0:T(8,128)(2,1)S(1)}, bf16[2,160,1024]{2,1,0:T(8,128)(2,1)S(1)}) custom-call(bf16[3,2,256,1024]{3,2,1,0:T(8,128)(2,1)S(1)} %bitcast.15, f32[3,3,1024]{2,1,0:T(4,128)S(1)} %copy-done.7), custom_call_target="tpu_custom_call" | custom-call | tf_op jit(solution)/shard_map/products/pallas_call | solution.py:81
  16.5 3.8 %mix_high.1 = (f32[2,128,1024]{2,1,0:T(8,128)S(1)}, bf16[2,128,1024]{2,1,0:T(8,128)(2,1)S(1)}) custom-call(f32[64,256]{1,0:T(8,128)S(1)} %maximum_maximum_fusion.line_ref, bf16[2,256,1024]{2,1,0:T(8,128)(2,1)S(1)} %get-tuple-element.42.low_ref.high_ref.product_ref.refs_1_, bf16[2,256,1024]{2,1,0:T(8,128)(2,1)S(1)} %get-tuple-element.42.low_ref.high_ref.product_ref.refs_1_, ...), custom_call_target="tpu_custom_call" | custom-call | tf_op jit(solution)/shard_map/mix_high/pallas_call | solution.py:126
  21.3 1.0 copy-done.4
  22.3 1.6 collective-permute-start.1
  23.9 2.4 %collective-permute-start.10 = (bf16[2,128,1024]{2,1,0:T(8,128)(2,1)S(1)}, bf16[2,128,1024]{2,1,0:T(8,128)(2,1)S(1)}, u32[]{:S(2)}, u32[]{:S(2)}) collective-permute-start(bf16[2,128,1024]{2,1,0:T(8,128)(2,1)S(1)} %get-tuple-element.46.refs_14_), channel_id=1, source_target_pairs={{0,3},{1,2},{2,1},{3,0},{4,7},{5,6},{6,5},{7,4},{8,11},{9,10},{10,... | collective-permute-start | bytes 1572872 | tf_op jit(solution)/shard_map/ppermute | solution.py:634
  26.9 4.9 %collective-permute-done.6.refs_8_.refs_1_ = bf16[320,1024]{1,0:T(8,128)(2,1)} collective-permute-done((bf16[320,1024]{1,0:T(8,128)(2,1)}, bf16[320,1024]{1,0:T(8,128)(2,1)}, u32[]{:S(2)}, u32[]{:S(2)}) %collective-permute-start.6) | collective-permute-done | bytes 655392 | tf_op jit(solution)/shard_map/ppermute | solution.py:635
  31.8 8.4 %collective-permute-done.1.refs_2_ = bf16[192,1024]{1,0:T(8,128)(2,1)} collective-permute-done((bf16[192,1024]{1,0:T(8,128)(2,1)S(1)}, bf16[192,1024]{1,0:T(8,128)(2,1)}, u32[]{:S(2)}, u32[]{:S(2)}) %collective-permute-start.1) | collective-permute-done | bytes 393248 | tf_op jit(solution)/shard_map/ppermute | solution.py:635
  40.2 1.7 %collective-permute-start.9 = (bf16[2,128,1024]{2,1,0:T(8,128)(2,1)S(1)}, bf16[2,128,1024]{2,1,0:T(8,128)(2,1)S(1)}, u32[]{:S(2)}, u32[]{:S(2)}) collective-permute-start(bf16[2,128,1024]{2,1,0:T(8,128)(2,1)S(1)} %get-tuple-element.46.refs_14_), channel_id=1, source_target_pairs={{0,2},{1,3},{2,0},{3,1},{4,6},{5,7},{6,4},{7,5},{8,10},{9,11},{10,... | collective-permute-start | bytes 1572872 | tf_op jit(solution)/shard_map/ppermute | solution.py:634
  43.6 5.3 %collective-permute-done.8.refs_15_ = bf16[2,128,1024]{2,1,0:T(8,128)(2,1)S(1)} collective-permute-done((bf16[2,128,1024]{2,1,0:T(8,128)(2,1)S(1)}, bf16[2,128,1024]{2,1,0:T(8,128)(2,1)S(1)}, u32[]{:S(2)}, u32[]{:S(2)}) %collective-permute-start.8) | collective-permute-done | bytes 524320 | tf_op jit(solution)/shard_map/ppermute | solution.py:634
  49.7 12.1 %collective-permute-done.2.refs_3_ = bf16[192,1024]{1,0:T(8,128)(2,1)} collective-permute-done((bf16[192,1024]{1,0:T(8,128)(2,1)}, bf16[192,1024]{1,0:T(8,128)(2,1)}, u32[]{:S(2)}, u32[]{:S(2)}) %collective-permute-start.2) | collective-permute-done | bytes 393248 | tf_op jit(solution)/shard_map/ppermute | solution.py:635
  62.7 1.2 collective-permute-done.5.refs_6_
  63.9 1.6 copy-done
  65.5 1.2 copy-done.6
  66.7 4.7 %grad_parts.2 = (f32[2,256,384]{2,1,0:T(8,128)S(1)}, bf16[2,256,384]{2,1,0:T(8,128)(2,1)S(1)}, bf16[2,256,384]{2,1,0:T(8,128)(2,1)S(1)}, bf16[2,256,384]{2,1,0:T(8,128)(2,1)S(1)}) custom-call(s32[3]{0:T(128)S(1)} %pad_add_fusion.pos_ref, bf16[512,1024]{1,0:T(8,128)(2,1)S(1)} %bitcast.22, bf16[1024,1024]{1,0:T(8,128)(2,1)S(1)} %copy-done, ...), custom_call_target="tpu_custom_call" | custom-call | tf_op jit(solution)/shard_map/grad_parts/pallas_call | solution.py:295
  71.5 2.5 %collective-permute-start.12 = (bf16[2,256,384]{2,1,0:T(8,128)(2,1)S(1)}, bf16[2,256,384]{2,1,0:T(8,128)(2,1)S(1)}, u32[]{:S(2)}, u32[]{:S(2)}) collective-permute-start(bf16[2,256,384]{2,1,0:T(8,128)(2,1)S(1)} %get-tuple-element.49), channel_id=1, source_target_pairs={{0,3},{1,2},{2,1},{3,0},{4,7},{5,6},{6,5},{7,4},{8,11},{9,10},{10,... | collective-permute-start | bytes 1179656 | tf_op jit(solution)/shard_map/ppermute | solution.py:634
  74.5 9.1 %collective-permute-done.12.refs_3_ = bf16[2,256,384]{2,1,0:T(8,128)(2,1)S(1)} collective-permute-done((bf16[2,256,384]{2,1,0:T(8,128)(2,1)S(1)}, bf16[2,256,384]{2,1,0:T(8,128)(2,1)S(1)}, u32[]{:S(2)}, u32[]{:S(2)}) %collective-permute-start.12) | collective-permute-done | bytes 393248 | tf_op jit(solution)/shard_map/ppermute | solution.py:634
  83.6 1.2 collective-permute-start.20
  84.8 1.8 %collective-permute-start.21 = (bf16[2,256,384]{2,1,0:T(8,128)(2,1)S(1)}, bf16[2,256,384]{2,1,0:T(8,128)(2,1)S(1)}, u32[]{:S(2)}, u32[]{:S(2)}) collective-permute-start(bf16[2,256,384]{2,1,0:T(8,128)(2,1)S(1)} %get-tuple-element.59), channel_id=1, source_target_pairs={{0,2},{1,3},{2,0},{3,1},{4,6},{5,7},{6,4},{7,5},{8,10},{9,11},{10,... | collective-permute-start | bytes 1179656 | tf_op jit(solution)/shard_map/ppermute | solution.py:634
  86.6 2.2 %collective-permute-start.16 = (bf16[2,160,1024]{2,1,0:T(8,128)(2,1)S(1)}, bf16[2,160,1024]{2,1,0:T(8,128)(2,1)S(1)}, u32[]{:S(2)}, u32[]{:S(2)}) collective-permute-start(bf16[2,160,1024]{2,1,0:T(8,128)(2,1)S(1)} %copy-done.20), channel_id=1, source_target_pairs={{0,4},{4,8},{8,12},{1,5},{5,9},{9,13},{2,6},{6,10},{10,14},{3,7},{... | collective-permute-start | bytes 1966088 | tf_op jit(solution)/shard_map/ppermute | solution.py:26
  88.8 7.2 %grad_parts.3 = (f32[2,256,640]{2,1,0:T(8,128)S(1)}, bf16[2,256,640]{2,1,0:T(8,128)(2,1)S(1)}, bf16[2,256,640]{2,1,0:T(8,128)(2,1)S(1)}, bf16[2,256,640]{2,1,0:T(8,128)(2,1)S(1)}) custom-call(s32[3]{0:T(128)S(1)} %pad_add_fusion.pos_ref, bf16[512,1024]{1,0:T(8,128)(2,1)S(1)} %bitcast.23, bf16[1024,1024]{1,0:T(8,128)(2,1)S(1)} %copy-done, ...), custom_call_target="tpu_custom_call" | custom-call | tf_op jit(solution)/shard_map/grad_parts/pallas_call | solution.py:295
  96.1 1.8 %collective-permute-start.25 = (bf16[2,256,640]{2,1,0:T(8,128)(2,1)S(1)}, bf16[2,256,640]{2,1,0:T(8,128)(2,1)S(1)}, u32[]{:S(2)}, u32[]{:S(2)}) collective-permute-start(bf16[2,256,640]{2,1,0:T(8,128)(2,1)S(1)} %get-tuple-element.73), channel_id=1, source_target_pairs={{0,3},{1,2},{2,1},{3,0},{4,7},{5,6},{6,5},{7,4},{8,11},{9,10},{10,... | collective-permute-start | bytes 1966088 | tf_op jit(solution)/shard_map/ppermute | solution.py:634
  98.3 1.3 collective-permute-start.23
  99.6 6.3 %block_output.2.refs_18_ = bf16[2,256,1024]{2,1,0:T(8,128)(2,1)} custom-call(s32[3]{0:T(128)S(1)} %pad_add_fusion.pos_ref, bf16[1024,1024]{1,0:T(8,128)(2,1)S(1)} %copy-done.1, bf16[192,1024]{1,0:T(8,128)(2,1)S(1)} %collective-permute-done.refs_1_, bf16[192,1024]{1,0:T(8,128)(2,1)} %collective-permute-done.1.refs_2_, ...), custom_call_target="tpu_custom_call" | custom-call | tf_op jit(solution)/shard_map/block_output/pallas_call | solution.py:340
  106.0 4.1 %mix_low.1 = (f32[2,128,1024]{2,1,0:T(8,128)S(1)}, bf16[2,128,1024]{2,1,0:T(8,128)(2,1)S(1)}, bf16[2,16,1024]{2,1,0:T(8,128)(2,1)S(1)}) custom-call(f32[64,256]{1,0:T(8,128)S(1)} %copy-done.10, bf16[2,160,1024]{2,1,0:T(8,128)(2,1)S(1)} %collective-permute-done.16.front_ref.refs_7_.refs_3_.refs_5_, bf16[2,256,1024]{2,1,0:T(8,128)(2,1)S(1)} %copy-done.3, ...), custom_call_target="tpu_custom_call" | custom-call | tf_op jit(solution)/shard_map/mix_low/pallas_call | solution.py:189
  110.2 1.5 mix_grads.2
  111.7 1.3 collective-permute-start.22
  113.0 2.3 %filter_sums.2.refs_7_ = f32[24,128]{1,0:T(8,128)S(1)} custom-call(bf16[2,256,384]{2,1,0:T(8,128)(2,1)S(1)} %get-tuple-element.61.refs_0_, bf16[2,256,1024]{2,1,0:T(8,128)(2,1)S(1)} %copy-done.3, bf16[2,16,1024]{2,1,0:T(8,128)(2,1)S(1)} %get-tuple-element.65.refs_2_, bf16[2,160,1024]{2,1,0:T(8,128)(2,1)S(1)} %collective-permute-done.16.front_ref.refs_7_.refs_3_.refs_5_), custom_call_target="tpu_custom_call" | custom-call | tf_op jit(solution)/shard_map/filter_sums/pallas_call | solution.py:467
  115.4 5.5 %collective-permute-done.22.refs_3_ = bf16[2,176,384]{2,1,0:T(8,128)(2,1)S(1)} collective-permute-done((bf16[2,176,384]{2,1,0:T(8,128)(2,1)S(1)}, bf16[2,176,384]{2,1,0:T(8,128)(2,1)S(1)}, u32[]{:S(2)}, u32[]{:S(2)}) %collective-permute-start.22) | collective-permute-done | bytes 270368 | tf_op jit(solution)/shard_map/ppermute | solution.py:26
  120.8 4.2 %input_grads.2 = (bf16[3,2,256,384]{3,2,1,0:T(8,128)(2,1)S(1)}, f32[3,24,128]{2,1,0:T(8,128)S(1)}) custom-call(bf16[2,256,384]{2,1,0:T(8,128)(2,1)S(1)} %get-tuple-element.61.refs_0_, bf16[2,256,384]{2,1,0:T(8,128)(2,1)S(1)} %get-tuple-element.62.refs_1_, f32[64,256]{1,0:T(8,128)S(1)} %concatenate.13.refs_2_, ...), custom_call_target="tpu_custom_call" | custom-call | tf_op jit(solution)/shard_map/input_grads/pallas_call | solution.py:577
  125.1 2.3 %collective-permute-done.24.refs_2_ = bf16[2,256,640]{2,1,0:T(8,128)(2,1)S(1)} collective-permute-done((bf16[2,256,640]{2,1,0:T(8,128)(2,1)S(1)}, bf16[2,256,640]{2,1,0:T(8,128)(2,1)S(1)}, u32[]{:S(2)}, u32[]{:S(2)}) %collective-permute-start.24) | collective-permute-done | bytes 655392 | tf_op jit(solution)/shard_map/ppermute | solution.py:634
  127.4 2.6 %mix_grads.3 = (bf16[2,256,640]{2,1,0:T(8,128)(2,1)S(1)}, bf16[2,256,640]{2,1,0:T(8,128)(2,1)S(1)}, bf16[2,176,640]{2,1,0:T(8,128)(2,1)S(1)}) custom-call(f32[2,256,640]{2,1,0:T(8,128)S(1)} %get-tuple-element.67.refs_0_, bf16[2,256,640]{2,1,0:T(8,128)(2,1)S(1)} %collective-permute-done.23.refs_1_, bf16[2,256,640]{2,1,0:T(8,128)(2,1)S(1)} %collective-permute-done.24.refs_2_, ...), custom_call_target="tpu_custom_call" | custom-call | tf_op jit(solution)/shard_map/mix_grads/pallas_call | solution.py:391
  130.0 1.3 collective-permute-start.26
  131.9 1.4 collective-permute-start.18
  133.4 1.5 collective-permute-start.19
  134.8 3.9 %filter_sums.3.refs_7_ = f32[40,128]{1,0:T(8,128)S(1)} custom-call(bf16[2,256,640]{2,1,0:T(8,128)(2,1)S(1)} %get-tuple-element.74.refs_0_, bf16[2,256,1024]{2,1,0:T(8,128)(2,1)S(1)} %copy-done.3, bf16[2,16,1024]{2,1,0:T(8,128)(2,1)S(1)} %get-tuple-element.65.refs_2_, bf16[2,160,1024]{2,1,0:T(8,128)(2,1)S(1)} %collective-permute-done.16.front_ref.refs_7_.refs_3_.refs_5_), custom_call_target="tpu_custom_call" | custom-call | tf_op jit(solution)/shard_map/filter_sums/pallas_call | solution.py:467
  138.7 5.4 %collective-permute-done.26.refs_3_ = bf16[2,176,640]{2,1,0:T(8,128)(2,1)S(1)} collective-permute-done((bf16[2,176,640]{2,1,0:T(8,128)(2,1)S(1)}, bf16[2,176,640]{2,1,0:T(8,128)(2,1)S(1)}, u32[]{:S(2)}, u32[]{:S(2)}) %collective-permute-start.26) | collective-permute-done | bytes 450592 | tf_op jit(solution)/shard_map/ppermute | solution.py:26
  144.1 7.0 %input_grads.3 = (bf16[3,2,256,640]{3,2,1,0:T(8,128)(2,1)S(1)}, f32[5,24,128]{2,1,0:T(8,128)S(1)}) custom-call(bf16[2,256,640]{2,1,0:T(8,128)(2,1)S(1)} %get-tuple-element.74.refs_0_, bf16[2,256,640]{2,1,0:T(8,128)(2,1)S(1)} %get-tuple-element.75.refs_1_, f32[64,256]{1,0:T(8,128)S(1)} %concatenate.13.refs_2_, ...), custom_call_target="tpu_custom_call" | custom-call | tf_op jit(solution)/shard_map/input_grads/pallas_call | solution.py:577
  151.2 1.3 collective-permute-done.27
  152.5 1.5 collective-permute-start.28
  154.0 2.6 %collective-permute-done.18.refs_16_ = bf16[2,128,1024]{2,1,0:T(8,128)(2,1)S(1)} collective-permute-done((bf16[2,128,1024]{2,1,0:T(8,128)(2,1)S(1)}, bf16[2,128,1024]{2,1,0:T(8,128)(2,1)S(1)}, u32[]{:S(2)}, u32[]{:S(2)}) %collective-permute-start.18) | collective-permute-done | bytes 524320 | tf_op jit(solution)/shard_map/ppermute | solution.py:634
  156.6 6.3 %block_output.3 = bf16[2,256,1024]{2,1,0:T(8,128)(2,1)} custom-call(s32[3]{0:T(128)S(1)} %pad_add_fusion.pos_ref, bf16[1024,1024]{1,0:T(8,128)(2,1)S(1)} %copy-done.1, bf16[192,1024]{1,0:T(8,128)(2,1)S(1)} %collective-permute-done.refs_1_, bf16[192,1024]{1,0:T(8,128)(2,1)} %collective-permute-done.1.refs_2_, ...), custom_call_target="tpu_custom_call", output_to_operand_aliasing={{}: (19, {})} | custom-call | tf_op jit(solution)/shard_map/block_output/pallas_call | solution.py:340
  162.9 2.5 %collective-permute-start.29 = (f32[8,24,128]{2,1,0:T(8,128)S(1)}, f32[8,24,128]{2,1,0:T(8,128)S(1)}, u32[]{:S(2)}, u32[]{:S(2)}) collective-permute-start(f32[8,24,128]{2,1,0:T(8,128)S(1)} %add.22), channel_id=1, source_target_pairs={{0,4},{4,0},{8,12},{12,8},{16,20},{20,16},{24,28},{28,24},{1,5},{5... | collective-permute-start | bytes 294920 | tf_op jit(solution)/shard_map/ppermute | solution.py:621
  165.9 2.0 %copy.14 = bf16[2,256,3,1024]{3,1,2,0:T(8,128)(2,1)} copy(bf16[2,256,3,1024]{3,1,0,2:T(8,128)(2,1)S(1)} %maximum_bitcast_fusion) | data formatting | bytes 6291456
  (94 shorter events, 11.2 us)
Async XLA Ops:
  2.4 19.9 %collective-permute-start = (bf16[192,1024]{1,0:T(8,128)(2,1)}, bf16[192,1024]{1,0:T(8,128)(2,1)S(1)}, u32[]{:S(2)}, u32[]{:S(2)}) collective-permute-start(bf16[192,1024]{1,0:T(8,128)(2,1)} %constant_dynamic-slice_fusion.1), channel_id=1, source_target_pairs={{0,4},{4,8},{8,12},{12,0},{1,5},{5,9},{9,13},{13,1},{2,6},{6,10},{... | collective-permute-start | bytes 1179656 | tf_op jit(solution)/shard_map/ppermute | solution.py:635
  7.4 3.8 %copy-start.22 = (bf16[64,128]{1,0:T(8,128)(2,1)S(1)}, bf16[64,128]{1,0:T(8,128)(2,1)}, u32[]{:S(2)}) copy-start(bf16[64,128]{1,0:T(8,128)(2,1)} %param.7) | copy-start | bytes 49156
  7.4 24.4 %collective-permute-start.6 = (bf16[320,1024]{1,0:T(8,128)(2,1)}, bf16[320,1024]{1,0:T(8,128)(2,1)}, u32[]{:S(2)}, u32[]{:S(2)}) collective-permute-start(bf16[320,1024]{1,0:T(8,128)(2,1)} %constant_dynamic-slice_fusion), channel_id=1, source_target_pairs={{0,4},{4,8},{8,12},{12,0},{1,5},{5,9},{9,13},{13,1},{2,6},{6,10},{... | collective-permute-start | bytes 1966088 | tf_op jit(solution)/shard_map/ppermute | solution.py:635
  12.8 3.6 %copy-start.21 = (f32[64,128]{1,0:T(8,128)S(1)}, f32[64,128]{1,0:T(8,128)}, u32[]{:S(2)}) copy-start(f32[64,128]{1,0:T(8,128)} %rev.6) | copy-start | bytes 98308
  15.5 0.8 copy-start.19
  16.4 25.5 %copy-start.9 = (f32[64,256]{1,0:T(8,128)}, f32[64,256]{1,0:T(8,128)S(1)}, u32[]{:S(2)}) copy-start(f32[64,256]{1,0:T(8,128)S(1)} %maximum_maximum_fusion.line_ref) | copy-start | bytes 196612
  20.3 1.0 copy-start.2
  21.3 1.0 copy-start.4
  22.3 17.9 %collective-permute-start.1 = (bf16[192,1024]{1,0:T(8,128)(2,1)S(1)}, bf16[192,1024]{1,0:T(8,128)(2,1)}, u32[]{:S(2)}, u32[]{:S(2)}) collective-permute-start(bf16[192,1024]{1,0:T(8,128)(2,1)S(1)} %collective-permute-done.refs_1_), channel_id=1, source_target_pairs={{0,4},{4,8},{8,12},{12,0},{1,5},{5,9},{9,13},{13,1},{2,6},{6,10},{... | collective-permute-start | bytes 1179656 | tf_op jit(solution)/shard_map/ppermute | solution.py:635
  23.9 18.9 %collective-permute-start.10 = (bf16[2,128,1024]{2,1,0:T(8,128)(2,1)S(1)}, bf16[2,128,1024]{2,1,0:T(8,128)(2,1)S(1)}, u32[]{:S(2)}, u32[]{:S(2)}) collective-permute-start(bf16[2,128,1024]{2,1,0:T(8,128)(2,1)S(1)} %get-tuple-element.46.refs_14_), channel_id=1, source_target_pairs={{0,3},{1,2},{2,1},{3,0},{4,7},{5,6},{6,5},{7,4},{8,11},{9,10},{10,... | collective-permute-start | bytes 1572872 | tf_op jit(solution)/shard_map/ppermute | solution.py:634
  26.3 22.6 %collective-permute-start.8 = (bf16[2,128,1024]{2,1,0:T(8,128)(2,1)S(1)}, bf16[2,128,1024]{2,1,0:T(8,128)(2,1)S(1)}, u32[]{:S(2)}, u32[]{:S(2)}) collective-permute-start(bf16[2,128,1024]{2,1,0:T(8,128)(2,1)S(1)} %get-tuple-element.46.refs_14_), channel_id=1, source_target_pairs={{0,1},{1,0},{2,3},{3,2},{4,5},{5,4},{6,7},{7,6},{8,9},{9,8},{10,11... | collective-permute-start | bytes 1572872 | tf_op jit(solution)/shard_map/ppermute | solution.py:634
  31.8 30.9 %collective-permute-start.7 = (bf16[320,1024]{1,0:T(8,128)(2,1)}, bf16[320,1024]{1,0:T(8,128)(2,1)}, u32[]{:S(2)}, u32[]{:S(2)}) collective-permute-start(bf16[320,1024]{1,0:T(8,128)(2,1)} %collective-permute-done.6.refs_8_.refs_1_), channel_id=1, source_target_pairs={{0,4},{4,8},{8,12},{12,0},{1,5},{5,9},{9,13},{13,1},{2,6},{6,10},{... | collective-permute-start | bytes 1966088 | tf_op jit(solution)/shard_map/ppermute | solution.py:635
  40.2 21.6 %collective-permute-start.2 = (bf16[192,1024]{1,0:T(8,128)(2,1)}, bf16[192,1024]{1,0:T(8,128)(2,1)}, u32[]{:S(2)}, u32[]{:S(2)}) collective-permute-start(bf16[192,1024]{1,0:T(8,128)(2,1)} %collective-permute-done.1.refs_2_), channel_id=1, source_target_pairs={{0,4},{4,8},{8,12},{12,0},{1,5},{5,9},{9,13},{13,1},{2,6},{6,10},{... | collective-permute-start | bytes 1179656 | tf_op jit(solution)/shard_map/ppermute | solution.py:635
  40.2 21.6 %collective-permute-start.9 = (bf16[2,128,1024]{2,1,0:T(8,128)(2,1)S(1)}, bf16[2,128,1024]{2,1,0:T(8,128)(2,1)S(1)}, u32[]{:S(2)}, u32[]{:S(2)}) collective-permute-start(bf16[2,128,1024]{2,1,0:T(8,128)(2,1)S(1)} %get-tuple-element.46.refs_14_), channel_id=1, source_target_pairs={{0,2},{1,3},{2,0},{3,1},{4,6},{5,7},{6,4},{7,5},{8,10},{9,11},{10,... | collective-permute-start | bytes 1572872 | tf_op jit(solution)/shard_map/ppermute | solution.py:634
  43.6 19.2 %collective-permute-start.3 = (bf16[192,1024]{1,0:T(8,128)(2,1)S(1)}, bf16[192,1024]{1,0:T(8,128)(2,1)}, u32[]{:S(2)}, u32[]{:S(2)}) collective-permute-start(bf16[192,1024]{1,0:T(8,128)(2,1)S(1)} %collective-permute-done.refs_1_), channel_id=1, source_target_pairs={{0,16},{16,0},{1,17},{17,1},{2,18},{18,2},{3,19},{19,3},{4,20},{20... | collective-permute-start | bytes 1179656 | tf_op jit(solution)/shard_map/ppermute | solution.py:636
  49.7 13.0 %collective-permute-start.4 = (bf16[192,1024]{1,0:T(8,128)(2,1)}, bf16[192,1024]{1,0:T(8,128)(2,1)}, u32[]{:S(2)}, u32[]{:S(2)}) collective-permute-start(bf16[192,1024]{1,0:T(8,128)(2,1)} %collective-permute-done.1.refs_2_), channel_id=1, source_target_pairs={{0,16},{16,0},{1,17},{17,1},{2,18},{18,2},{3,19},{19,3},{4,20},{20... | collective-permute-start | bytes 1179656 | tf_op jit(solution)/shard_map/ppermute | solution.py:636
  61.8 2.1 %collective-permute-start.5 = (bf16[192,1024]{1,0:T(8,128)(2,1)}, bf16[192,1024]{1,0:T(8,128)(2,1)}, u32[]{:S(2)}, u32[]{:S(2)}) collective-permute-start(bf16[192,1024]{1,0:T(8,128)(2,1)} %collective-permute-done.2.refs_3_), channel_id=1, source_target_pairs={{0,16},{16,0},{1,17},{17,1},{2,18},{18,2},{3,19},{19,3},{4,20},{20... | collective-permute-start | bytes 1179656 | tf_op jit(solution)/shard_map/ppermute | solution.py:636
  62.7 20.9 %collective-permute-start.11 = (bf16[320,1024]{1,0:T(8,128)(2,1)}, bf16[320,1024]{1,0:T(8,128)(2,1)}, u32[]{:S(2)}, u32[]{:S(2)}) collective-permute-start(bf16[320,1024]{1,0:T(8,128)(2,1)} %collective-permute-done.7.refs_9_.refs_2_), channel_id=1, source_target_pairs={{0,4},{4,8},{8,12},{12,0},{1,5},{5,9},{9,13},{13,1},{2,6},{6,10},{... | collective-permute-start | bytes 1966088 | tf_op jit(solution)/shard_map/ppermute | solution.py:635
  63.9 1.6 copy-start
  65.5 1.2 copy-start.6
  66.7 19.9 %copy-start.20 = (bf16[2,160,1024]{2,1,0:T(8,128)(2,1)S(1)}, bf16[2,160,1024]{2,1,0:T(8,128)(2,1)}, u32[]{:S(2)}) copy-start(bf16[2,160,1024]{2,1,0:T(8,128)(2,1)} %copy-done.19) | copy-start | bytes 1966084
  71.5 12.1 %collective-permute-start.12 = (bf16[2,256,384]{2,1,0:T(8,128)(2,1)S(1)}, bf16[2,256,384]{2,1,0:T(8,128)(2,1)S(1)}, u32[]{:S(2)}, u32[]{:S(2)}) collective-permute-start(bf16[2,256,384]{2,1,0:T(8,128)(2,1)S(1)} %get-tuple-element.49), channel_id=1, source_target_pairs={{0,3},{1,2},{2,1},{3,0},{4,7},{5,6},{6,5},{7,4},{8,11},{9,10},{10,... | collective-permute-start | bytes 1179656 | tf_op jit(solution)/shard_map/ppermute | solution.py:634
  74.0 12.6 %collective-permute-start.13 = (bf16[320,1024]{1,0:T(8,128)(2,1)}, bf16[320,1024]{1,0:T(8,128)(2,1)S(1)}, u32[]{:S(2)}, u32[]{:S(2)}) collective-permute-start(bf16[320,1024]{1,0:T(8,128)(2,1)} %collective-permute-done.6.refs_8_.refs_1_), channel_id=1, source_target_pairs={{0,16},{16,0},{1,17},{17,1},{2,18},{18,2},{3,19},{19,3},{4,20},{20... | collective-permute-start | bytes 1966088 | tf_op jit(solution)/shard_map/ppermute | solution.py:636
  74.0 14.8 %collective-permute-start.14 = (bf16[320,1024]{1,0:T(8,128)(2,1)}, bf16[320,1024]{1,0:T(8,128)(2,1)S(1)}, u32[]{:S(2)}, u32[]{:S(2)}) collective-permute-start(bf16[320,1024]{1,0:T(8,128)(2,1)} %collective-permute-done.7.refs_9_.refs_2_), channel_id=1, source_target_pairs={{0,16},{16,0},{1,17},{17,1},{2,18},{18,2},{3,19},{19,3},{4,20},{20... | collective-permute-start | bytes 1966088 | tf_op jit(solution)/shard_map/ppermute | solution.py:636
  83.6 5.2 %collective-permute-start.15 = (bf16[320,1024]{1,0:T(8,128)(2,1)}, bf16[320,1024]{1,0:T(8,128)(2,1)S(1)}, u32[]{:S(2)}, u32[]{:S(2)}) collective-permute-start(bf16[320,1024]{1,0:T(8,128)(2,1)} %collective-permute-done.11.refs_10_.refs_3_), channel_id=1, source_target_pairs={{0,16},{16,0},{1,17},{17,1},{2,18},{18,2},{3,19},{19,3},{4,20},{20... | collective-permute-start | bytes 1966088 | tf_op jit(solution)/shard_map/ppermute | solution.py:636
  83.6 12.5 %collective-permute-start.20 = (bf16[2,256,384]{2,1,0:T(8,128)(2,1)S(1)}, bf16[2,256,384]{2,1,0:T(8,128)(2,1)S(1)}, u32[]{:S(2)}, u32[]{:S(2)}) collective-permute-start(bf16[2,256,384]{2,1,0:T(8,128)(2,1)S(1)} %get-tuple-element.58), channel_id=1, source_target_pairs={{0,1},{1,0},{2,3},{3,2},{4,5},{5,4},{6,7},{7,6},{8,9},{9,8},{10,11... | collective-permute-start | bytes 1179656 | tf_op jit(solution)/shard_map/ppermute | solution.py:634
  84.8 11.3 %collective-permute-start.21 = (bf16[2,256,384]{2,1,0:T(8,128)(2,1)S(1)}, bf16[2,256,384]{2,1,0:T(8,128)(2,1)S(1)}, u32[]{:S(2)}, u32[]{:S(2)}) collective-permute-start(bf16[2,256,384]{2,1,0:T(8,128)(2,1)S(1)} %get-tuple-element.59), channel_id=1, source_target_pairs={{0,2},{1,3},{2,0},{3,1},{4,6},{5,7},{6,4},{7,5},{8,10},{9,11},{10,... | collective-permute-start | bytes 1179656 | tf_op jit(solution)/shard_map/ppermute | solution.py:634
  86.6 19.4 %collective-permute-start.16 = (bf16[2,160,1024]{2,1,0:T(8,128)(2,1)S(1)}, bf16[2,160,1024]{2,1,0:T(8,128)(2,1)S(1)}, u32[]{:S(2)}, u32[]{:S(2)}) collective-permute-start(bf16[2,160,1024]{2,1,0:T(8,128)(2,1)S(1)} %copy-done.20), channel_id=1, source_target_pairs={{0,4},{4,8},{8,12},{1,5},{5,9},{9,13},{2,6},{6,10},{10,14},{3,7},{... | collective-permute-start | bytes 1966088 | tf_op jit(solution)/shard_map/ppermute | solution.py:26
  88.8 10.8 %copy-start.1 = (bf16[1024,1024]{1,0:T(8,128)(2,1)S(1)}, bf16[1024,1024]{1,0:T(8,128)(2,1)}, u32[]{:S(2)}) copy-start(bf16[1024,1024]{1,0:T(8,128)(2,1)} %refs_7_.3) | copy-start | bytes 6291460
  88.8 10.8 %copy-start.12 = (bf16[2,128,1024]{2,1,0:T(8,128)(2,1)S(1)}, bf16[2,128,1024]{2,1,0:T(8,128)(2,1)}, u32[]{:S(2)}) copy-start(bf16[2,128,1024]{2,1,0:T(8,128)(2,1)} %copy-done.11) | copy-start | bytes 1572868
  88.8 10.8 %copy-start.14 = (bf16[2,128,1024]{2,1,0:T(8,128)(2,1)S(1)}, bf16[2,128,1024]{2,1,0:T(8,128)(2,1)}, u32[]{:S(2)}) copy-start(bf16[2,128,1024]{2,1,0:T(8,128)(2,1)} %copy-done.13) | copy-start | bytes 1572868
  88.8 10.8 %copy-start.16 = (bf16[2,128,1024]{2,1,0:T(8,128)(2,1)S(1)}, bf16[2,128,1024]{2,1,0:T(8,128)(2,1)}, u32[]{:S(2)}) copy-start(bf16[2,128,1024]{2,1,0:T(8,128)(2,1)} %copy-done.15) | copy-start | bytes 1572868
  88.8 10.8 %copy-start.18 = (bf16[2,128,1024]{2,1,0:T(8,128)(2,1)S(1)}, bf16[2,128,1024]{2,1,0:T(8,128)(2,1)}, u32[]{:S(2)}) copy-start(bf16[2,128,1024]{2,1,0:T(8,128)(2,1)} %copy-done.17) | copy-start | bytes 1572868
  96.1 29.0 %collective-permute-start.25 = (bf16[2,256,640]{2,1,0:T(8,128)(2,1)S(1)}, bf16[2,256,640]{2,1,0:T(8,128)(2,1)S(1)}, u32[]{:S(2)}, u32[]{:S(2)}) collective-permute-start(bf16[2,256,640]{2,1,0:T(8,128)(2,1)S(1)} %get-tuple-element.73), channel_id=1, source_target_pairs={{0,3},{1,2},{2,1},{3,0},{4,7},{5,6},{6,5},{7,4},{8,11},{9,10},{10,... | collective-permute-start | bytes 1966088 | tf_op jit(solution)/shard_map/ppermute | solution.py:634
  97.9 29.5 %collective-permute-start.24 = (bf16[2,256,640]{2,1,0:T(8,128)(2,1)S(1)}, bf16[2,256,640]{2,1,0:T(8,128)(2,1)S(1)}, u32[]{:S(2)}, u32[]{:S(2)}) collective-permute-start(bf16[2,256,640]{2,1,0:T(8,128)(2,1)S(1)} %get-tuple-element.71), channel_id=1, source_target_pairs={{0,2},{1,3},{2,0},{3,1},{4,6},{5,7},{6,4},{7,5},{8,10},{9,11},{10,... | collective-permute-start | bytes 1966088 | tf_op jit(solution)/shard_map/ppermute | solution.py:634
  98.3 7.7 %copy-start.3 = (bf16[2,256,1024]{2,1,0:T(8,128)(2,1)S(1)}, bf16[2,256,1024]{2,1,0:T(8,128)(2,1)}, u32[]{:S(2)}) copy-start(bf16[2,256,1024]{2,1,0:T(8,128)(2,1)} %copy-done.2) | copy-start | bytes 3145732
  98.3 7.7 %copy-start.8 = (f32[3,3,1024]{2,1,0:T(4,128)S(1)}, f32[3,3,1024]{2,1,0:T(4,128)}, u32[]{:S(2)}) copy-start(f32[3,3,1024]{2,1,0:T(4,128)} %refs_6_.3) | copy-start | bytes 110596
  98.3 7.7 %copy-start.10 = (f32[64,256]{1,0:T(8,128)S(1)}, f32[64,256]{1,0:T(8,128)}, u32[]{:S(2)}) copy-start(f32[64,256]{1,0:T(8,128)} %copy-done.9) | copy-start | bytes 196612
  98.3 29.1 %collective-permute-start.23 = (bf16[2,256,640]{2,1,0:T(8,128)(2,1)S(1)}, bf16[2,256,640]{2,1,0:T(8,128)(2,1)S(1)}, u32[]{:S(2)}, u32[]{:S(2)}) collective-permute-start(bf16[2,256,640]{2,1,0:T(8,128)(2,1)S(1)} %get-tuple-element.69), channel_id=1, source_target_pairs={{0,1},{1,0},{2,3},{3,2},{4,5},{5,4},{6,7},{7,6},{8,9},{9,8},{10,11... | collective-permute-start | bytes 1966088 | tf_op jit(solution)/shard_map/ppermute | solution.py:634
  106.0 4.2 %copy-start.5 = (f32[2,128,1024]{2,1,0:T(8,128)S(1)}, f32[2,128,1024]{2,1,0:T(8,128)}, u32[]{:S(2)}) copy-start(f32[2,128,1024]{2,1,0:T(8,128)} %copy-done.4) | copy-start | bytes 3145732
  111.7 9.1 %collective-permute-start.22 = (bf16[2,176,384]{2,1,0:T(8,128)(2,1)S(1)}, bf16[2,176,384]{2,1,0:T(8,128)(2,1)S(1)}, u32[]{:S(2)}, u32[]{:S(2)}) collective-permute-start(bf16[2,176,384]{2,1,0:T(8,128)(2,1)S(1)} %get-tuple-element.63), channel_id=1, source_target_pairs={{4,0},{8,4},{12,8},{5,1},{9,5},{13,9},{6,2},{10,6},{14,10},{7,3},{... | collective-permute-start | bytes 811016 | tf_op jit(solution)/shard_map/ppermute | solution.py:26
  130.0 14.1 %collective-permute-start.26 = (bf16[2,176,640]{2,1,0:T(8,128)(2,1)S(1)}, bf16[2,176,640]{2,1,0:T(8,128)(2,1)S(1)}, u32[]{:S(2)}, u32[]{:S(2)}) collective-permute-start(bf16[2,176,640]{2,1,0:T(8,128)(2,1)S(1)} %get-tuple-element.76), channel_id=1, source_target_pairs={{4,0},{8,4},{12,8},{5,1},{9,5},{13,9},{6,2},{10,6},{14,10},{7,3},{... | collective-permute-start | bytes 1351688 | tf_op jit(solution)/shard_map/ppermute | solution.py:26
  131.3 22.7 %collective-permute-start.17 = (bf16[2,128,1024]{2,1,0:T(8,128)(2,1)S(1)}, bf16[2,128,1024]{2,1,0:T(8,128)(2,1)S(1)}, u32[]{:S(2)}, u32[]{:S(2)}) collective-permute-start(bf16[2,128,1024]{2,1,0:T(8,128)(2,1)S(1)} %get-tuple-element.57.refs_14_), channel_id=1, source_target_pairs={{0,1},{1,0},{2,3},{3,2},{4,5},{5,4},{6,7},{7,6},{8,9},{9,8},{10,11... | collective-permute-start | bytes 1572872 | tf_op jit(solution)/shard_map/ppermute | solution.py:634
  131.9 24.6 %collective-permute-start.18 = (bf16[2,128,1024]{2,1,0:T(8,128)(2,1)S(1)}, bf16[2,128,1024]{2,1,0:T(8,128)(2,1)S(1)}, u32[]{:S(2)}, u32[]{:S(2)}) collective-permute-start(bf16[2,128,1024]{2,1,0:T(8,128)(2,1)S(1)} %get-tuple-element.57.refs_14_), channel_id=1, source_target_pairs={{0,2},{1,3},{2,0},{3,1},{4,6},{5,7},{6,4},{7,5},{8,10},{9,11},{10,... | collective-permute-start | bytes 1572872 | tf_op jit(solution)/shard_map/ppermute | solution.py:634
  133.4 23.2 %collective-permute-start.19 = (bf16[2,128,1024]{2,1,0:T(8,128)(2,1)S(1)}, bf16[2,128,1024]{2,1,0:T(8,128)(2,1)S(1)}, u32[]{:S(2)}, u32[]{:S(2)}) collective-permute-start(bf16[2,128,1024]{2,1,0:T(8,128)(2,1)S(1)} %get-tuple-element.57.refs_14_), channel_id=1, source_target_pairs={{0,3},{1,2},{2,1},{3,0},{4,7},{5,6},{6,5},{7,4},{8,11},{9,10},{10,... | collective-permute-start | bytes 1572872 | tf_op jit(solution)/shard_map/ppermute | solution.py:634
  151.1 1.4 collective-permute-start.27
  152.5 10.4 %collective-permute-start.28 = (f32[8,24,128]{2,1,0:T(8,128)S(1)}, f32[8,24,128]{2,1,0:T(8,128)S(1)}, u32[]{:S(2)}, u32[]{:S(2)}) collective-permute-start(f32[8,24,128]{2,1,0:T(8,128)S(1)} %add.21), channel_id=1, source_target_pairs={{0,8},{4,12},{8,0},{12,4},{16,24},{20,28},{24,16},{28,20},{1,9},{5... | collective-permute-start | bytes 294920 | tf_op jit(solution)/shard_map/ppermute | solution.py:621
  162.9 5.1 %collective-permute-start.29 = (f32[8,24,128]{2,1,0:T(8,128)S(1)}, f32[8,24,128]{2,1,0:T(8,128)S(1)}, u32[]{:S(2)}, u32[]{:S(2)}) collective-permute-start(f32[8,24,128]{2,1,0:T(8,128)S(1)} %add.22), channel_id=1, source_target_pairs={{0,4},{4,0},{8,12},{12,8},{16,20},{20,16},{24,28},{28,24},{1,5},{5... | collective-permute-start | bytes 294920 | tf_op jit(solution)/shard_map/ppermute | solution.py:621
  (5 other events, 4.0 us)
